TPU v7x, 32 devices: a whole 2x2x4 slice. The times are simulated.
32 devices in a mesh: dom: 8 (over z, y), tile: 4 (over x, core).
Axes of the slice: x: 2, y: 2, z: 4, core: 2. Of those that a mesh axis runs over, the one named last changes fastest.
Arguments:
- tile_latent: bfloat16 [4096, 512], P(('dom', 'tile')), may hold values from -6 to 6
- relay_pick: int32 [32, 128], P(('dom', 'tile')), may hold values from 0 to 127, as said below
- relay_from: int32 [4096], P(('dom', 'tile')), may hold values from 0 to 255, as said below
- cut_pick: int32 [32, 32], P(('dom', 'tile')), may hold values from 0 to 127, as said below
- edge_latent: bfloat16 [24576, 512], P(('dom', 'tile')), may hold values from -6 to 6
- edge_sender: int32 [24576], P(('dom', 'tile')), may hold values from 0 to 543, as said below
- edge_receiver: int32 [24576], P(('dom', 'tile')), may hold values from 0 to 127, as said below
- edge_in: bfloat16 [1536, 512], replicated, may hold values from -0.15625 to 0.15625
- edge_out: bfloat16 [512, 512], replicated
- node_in: bfloat16 [1024, 512], replicated, may hold values from -0.1875 to 0.1875
- node_out: bfloat16 [512, 512], replicated
- node_cot: bfloat16 [4096, 512], P(('dom', 'tile')), may hold values from -6 to 6
- edge_cot: bfloat16 [24576, 512], P(('dom', 'tile')), may hold values from -6 to 6
Outputs:
- node_update: bfloat16 [4096, 512], P(('dom', 'tile'))
- edge_update: bfloat16 [24576, 512], P(('dom', 'tile'))
- latent_grad: bfloat16 [4096, 512], P(('dom', 'tile'))
- edge_grad: bfloat16 [24576, 512], P(('dom', 'tile'))
- weight_grad: float32 [3584, 512], P('dom', 'tile')
Inputs may be any that keep to these rules, and one draw needn't show every extreme that they name: `relay_pick`: slot j of the block for partition q on device (p, t) carries a row when j is under that pair's count; the counts depend on the partition offset q - p and are 16 or half of it, zero for q = p; the other slots name rows that no one reads. No tile row goes out twice, and the rows that go out nowhere stay on their device. `relay_from`: each device's block names 128 distinct places: its own staying tile rows (below 128) or received slots that carry a row, 128 + s * 16 + j for slot j from partition s. `cut_pick`: distinct rows within a device. `edge_sender`: below 512: a node of the device's own partition; above: a halo slot, first the 16 from the lower partition, then the 16 from the upper. `edge_receiver`: not falling within a device.
All inputs are finite; a program needn't handle non-finite values.
Results may differ from a plain program's by a relative error of at most 0.013.
Values may be sent and summed in bfloat16 or wider, within the bound.
No kernel may reach another device: no remote copies, remote signals or barrier semaphores. Data moves between devices by JAX's collectives and lax.ppermute only.
A program may use at most 128 MiB of HBM per device.

v0:
```python
import jax
import jax.numpy as jnp
from jax import lax
from jax.sharding import PartitionSpec as P

EPSILON = 1e-05


def extended(cells, sides, width):
    for axis, dim in sides:
        count = lax.axis_size(axis)
        head = lax.slice_in_dim(cells, 0, width, axis=dim)
        tail = lax.slice_in_dim(cells, cells.shape[dim] - width, cells.shape[dim], axis=dim)
        cells = jnp.concatenate(
            [
                lax.ppermute(tail, axis, [(i, (i + 1) % count) for i in range(count)]),
                cells,
                lax.ppermute(head, axis, [((i + 1) % count, i) for i in range(count)]),
            ],
            axis=dim,
        )
    return cells


def layer_norm(values):
    center = values - jnp.mean(values, -1, keepdims=True)
    inverse = lax.rsqrt(jnp.mean(center * center, -1, keepdims=True) + EPSILON)
    return (center * inverse, inverse)


def norm_grad(normed, inverse, upstream):
    mean_up = jnp.mean(upstream, -1, keepdims=True)
    mean_cross = jnp.mean(upstream * normed, -1, keepdims=True)
    return inverse * (upstream - mean_up - normed * mean_cross)


def silu_grad(values):
    sigmoid = jax.nn.sigmoid(values)
    return sigmoid * (1.0 + values * (1.0 - sigmoid))


def flat_dot(left_mat, right_mat):
    return jnp.dot(left_mat, right_mat, preferred_element_type=jnp.float32)


def inner_dot(left_mat, right_mat):
    return lax.dot_general(
        left_mat, right_mat, (((0,), (0,)), ((), ())), preferred_element_type=jnp.float32
    )


def outer_dot(left_mat, right_mat):
    return lax.dot_general(
        left_mat, right_mat, (((1,), (1,)), ((), ())), preferred_element_type=jnp.float32
    )


def split_parts(values):
    high_part = values.astype(jnp.bfloat16)
    low_part = (values - high_part.astype(jnp.float32)).astype(jnp.bfloat16)
    return (high_part, low_part)


def split_sum(onehot, values):
    high_part, low_part = split_parts(values)
    return inner_dot(onehot, high_part) + inner_dot(onehot, low_part)


def body(
    tile_latent,
    relay_pick,
    relay_from,
    cut_pick,
    edge_latent,
    edge_sender,
    edge_receiver,
    edge_in,
    edge_out,
    node_in,
    node_out,
    node_cot,
    edge_cot,
):
    feat_dim = edge_out.shape[0]
    node_count = tile_latent.shape[0]
    dom_count = lax.axis_size("dom")
    part_count = lax.axis_size("tile") * node_count
    slot_count = relay_pick.shape[1] // dom_count
    halo_rows = cut_pick.shape[1] // 2
    pick_list = relay_pick[0]
    cut_list = cut_pick[0]
    w_edge = edge_in[:feat_dim]
    w_send = edge_in[feat_dim : 2 * feat_dim]
    w_recv = edge_in[2 * feat_dim :]
    w_node = node_in[:feat_dim]
    w_agg = node_in[feat_dim:]
    outgoing = jnp.take(tile_latent, pick_list, axis=0).reshape(dom_count, slot_count, feat_dim)
    incoming = lax.all_to_all(outgoing, "dom", split_axis=0, concat_axis=0, tiled=True)
    pooled = jnp.concatenate([tile_latent, incoming.reshape(dom_count * slot_count, feat_dim)], 0)
    latent = jnp.take(pooled, relay_from, axis=0)
    part_rows = lax.all_gather(latent, "tile", axis=0, tiled=True)
    cut_rows = jnp.take(latent, cut_list, axis=0).reshape(2, halo_rows, feat_dim)
    rim_rows = extended(cut_rows, (("dom", 0),), 1)
    row_table = jnp.concatenate([part_rows, rim_rows[0], rim_rows[3]], 0)
    send_rows = jnp.take(row_table, edge_sender, axis=0)
    send_term = flat_dot(send_rows, w_send)
    recv_rows = jnp.take(latent, edge_receiver, axis=0)
    recv_proj = flat_dot(latent, w_recv)
    edge_pre = (
        flat_dot(edge_latent, w_edge) + send_term + jnp.take(recv_proj, edge_receiver, axis=0)
    )
    edge_act = jax.nn.silu(edge_pre).astype(jnp.bfloat16)
    edge_lin = flat_dot(edge_act, edge_out)
    edge_normed, edge_inv = layer_norm(edge_lin)
    edge_new = (edge_latent.astype(jnp.float32) + edge_normed).astype(jnp.bfloat16)
    incidence = (edge_receiver[:, None] == jnp.arange(node_count, dtype=jnp.int32)[None, :]).astype(
        jnp.bfloat16
    )
    aggregate = inner_dot(incidence, edge_new).astype(jnp.bfloat16)
    node_pre = flat_dot(latent, w_node) + flat_dot(aggregate, w_agg)
    node_act = jax.nn.silu(node_pre).astype(jnp.bfloat16)
    node_lin = flat_dot(node_act, node_out)
    node_normed, node_inv = layer_norm(node_lin)
    node_new = (latent.astype(jnp.float32) + node_normed).astype(jnp.bfloat16)
    node_upstream = node_cot.astype(jnp.float32)
    node_lin_grad = norm_grad(node_normed, node_inv, node_upstream).astype(jnp.bfloat16)
    grad_node_out = inner_dot(node_act, node_lin_grad)
    node_pre_grad = (outer_dot(node_lin_grad, node_out) * silu_grad(node_pre)).astype(jnp.bfloat16)
    grad_node_in = jnp.concatenate(
        [inner_dot(latent, node_pre_grad), inner_dot(aggregate, node_pre_grad)], 0
    )
    node_direct = node_upstream + outer_dot(node_pre_grad, w_node)
    agg_grad = outer_dot(node_pre_grad, w_agg)
    edge_up = edge_cot.astype(jnp.float32) + jnp.take(agg_grad, edge_receiver, axis=0)
    edge_lin_grad = norm_grad(edge_normed, edge_inv, edge_up).astype(jnp.bfloat16)
    grad_edge_out = inner_dot(edge_act, edge_lin_grad)
    edge_pre_grad = (outer_dot(edge_lin_grad, edge_out) * silu_grad(edge_pre)).astype(jnp.bfloat16)
    edge_grad = (edge_up + outer_dot(edge_pre_grad, w_edge)).astype(jnp.bfloat16)
    recv_grad = split_sum(incidence, outer_dot(edge_pre_grad, w_recv))
    node_local = node_direct + recv_grad
    table_rows = part_count + 2 * halo_rows
    sender_onehot = (
        edge_sender[:, None] == jnp.arange(table_rows, dtype=jnp.int32)[None, :]
    ).astype(jnp.bfloat16)
    table_grad = split_sum(sender_onehot, outer_dot(edge_pre_grad, w_send))
    own_grad = lax.psum_scatter(table_grad[:part_count], "tile", scatter_dimension=0, tiled=True)
    rim_grad = extended(
        table_grad[part_count:].reshape(2, halo_rows, feat_dim).astype(jnp.bfloat16),
        (("dom", 0),),
        1,
    ).astype(jnp.float32)
    node_total = (
        node_local
        + own_grad
        + jax.ops.segment_sum(jnp.concatenate([rim_grad[0], rim_grad[3]], 0), cut_list, node_count)
    )
    send_weight = inner_dot(send_rows, edge_pre_grad)
    node_grad = node_total.astype(jnp.bfloat16)
    pool_grad = (
        jnp.zeros((node_count + dom_count * slot_count, feat_dim), jnp.bfloat16)
        .at[relay_from]
        .set(node_grad)
    )
    slot_back = lax.all_to_all(
        pool_grad[node_count:].reshape(dom_count, slot_count, feat_dim),
        "dom",
        split_axis=0,
        concat_axis=0,
        tiled=True,
    )
    latent_grad = (
        pool_grad[:node_count]
        .at[pick_list]
        .add(slot_back.reshape(dom_count * slot_count, feat_dim))
    )
    grad_edge_in = jnp.concatenate(
        [inner_dot(edge_latent, edge_pre_grad), send_weight, inner_dot(recv_rows, edge_pre_grad)], 0
    )
    weight_terms = jnp.concatenate([grad_edge_in, grad_edge_out, grad_node_in, grad_node_out], 0)
    by_rows = lax.psum_scatter(weight_terms, "dom", scatter_dimension=0, tiled=True)
    weight_shard = lax.psum_scatter(by_rows, "tile", scatter_dimension=1, tiled=True)
    return (node_new, edge_new, latent_grad, edge_grad, weight_shard)


def solution(mesh):
    in_specs = (
        P(("dom", "tile"), None),
        P(("dom", "tile"), None),
        P(("dom", "tile")),
        P(("dom", "tile"), None),
        P(("dom", "tile"), None),
        P(("dom", "tile")),
        P(("dom", "tile")),
        P(),
        P(),
        P(),
        P(),
        P(("dom", "tile"), None),
        P(("dom", "tile"), None),
    )
    out_specs = (
        P(("dom", "tile"), None),
        P(("dom", "tile"), None),
        P(("dom", "tile"), None),
        P(("dom", "tile"), None),
        P("dom", "tile"),
    )
    return jax.shard_map(body, mesh=mesh, in_specs=in_specs, out_specs=out_specs, check_vma=False)
```

profile of v0, /device:TPU:0, one launch (start us, length us, event | category | flops | bytes accessed | tf_op | source)
XLA Modules:
  0.0 274.3 jit_solution(5162832244070648056)
XLA Ops:
  9.2 1.3 reduce.3
  10.6 1.8 gather_fusion
  13.1 7.3 %all-to-all-start = ((bf16[8,16,512]{2,1,0:T(8,128)(2,1)}), bf16[8,16,512]{2,1,0:T(8,128)(2,1)S(1)}, u32[]{:S(2)}, u32[]{:S(2)}) async-start(bf16[8,16,512]{2,1,0:T(8,128)(2,1)} %broadcast_select_fusion.4), calls=%async_computation | async-start | bytes 262144 | tf_op jit(solution)/shard_map/all_to_all | solution.py:98
  20.6 2.9 %fusion.22 = f32[768,512]{1,0:T(8,128)} fusion(bf16[768,512]{1,0:T(8,128)(2,1)S(1)} %copy-done.9, bf16[1536,512]{1,0:T(8,128)(2,1)} %param.22), kind=kOutput, calls=%fused_computation.60 | convolution fusion | flops 402653184 | bytes 2883584 | tf_op jit(solution)/shard_map/dot_general | solution.py:43
  23.5 1.2 copy.24
  25.0 2.8 %all-to-all-done = bf16[8,16,512]{2,1,0:T(8,128)(2,1)S(1)} async-done(((bf16[8,16,512]{2,1,0:T(8,128)(2,1)}), bf16[8,16,512]{2,1,0:T(8,128)(2,1)S(1)}, u32[]{:S(2)}, u32[]{:S(2)}) %all-to-all-start) | async-done | bytes 131104 | tf_op jit(solution)/shard_map/all_to_all | solution.py:98
  27.8 0.8 gather_fusion.1
  28.7 1.3 fusion.16
  31.0 2.0 collective-permute-start.1
  33.0 7.3 %all_gather.3 = bf16[512,512]{1,0:T(8,128)(2,1)S(1)} all-gather(bf16[128,512]{1,0:T(8,128)(2,1)S(1)} %broadcast_select_fusion.3), channel_id=1, replica_groups=mesh['dom'=8,'tile'=4] {'tile'}, dimensions={0}, use_global_device_ids=true | all-gather | bytes 655360 | tf_op jit(solution)/shard_map/all_gather | solution.py:101
  40.4 3.3 %gather_fusion.4 = bf16[768,512]{1,0:T(8,128)(2,1)} fusion(bf16[128,512]{1,0:T(8,128)(2,1)S(1)} %broadcast_select_fusion.3, s32[1024]{0:T(1024)S(1)} %get-tuple-element.35), kind=kCustom, calls=%fused_computation.6 | custom fusion | bytes 1575936 | tf_op jit(solution)/shard_map/jit(_take)/gather | solution.py:107
  43.7 3.1 %gather_fusion.5 = f32[768,512]{1,0:T(8,128)} fusion(f32[128,512]{1,0:T(8,128)S(1)} %fusion.16, s32[1024]{0:T(1024)S(1)} %get-tuple-element.35), kind=kCustom, calls=%fused_computation.clone | custom fusion | bytes 3148800 | tf_op jit(solution)/shard_map/jit(_take)/gather | solution.py:110
  46.8 2.7 gather_fusion.3
  49.6 2.9 %select_add_fusion.1 = f32[768,512]{1,0:T(8,128)S(1)} fusion(f32[768,512]{1,0:T(8,128)} %gather_fusion.5, f32[768,512]{1,0:T(8,128)} %fusion.22, pred[768]{0:T(1024)(128)(4,1)S(1)} %get-tuple-element.39, bf16[1536,512]{1,0:T(8,128)(2,1)} %param.22, bf16[768,512]{1,0:T(8,128)(2,1)S(1)} %gather_fusion.3, pred[768]{0:T(1024)(128)(4,1)S(1)} %get-tuple-element.40), kind=kOutput, calls=%fused_computation.14 | convolution fusion | flops 404226048 | bytes 6030848 | tf_op jit(solution)/shard_map/dot_general | solution.py:43
  52.5 1.2 copy-done.14
  54.7 1.5 copy-done.11
  58.4 0.9 convert_reduce_fusion
  60.0 3.1 %gather_fusion.6 = f32[768,512]{1,0:T(8,128)} fusion(f32[128,512]{1,0:T(8,128)S(1)} %fusion.11, s32[1024]{0:T(1024)S(1)} %get-tuple-element.35), kind=kCustom, calls=%fused_computation.1.clone | custom fusion | bytes 3148800 | tf_op jit(solution)/shard_map/jit(_take)/gather | solution.py:134
  63.1 1.9 copy.26
  65.1 2.0 fusion.55
  67.6 0.8 copy-done.15
  68.5 0.9 multiply_convert_fusion
  69.6 1.6 fusion.3
  71.2 1.7 convolution_dynamic-update-slice_fusion.2
  72.9 1.7 convolution_dynamic-update-slice_fusion.1
  74.6 1.6 convolution_dynamic-update-slice_fusion
  76.2 1.3 convolution_dynamic-update-slice_fusion.5
  77.5 1.3 convolution_dynamic-update-slice_fusion.4
  78.9 1.4 convolution_dynamic-update-slice_fusion.3
  80.6 1.9 fusion.18
  82.5 0.9 fusion
  83.4 1.8 fusion.62
  85.1 1.2 slice.95
  86.4 127.4 %reduce-scatter.6.cloned.1.call-done = f32[448,512]{1,0:T(8,128)} async-done(((f32[3584,512]{1,0:T(8,128)}), f32[448,512]{1,0:T(8,128)}) %reduce-scatter.6.cloned.1.call-update) | async-done | bytes 917520 | tf_op jit(solution)/shard_map/reduce_scatter | solution.py:180
  214.6 2.4 collective-permute-start.3
  216.9 1.9 fusion.14
  219.3 1.2 convolution_add_fusion
  220.5 2.3 copy.28
  223.6 16.7 %reduce-scatter.4.cloned.1.call-done = f32[128,512]{1,0:T(8,128)} async-done(((f32[512,512]{1,0:T(8,128)}), f32[128,512]{1,0:T(8,128)}) %reduce-scatter.4.cloned.1.call-update) | async-done | bytes 262160 | tf_op jit(solution)/shard_map/reduce_scatter | solution.py:146
  240.3 1.5 fusion.5
  241.8 1.0 scatter_custom_fusion
  242.9 1.3 scatter_custom_fusion.1
  244.8 5.5 %all-to-all-start.1 = ((bf16[8,16,512]{2,1,0:T(8,128)(2,1)}), bf16[8,16,512]{2,1,0:T(8,128)(2,1)S(1)}, u32[]{:S(2)}, u32[]{:S(2)}) async-start(bf16[8,16,512]{2,1,0:T(8,128)(2,1)} %bitcast.16), calls=%async_computation.2 | async-start | bytes 262144 | tf_op jit(solution)/shard_map/all_to_all | solution.py:164
  250.3 2.9 %add_convert_fusion = bf16[768,512]{0,1:T(8,128)(2,1)} fusion(bf16[768,512]{1,0:T(8,128)(2,1)} %copy-done.5, bf16[1536,512]{1,0:T(8,128)(2,1)} %param.22, f32[768,512]{0,1:T(8,128)S(1)} %copy.26, pred[768]{0:T(1024)(128)(4,1)S(1)} %copy-done.27, bf16[768,512]{0,1:T(8,128)(2,1)S(1)} %copy.25), kind=kOutput, calls=%fused_computation.15 | convolution fusion | flops 404619264 | bytes 4457216 | tf_op jit(solution)/shard_map/dot_general | solution.py:53
  253.2 2.3 copy.29
  255.5 2.2 all-to-all-done.1
  257.7 1.5 scatter_fusion
  259.2 8.6 %reduce-scatter.8.cloned.1.call-done = f32[448,128]{1,0:T(8,128)} async-done(((f32[448,512]{1,0:T(8,128)}), f32[448,128]{1,0:T(8,128)}) %reduce-scatter.8.cloned.1.call-update) | async-done | bytes 229392 | tf_op jit(solution)/shard_map/reduce_scatter | solution.py:181
  (143 shorter events, 12.0 us)
Async XLA Ops:
  7.2 46.5 %copy-start = (bf16[512,512]{1,0:T(8,128)(2,1)S(1)}, bf16[512,512]{1,0:T(8,128)(2,1)}, u32[]{:S(2)}) copy-start(bf16[512,512]{1,0:T(8,128)(2,1)} %param.23) | copy-start | bytes 1572868
  7.2 13.3 %copy-start.39 = (s32[1,32]{1,0:T(1,128)S(1)}, s32[1,32]{1,0:T(1,128)}, u32[]{:S(2)}) copy-start(s32[1,32]{1,0:T(1,128)} %param.18) | copy-start | bytes 388
  7.2 13.3 %copy-start.38 = (s32[128]{0:T(128)S(1)}, s32[128]{0:T(128)}, u32[]{:S(2)}) copy-start(s32[128]{0:T(128)} %param.17) | copy-start | bytes 1540
  7.2 13.3 %copy-start.23 = (s32[768]{0:T(1024)S(1)}, s32[768]{0:T(1024)}, u32[]{:S(2)}) copy-start(s32[768]{0:T(1024)} %param.21) | copy-start | bytes 9220
  7.2 13.3 %copy-start.24 = (s32[768]{0:T(1024)S(1)}, s32[768]{0:T(1024)}, u32[]{:S(2)}) copy-start(s32[768]{0:T(1024)} %param.20) | copy-start | bytes 9220
  7.2 13.4 %copy-start.9 = (bf16[768,512]{1,0:T(8,128)(2,1)S(1)}, bf16[768,512]{1,0:T(8,128)(2,1)}, u32[]{:S(2)}) copy-start(bf16[768,512]{1,0:T(8,128)(2,1)} %param.19) | copy-start | bytes 2359300
  8.6 14.8 %copy-start.30 = (s32[128]{0:T(128)}, s32[128]{0:T(128)S(1)}, u32[]{:S(2)}) copy-start(s32[128]{0:T(128)S(1)} %fusion.49) | copy-start | bytes 1540
  13.1 14.6 %all-to-all-start = ((bf16[8,16,512]{2,1,0:T(8,128)(2,1)}), bf16[8,16,512]{2,1,0:T(8,128)(2,1)S(1)}, u32[]{:S(2)}, u32[]{:S(2)}) async-start(bf16[8,16,512]{2,1,0:T(8,128)(2,1)} %broadcast_select_fusion.4), calls=%async_computation | async-start | bytes 262144 | tf_op jit(solution)/shard_map/all_to_all | solution.py:98
  20.4 193.4 %reduce-scatter.6.cloned.1.call-start = ((), (), s32[]{:S(2)}) async-start(), calls=%async_computation.6 | async-start | bytes 8257536 | tf_op jit(solution)/shard_map/reduce_scatter | solution.py:180
  20.5 4.2 %copy-start.34 = (s32[128]{0:T(128)}, s32[128]{0:T(128)S(1)}, u32[]{:S(2)}) copy-start(s32[128]{0:T(128)S(1)} %compare_select_fusion.6) | copy-start | bytes 1540
  20.6 4.1 %copy-start.17 = (bf16[768,512]{1,0:T(8,128)(2,1)S(1)}, bf16[768,512]{1,0:T(8,128)(2,1)}, u32[]{:S(2)}) copy-start(bf16[768,512]{1,0:T(8,128)(2,1)} %param.27) | copy-start | bytes 2359300
  23.5 4.3 %copy-start.4 = (bf16[128,512]{1,0:T(8,128)(2,1)S(1)}, bf16[128,512]{1,0:T(8,128)(2,1)}, u32[]{:S(2)}) copy-start(bf16[128,512]{1,0:T(8,128)(2,1)} %param.15) | copy-start | bytes 393220
  24.9 5.1 %copy-start.7 = (bf16[1024,512]{1,0:T(8,128)(2,1)S(1)}, bf16[1024,512]{1,0:T(8,128)(2,1)}, u32[]{:S(2)}) copy-start(bf16[1024,512]{1,0:T(8,128)(2,1)} %param.24) | copy-start | bytes 3145732
  25.0 24.6 %copy-start.26 = (pred[768]{0:T(1024)(128)(4,1)}, pred[768]{0:T(1024)(128)(4,1)S(1)}, u32[]{:S(2)}) copy-start(pred[768]{0:T(1024)(128)(4,1)S(1)} %get-tuple-element.39) | copy-start | bytes 2308
  25.0 24.6 %copy-start.28 = (pred[768]{0:T(1024)(128)(4,1)}, pred[768]{0:T(1024)(128)(4,1)S(1)}, u32[]{:S(2)}) copy-start(pred[768]{0:T(1024)(128)(4,1)S(1)} %get-tuple-element.40) | copy-start | bytes 2308
  31.0 15.8 %collective-permute-start.1 = (bf16[1,16,512]{2,1,0:T(8,128)(2,1)S(1)}, bf16[1,16,512]{2,1,0:T(8,128)(2,1)S(1)}, u32[]{:S(2)}, u32[]{:S(2)}) collective-permute-start(bf16[1,16,512]{2,1,0:T(8,128)(2,1)S(1)} %get-tuple-element.28), channel_id=1, source_target_pairs={{4,0},{8,4},{12,8},{16,12},{20,16},{24,20},{28,24},{0,28},{5,1},{9... | collective-permute-start | bytes 49160 | tf_op jit(solution)/shard_map/ppermute | solution.py:18
  32.9 13.9 %collective-permute-start = (bf16[1,16,512]{2,1,0:T(8,128)(2,1)S(1)}, bf16[1,16,512]{2,1,0:T(8,128)(2,1)S(1)}, u32[]{:S(2)}, u32[]{:S(2)}) collective-permute-start(bf16[1,16,512]{2,1,0:T(8,128)(2,1)S(1)} %get-tuple-element.27), channel_id=1, source_target_pairs={{0,4},{4,8},{8,12},{12,16},{16,20},{20,24},{24,28},{28,0},{1,5},{5... | collective-permute-start | bytes 49160 | tf_op jit(solution)/shard_map/ppermute | solution.py:16
  49.5 3.0 %copy-start.12 = (bf16[768,512]{1,0:T(8,128)(2,1)}, bf16[768,512]{1,0:T(8,128)(2,1)S(1)}, u32[]{:S(2)}) copy-start(bf16[768,512]{1,0:T(8,128)(2,1)S(1)} %gather_fusion.3) | copy-start | bytes 2359300
  54.5 2.0 copy-start.1
  54.5 1.7 copy-start.11
  56.2 1.3 copy-start.8
  56.4 1.8 copy-start.6
  56.4 1.4 copy-start.37
  57.9 1.8 copy-start.21
  58.2 1.5 copy-start.32
  58.4 1.2 copy-start.35
  63.1 1.9 copy-start.27
  65.0 2.0 copy-start.2
  67.1 1.4 copy-start.15
  69.6 3.3 %copy-start.5 = (bf16[768,512]{1,0:T(8,128)(2,1)}, bf16[768,512]{1,0:T(8,128)(2,1)S(1)}, u32[]{:S(2)}) copy-start(bf16[768,512]{1,0:T(8,128)(2,1)S(1)} %multiply_convert_fusion) | copy-start | bytes 2359300
  69.6 1.6 copy-start.13
  69.6 1.6 copy-start.29
  71.2 1.7 copy-start.16
  76.2 2.7 copy-start.19
  76.2 2.7 copy-start.22
  76.2 2.7 copy-start.33
  76.2 2.7 copy-start.36
  76.2 2.7 copy-start.41
  76.2 2.7 copy-start.43
  80.3 2.2 copy-start.25
  80.3 160.0 %reduce-scatter.4.cloned.1.call-start = ((), (), s32[]{:S(2)}) async-start(), calls=%async_computation.5 | async-start | bytes 1310720 | tf_op jit(solution)/shard_map/reduce_scatter | solution.py:146
  86.3 181.5 %reduce-scatter.8.cloned.1.call-start = ((), (), s32[]{:S(2)}) async-start(), calls=%async_computation.7 | async-start | bytes 1146880 | tf_op jit(solution)/shard_map/reduce_scatter | solution.py:181
  214.6 9.0 %collective-permute-start.3 = (bf16[1,16,512]{2,1,0:T(8,128)(2,1)S(1)}, bf16[1,16,512]{2,1,0:T(8,128)(2,1)S(1)}, u32[]{:S(2)}, u32[]{:S(2)}) collective-permute-start(bf16[1,16,512]{2,1,0:T(8,128)(2,1)S(1)} %get-tuple-element.21), channel_id=1, source_target_pairs={{4,0},{8,4},{12,8},{16,12},{20,16},{24,20},{28,24},{0,28},{5,1},{9... | collective-permute-start | bytes 49160 | tf_op jit(solution)/shard_map/ppermute | solution.py:18
  216.9 6.7 %collective-permute-start.2 = (bf16[1,16,512]{2,1,0:T(8,128)(2,1)S(1)}, bf16[1,16,512]{2,1,0:T(8,128)(2,1)S(1)}, u32[]{:S(2)}, u32[]{:S(2)}) collective-permute-start(bf16[1,16,512]{2,1,0:T(8,128)(2,1)S(1)} %get-tuple-element.20), channel_id=1, source_target_pairs={{0,4},{4,8},{8,12},{12,16},{16,20},{20,24},{24,28},{28,0},{1,5},{5... | collective-permute-start | bytes 49160 | tf_op jit(solution)/shard_map/ppermute | solution.py:16
  219.3 21.0 %copy-start.20 = (bf16[128,512]{1,0:T(8,128)(2,1)S(1)}, bf16[128,512]{1,0:T(8,128)(2,1)}, u32[]{:S(2)}) copy-start(bf16[128,512]{1,0:T(8,128)(2,1)} %param.26) | copy-start | bytes 393220
  244.8 12.9 %all-to-all-start.1 = ((bf16[8,16,512]{2,1,0:T(8,128)(2,1)}), bf16[8,16,512]{2,1,0:T(8,128)(2,1)S(1)}, u32[]{:S(2)}, u32[]{:S(2)}) async-start(bf16[8,16,512]{2,1,0:T(8,128)(2,1)} %bitcast.16), calls=%async_computation.2 | async-start | bytes 262144 | tf_op jit(solution)/shard_map/all_to_all | solution.py:164
  253.2 4.5 %copy-start.31 = (s32[128]{0:T(128)S(1)}, s32[128]{0:T(128)}, u32[]{:S(2)}) copy-start(s32[128]{0:T(128)} %copy-done.30) | copy-start | bytes 1540
  259.1 8.6 %copy-start.3 = (bf16[128,512]{1,0:T(8,128)(2,1)}, bf16[128,512]{1,0:T(8,128)(2,1)S(1)}, u32[]{:S(2)}) copy-start(bf16[128,512]{1,0:T(8,128)(2,1)S(1)} %scatter_fusion) | copy-start | bytes 393220
  (5 other events, 4.6 us)
Sparse Core Ops, SparseCore 0:
  80.4 133.3 reduce-scatter.5
  216.3 23.9 reduce-scatter.3
  243.6 24.0 reduce-scatter.7
where the time goes:
time: 275 us; the launch traced here: 274 us
  waiting for transfers between devices  158 us (57%)
  matrix products  33.8 us (12%)
  local copies, waits for them, and re-layouts  31.8 us (12%)
  starting transfers between devices  17.6 us (6%)
  between operations  14.4 us (5%)
  other arithmetic  11.5 us (4%)
  blocking collectives  7.34 us (3%)
    reduce_scatter x1, waiting for transfers between devices, body(): lax.psum_scatter(weight_terms, 'dom', scatter_dimension=0, tiled=True)  127 us
    reduce_scatter x1, waiting for transfers between devices, body(): lax.psum_scatter(table_grad[:part_count], 'tile', scatter_dimension=0, ti...  16.7 us
    dot_general x12, matrix products, inner_dot(): lax.dot_general(left_mat, right_mat, (((0,), (0,)), ((), ())), preferred_...  15.5 us
    unnamed x93, local copies, waits for them, and re-layouts  11 us
    dot_general x7, matrix products, outer_dot(): lax.dot_general(left_mat, right_mat, (((1,), (1,)), ((), ())), preferred_...  9.66 us
    reduce_scatter x1, waiting for transfers between devices, body(): lax.psum_scatter(by_rows, 'tile', scatter_dimension=1, tiled=True)  8.61 us
    dot_general x7, matrix products, flat_dot(): return jnp.dot(left_mat, right_mat, preferred_element_type=jnp.float32)  8.6 us
    all_gather x1, blocking collectives, body(): part_rows = lax.all_gather(latent, 'tile', axis=0, tiled=True)  7.34 us
  transfers between devices with their start and end apart: 9, of which 5 were waited for; matrix products, arithmetic and copies ran while one was open for 13% of the time, Pallas kernels for 0%

commit v1 on v0

v1 whole, which is shorter than its diff:
```python
import functools

import jax
import jax.numpy as jnp
from jax import lax
from jax.experimental import pallas as pl
from jax.experimental.pallas import tpu as pltpu
from jax.sharding import PartitionSpec as P

EPSILON = 1e-05
BF16 = jnp.bfloat16
F32 = jnp.float32
ROWS = 256
CHUNK = 32
VMEM_LIMIT = 30 * 1024 * 1024
SMALL_LIMIT = 8 * 1024 * 1024


def layer_norm(values):
    center = values - jnp.mean(values, -1, keepdims=True)
    inverse = lax.rsqrt(jnp.mean(center * center, -1, keepdims=True) + EPSILON)
    return (center * inverse, inverse)


def norm_grad(normed, inverse, upstream):
    mean_up = jnp.mean(upstream, -1, keepdims=True)
    mean_cross = jnp.mean(upstream * normed, -1, keepdims=True)
    return inverse * (upstream - mean_up - normed * mean_cross)


def silu_pair(values):
    sigmoid = 0.5 * jnp.tanh(0.5 * values) + 0.5
    return values * sigmoid, sigmoid * (1.0 + values * (1.0 - sigmoid))


def flat_dot(left_mat, right_mat):
    return jnp.dot(left_mat, right_mat, preferred_element_type=F32)


def inner_dot(left_mat, right_mat):
    return lax.dot_general(
        left_mat, right_mat, (((0,), (0,)), ((), ())), preferred_element_type=F32
    )


def outer_dot(left_mat, right_mat):
    return lax.dot_general(
        left_mat, right_mat, (((1,), (1,)), ((), ())), preferred_element_type=F32
    )


def split_parts(values):
    high_part = values.astype(BF16)
    return high_part, (values - high_part.astype(F32)).astype(BF16)


def marks(hits):
    return jnp.where(hits, 1.0, 0.0).astype(BF16)


def hot_columns(index_row, count, first=0):
    shape = (count, index_row.shape[-1])
    at = lax.broadcasted_iota(jnp.int32, shape, 0) + first
    return marks(jnp.broadcast_to(index_row.reshape(1, -1), shape) == at)


def as_column(index_row):
    shape = (128, index_row.shape[-1])
    return jnp.transpose(jnp.broadcast_to(index_row.reshape(1, -1), shape))


def hot_rows(index_column, count):
    at = lax.broadcasted_iota(jnp.int32, index_column.shape, 1)
    return jnp.concatenate(
        [marks(index_column == at + 128 * k) for k in range(count // 128)], 1
    )


class Kept:
    def __init__(self, array):
        self.array = array


def call(kernel, name, outs, ins, scratch, scalars=(), limit=VMEM_LIMIT):
    def spec(array):
        return pl.BlockSpec(memory_space=pltpu.VMEM if isinstance(array, Kept) else pltpu.HBM)

    def placed(array):
        if isinstance(array, Kept):
            return array.array
        return pltpu.with_memory_space_constraint(array, pltpu.HBM)

    shapes = [
        pltpu.SemaphoreType.DMA((s,)) if isinstance(s, int) else pltpu.VMEM(s.shape, s.dtype)
        for s in scratch
    ]
    return pl.pallas_call(
        kernel,
        out_shape=[
            array.array if isinstance(array, Kept) else pltpu.HBM(array.shape, array.dtype)
            for array in outs
        ],
        in_specs=[pl.BlockSpec(memory_space=pltpu.SMEM)] * len(scalars) + [spec(a) for a in ins],
        out_specs=[spec(array) for array in outs],
        scratch_shapes=shapes,
        compiler_params=pltpu.CompilerParams(vmem_limit_bytes=limit),
        name=name,
    )(*scalars, *[placed(array) for array in ins])


class Copies:
    def __init__(self, sems):
        self.sems = sems
        self.made = 0
        self.open = []

    def start(self, source, target):
        copy = pltpu.make_async_copy(source, target, self.sems.at[self.made])
        copy.start()
        self.made += 1
        self.open.append(copy)
        return copy

    def finish(self):
        for copy in self.open:
            copy.wait()


def pick_kernel(pick_hbm, tile_hbm, out_ref, pick_ref, pick, tile, in_sems):
    loads = Copies(in_sems)
    loads.start(pick_hbm, pick)
    loads.start(tile_hbm, tile)
    loads.finish()
    pick_ref[...] = pick[...]
    rows = hot_rows(as_column(pick[...]), tile.shape[0])
    out_ref[...] = flat_dot(rows, tile[...]).astype(BF16)


def pool_kernel(
    where_ref,
    from_hbm,
    cut_hbm,
    tile_hbm,
    came_ref,
    latent_ref,
    first_ref,
    second_ref,
    from_ref,
    cut_ref,
    at,
    cut,
    tile,
    ends,
    in_sems,
):
    loads = Copies(in_sems)
    for source, target in ((from_hbm, at), (cut_hbm, cut), (tile_hbm, tile)):
        loads.start(source, target)
    loads.finish()
    from_ref[...] = at[...].reshape(from_ref.shape)
    cut_ref[...] = cut[...]
    nodes = tile.shape[0]
    halo = first_ref.shape[0]
    rows = hot_rows(as_column(at[...]), nodes + came_ref.shape[0])
    value = flat_dot(rows[:, :nodes], tile[...]) + flat_dot(rows[:, nodes:], came_ref[...])
    value = value.astype(BF16)
    latent_ref[...] = value
    ends[...] = inner_dot(hot_columns(cut[...], nodes), value).astype(BF16)
    turn = pl.multiple_of(where_ref[2], halo)
    first_ref[...] = ends[pl.ds(turn, halo), :]
    second_ref[...] = ends[pl.ds(halo - turn, halo), :]


def base_kernel(
    receiver_hbm,
    edge_hbm,
    edge_in_hbm,
    edge_out_hbm,
    latent_ref,
    base_ref,
    w_send_ref,
    edge_out_ref,
    receiver,
    edge_lat,
    w_edge,
    w_recv,
    in_sems,
):
    feat = edge_out_ref.shape[0]
    loads = Copies(in_sems)
    first = [
        loads.start(receiver_hbm, receiver),
        loads.start(edge_hbm, edge_lat),
        loads.start(edge_in_hbm.at[0:feat], w_edge),
        loads.start(edge_in_hbm.at[2 * feat : 3 * feat], w_recv),
    ]
    second = [
        loads.start(edge_in_hbm.at[feat : 2 * feat], w_send_ref),
        loads.start(edge_out_hbm, edge_out_ref),
    ]
    for copy in first:
        copy.wait()
    column = as_column(receiver[...])
    latent = latent_ref[...]
    for at in range(0, edge_lat.shape[0], ROWS):
        rows = slice(at, at + ROWS)
        taken = flat_dot(hot_rows(column[rows], latent.shape[0]), latent).astype(BF16)
        base_ref[rows, :] = flat_dot(edge_lat[rows, :], w_edge[...]) + flat_dot(taken, w_recv[...])
    for copy in second:
        copy.wait()


def put(weights, first, terms):
    for t in range(terms.shape[1] // 128):
        weights[t, first : first + terms.shape[0], :] = terms[:, t * 128 : (t + 1) * 128].astype(
            BF16
        )


def block_kernel(
    places,
    where_ref,
    sender_hbm,
    receiver_hbm,
    latent_ref,
    near_ref,
    far_ref,
    cross_ref,
    first_ref,
    second_ref,
    base_ref,
    w_send,
    edge_out,
    edge_hbm,
    edge_t_hbm,
    w_recv_hbm,
    node_in_hbm,
    node_out_hbm,
    node_cot_hbm,
    edge_cot_hbm,
    node_new_hbm,
    edge_new_hbm,
    pre_grad_hbm,
    agg_parts_hbm,
    local_ref,
    keep_upper_ref,
    keep_lower_ref,
    send_upper_ref,
    send_lower_ref,
    own_ref,
    opposite_ref,
    back_first_ref,
    back_second_ref,
    sender,
    receiver,
    table,
    edge_lat,
    edge_t,
    picked,
    w_recv,
    node_x,
    node_in,
    node_out,
    node_cot,
    edge_cot,
    node_new,
    node_act,
    node_lin_grad,
    node_pre_grad,
    agg_parts,
    node_work,
    node_slope,
    edge_new,
    act,
    lin_grad,
    pre_grad,
    work,
    slope,
    normed,
    inverse,
    edge_up,
    back_work,
    weights,
    sums,
    core_sums,
    in_sems,
    out_sems,
):
    feat = edge_out.shape[0]
    nodes = node_cot.shape[0]
    edges = edge_lat.shape[0]
    halo = first_ref.shape[0]
    tiles, _, width = weights.shape
    core = where_ref[0]
    tile = where_ref[1]
    turn = pl.multiple_of(where_ref[2], halo)
    part = tiles * nodes
    held = part + 2 * halo
    loads = Copies(in_sems)
    stores = Copies(out_sems)

    def rows_of(mask):
        return pl.ds(pl.multiple_of((tile ^ mask) * nodes, nodes), nodes)

    first = [
        loads.start(sender_hbm, sender),
        loads.start(receiver_hbm, receiver),
    ]
    second = [loads.start(edge_hbm, edge_lat)]
    third = [
        loads.start(node_in_hbm, node_in),
        loads.start(node_out_hbm, node_out),
        loads.start(node_cot_hbm, node_cot),
    ]
    fourth = [loads.start(edge_cot_hbm, edge_cot)]
    fifth = [
        loads.start(edge_t_hbm, edge_t),
        loads.start(w_recv_hbm.at[2 * feat : 3 * feat], w_recv),
    ]

    for mask, ref in enumerate((latent_ref, near_ref, far_ref, cross_ref)):
        table[rows_of(mask), :] = ref[...]
    table[pl.ds(part + turn, halo), :] = first_ref[...]
    table[pl.ds(part + halo - turn, halo), :] = second_ref[...]
    table[held:, :] = jnp.zeros((table.shape[0] - held, feat), BF16)
    for copy in first:
        copy.wait()
    latent = latent_ref[...]
    node_x[:, 0:feat] = latent
    sender_column = as_column(sender[...])
    receiver_hot = hot_rows(as_column(receiver[...]), nodes)
    receiver_rows = hot_columns(receiver[...], nodes)
    blocks = [slice(at, at + ROWS) for at in range(0, edges, ROWS)]

    def chunks(rows):
        return [slice(at, at + CHUNK) for at in range(rows.start, rows.stop, CHUNK)]

    for rows in blocks:
        hot = hot_rows(sender_column[rows], table.shape[0])
        picked[rows, :] = flat_dot(hot, table[...]).astype(BF16)
    for rows in blocks:
        work[rows, :] = flat_dot(picked[rows, :], w_send[...])
        for c in chunks(rows):
            value, slope[c, :] = silu_pair(base_ref[c, :] + work[c, :])
            act[c, :] = value.astype(BF16)
        normed[rows, :] = flat_dot(act[rows, :], edge_out[...])
        if rows.start == 0:
            for copy in second:
                copy.wait()
        for c in chunks(rows):
            value, scale = layer_norm(normed[c, :])
            normed[c, :] = value
            inverse[c, :] = scale
            edge_new[c, :] = (edge_lat[c, :].astype(F32) + value).astype(BF16)
    stores.start(edge_new, edge_new_hbm)
    node_x[:, feat:] = flat_dot(receiver_rows, edge_new[...]).astype(BF16)

    for copy in third:
        copy.wait()
    node_rows = slice(0, nodes)
    node_work[...] = flat_dot(node_x[...], node_in[...])
    for c in chunks(node_rows):
        value, node_slope[c, :] = silu_pair(node_work[c, :])
        node_act[c, :] = value.astype(BF16)
    node_work[...] = flat_dot(node_act[...], node_out[...])
    for c in chunks(node_rows):
        value, scale = layer_norm(node_work[c, :])
        node_new[c, :] = (node_x[c, 0:feat].astype(F32) + value).astype(BF16)
        up = node_cot[c, :].astype(F32)
        node_lin_grad[c, :] = norm_grad(value, scale, up).astype(BF16)
    stores.start(node_new, node_new_hbm)
    node_work[...] = outer_dot(node_lin_grad[...], node_out[...])
    for c in chunks(node_rows):
        node_pre_grad[c, :] = (node_work[c, :] * node_slope[c, :]).astype(BF16)
    node_work[...] = outer_dot(node_pre_grad[...], node_in[feat:, :])
    for c in chunks(node_rows):
        agg_parts[c, :], low_part = split_parts(node_work[c, :])
        agg_parts[slice(c.start + nodes, c.stop + nodes), :] = low_part
    stores.start(agg_parts, agg_parts_hbm)

    for copy in fourth:
        copy.wait()
    for rows in blocks:
        hot = receiver_hot[rows]
        edge_up[rows, :] = flat_dot(jnp.concatenate([hot, hot], 1), agg_parts[...])
        for c in chunks(rows):
            up = edge_cot[c, :].astype(F32) + edge_up[c, :]
            edge_up[c, :] = up
            lin_grad[c, :] = norm_grad(normed[c, :], inverse[c, :], up).astype(BF16)
        back_work[rows, :] = outer_dot(lin_grad[rows, :], edge_out[...])
        for c in chunks(rows):
            pre_grad[c, :] = (back_work[c, :] * slope[c, :]).astype(BF16)
    stores.start(pre_grad, pre_grad_hbm)
    taken = flat_dot(receiver_rows, pre_grad[...])

    def give(which, keep_ref, send_ref):
        for source, rows, first, count in places[which]:
            to = pl.ds(first, count)
            stores.start(weights.at[2 * source + core, rows], keep_ref.at[to])
            stores.start(weights.at[2 * source + 1 - core, rows], send_ref.at[to])

    part_rows = sums.shape[0] // 2
    for start in (0, part_rows):
        sums[start : start + part_rows, :] = flat_dot(
            hot_columns(sender[...], part_rows, start), pre_grad[...]
        )
    back_first_ref[...] = sums[pl.ds(part + turn, halo), :].astype(BF16)
    back_second_ref[...] = sums[pl.ds(part + halo - turn, halo), :].astype(BF16)
    for mask, ref, first in (
        (0, own_ref, 0),
        (2, opposite_ref, 0),
        (1, core_sums, 0),
        (3, core_sums, part),
    ):
        value = sums[rows_of(mask), :].astype(ref.dtype)
        for at in range(tiles):
            lanes = slice(at * width, (at + 1) * width)
            ref[first + at * nodes : first + (at + 1) * nodes, :] = value[:, lanes]
    stores.start(core_sums, send_upper_ref.at[pl.ds(send_lower_ref.shape[0], 2 * part)])
    put(weights, 4 * feat, inner_dot(node_x[...], node_pre_grad[...]))
    put(weights, 6 * feat, inner_dot(node_act[...], node_lin_grad[...]))
    put(weights, 3 * feat, inner_dot(act[...], lin_grad[...]))
    give(0, keep_upper_ref, send_upper_ref)
    high_part, low_part = split_parts(taken)
    put(weights, 2 * feat, inner_dot(latent, high_part) + inner_dot(latent, low_part))
    put(weights, feat, inner_dot(picked[...], pre_grad[...]))
    for copy in fifth:
        copy.wait()
    put(weights, 0, flat_dot(edge_t[...], pre_grad[...]))
    give(1, keep_lower_ref, send_lower_ref)
    local_ref[...] = (
        node_cot[...].astype(F32)
        + outer_dot(node_pre_grad[...], node_in[0:feat, :])
        + (outer_dot(high_part, w_recv[...]) + outer_dot(low_part, w_recv[...]))
    )
    stores.finish()


def edge_grad_kernel(
    receiver_hbm,
    pre_grad_hbm,
    edge_cot_hbm,
    w_hbm,
    agg_parts_hbm,
    out_hbm,
    receiver,
    pre_grad,
    edge_cot,
    w_edge,
    agg_parts,
    work,
    out,
    in_sems,
    out_sems,
):
    loads, stores = Copies(in_sems), Copies(out_sems)
    for source, target in (
        (receiver_hbm, receiver),
        (agg_parts_hbm, agg_parts),
        (w_hbm.at[0 : w_edge.shape[0]], w_edge),
        (pre_grad_hbm, pre_grad),
        (edge_cot_hbm, edge_cot),
    ):
        loads.start(source, target)
    loads.finish()
    column = as_column(receiver[...])
    for at in range(0, out.shape[0], ROWS):
        rows = slice(at, at + ROWS)
        hot = hot_rows(column[rows], agg_parts.shape[0] // 2)
        work[rows, :] = flat_dot(jnp.concatenate([hot, hot], 1), agg_parts[...]) + outer_dot(
            pre_grad[rows, :], w_edge[...]
        )
        for start in range(at, at + ROWS, CHUNK):
            c = slice(start, start + CHUNK)
            out[c, :] = (edge_cot[c, :].astype(F32) + work[c, :]).astype(BF16)
        stores.start(out.at[rows], out_hbm.at[rows])
    stores.finish()


def node_kernel(
    where_ref,
    from_ref,
    cut_ref,
    w_send_ref,
    local_ref,
    total_ref,
    first_ref,
    second_ref,
    stay_ref,
    slot_ref,
    ends,
):
    nodes, feat = local_ref.shape
    halo = first_ref.shape[0]
    width = total_ref.shape[1]
    turn = pl.multiple_of(where_ref[2], halo)
    ends[pl.ds(turn, halo), :] = first_ref[...]
    ends[pl.ds(halo - turn, halo), :] = second_ref[...]
    value = jnp.concatenate(
        [total_ref[block * nodes : (block + 1) * nodes, :] for block in range(feat // width)], 1
    )
    value = value + flat_dot(hot_columns(cut_ref[...], nodes), ends[...])
    high_part, low_part = split_parts(value)
    w_send = w_send_ref[...]
    grad = local_ref[...] + (outer_dot(high_part, w_send) + outer_dot(low_part, w_send))
    grad = grad.astype(BF16)
    where = from_ref[...]
    slot_ref[...] = flat_dot(hot_columns(where, slot_ref.shape[0], nodes), grad).astype(BF16)
    stay_ref[...] = flat_dot(hot_columns(where, nodes), grad).astype(BF16)


def back_kernel(pick_ref, stay_ref, came_ref, out_hbm, out, out_sems):
    stores = Copies(out_sems)
    hot = hot_columns(pick_ref[...], stay_ref.shape[0])
    out[...] = (stay_ref[...].astype(F32) + flat_dot(hot, came_ref[...])).astype(BF16)
    stores.start(out, out_hbm)
    stores.finish()


def flip(values, axis, mask):
    count = lax.axis_size(axis)
    return lax.ppermute(values, axis, [(i, i ^ mask) for i in range(count)])


def meet(values, axis, step):
    count = lax.axis_size(axis)
    pairs = [(i, (i + (step if i % 2 == 0 else -step)) % count) for i in range(count)]
    return lax.ppermute(values, axis, pairs)


def axis_bits(axis):
    return [(axis, b) for b in range(lax.axis_size(axis).bit_length() - 1)]


def exchange_orders():
    cross, dom_bits = axis_bits("tile")[1:], axis_bits("dom")
    side, line = dom_bits[:1], dom_bits[1:-1]
    return side + cross + line, line + side + cross


def block_places(order, rows, low):
    found = []
    for index in range(1 << len(order)):
        upper = block = 0
        for at, (axis, bit) in enumerate(order):
            value = (index >> (len(order) - 1 - at)) & 1
            if axis == "tile":
                upper |= value << (bit - 1)
            else:
                block |= value << bit
        start = low + block * rows
        found.append((upper, slice(start, start + rows), index * rows, rows))
    return found


def after(values, *others):
    return lax.optimization_barrier((values, others))[0]


def total_of(values):
    return functools.reduce(jnp.add, [v.astype(F32) for v in values])


class Exchange:
    def __init__(self, values, count, order):
        self.values = values
        self.count = count
        self.order = list(order)
        self.outgoing = None

    def rows(self, arrays, skip):
        found = [
            lax.dynamic_slice_in_dim(array, row + skip, self.count, 0)
            for array, (_, row) in zip(arrays, self.values)
        ]
        return total_of(found)

    def cut(self, *others):
        arrays = after([array for array, _ in self.values], *others)
        self.count //= 2
        axis, bit = self.order[0]
        mine = (lax.axis_index(axis) >> bit) & 1
        self.outgoing = self.rows(arrays, (1 - mine) * self.count).astype(BF16)
        self.values = [(self.rows(arrays, mine * self.count).astype(BF16), 0)]
        return self.outgoing

    def send(self):
        axis, bit = self.order.pop(0)
        self.values.append((flip(self.outgoing, axis, 1 << bit), 0))

    def total(self):
        return self.rows([array for array, _ in self.values], 0)


def cut_all(parts, *others):
    return [part.cut(*others) for part in parts]


def send_all(parts):
    for part in parts:
        part.send()


def body(
    tile_latent,
    relay_pick,
    relay_from,
    cut_pick,
    edge_latent,
    edge_sender,
    edge_receiver,
    edge_in,
    edge_out,
    node_in,
    node_out,
    node_cot,
    edge_cot,
):
    nodes, feat = tile_latent.shape
    edges = edge_latent.shape[0]
    doms, tiles = lax.axis_size("dom"), lax.axis_size("tile")
    slots = relay_pick.shape[1]
    halo = cut_pick.shape[1] // 2
    table_rows = -(-(tiles * nodes + 2 * halo) // nodes) * nodes
    half, width = 7 * feat // 2, feat // tiles
    sds = jax.ShapeDtypeStruct
    node_bf16 = sds((nodes, feat), BF16)
    node_f32 = sds((nodes, feat), F32)
    edge_bf16 = sds((edges, feat), BF16)
    edge_f32 = sds((edges, feat), F32)
    slot_bf16 = sds((slots, feat), BF16)
    halo_bf16 = sds((halo, feat), BF16)
    square = sds((feat, feat), BF16)
    node_index = sds((nodes,), jnp.int32)
    edge_index = sds((edges,), jnp.int32)

    def exchange(rows):
        blocks = rows.reshape(doms, slots // doms, feat)
        return lax.all_to_all(blocks, "dom", split_axis=0, concat_axis=0, tiled=True).reshape(
            slots, feat
        )

    tile = lax.axis_index("tile")
    turn = jnp.where(lax.axis_index("dom") % 2 == 0, halo, 0)
    where = jnp.stack([tile & 1, tile, turn]).astype(jnp.int32)
    outgoing, pick_row = call(
        pick_kernel,
        "pick",
        [Kept(slot_bf16), Kept(relay_pick)],
        [relay_pick, tile_latent],
        [relay_pick, tile_latent, 2],
        limit=SMALL_LIMIT,
    )
    edge_t = jnp.transpose(after(edge_latent, outgoing))
    came = after(exchange(outgoing), edge_t)
    latent, first, second, from_row, cut_row = call(
        pool_kernel,
        "pool",
        [Kept(node_bf16), Kept(halo_bf16), Kept(halo_bf16)]
        + [Kept(sds((1, nodes), jnp.int32)), Kept(cut_pick)],
        [relay_from, cut_pick, tile_latent, Kept(came)],
        [node_index, cut_pick, node_bf16, sds((2 * halo, feat), BF16), 3],
        [where],
        SMALL_LIMIT,
    )
    far = flip(latent, "tile", 2)
    near = flip(latent, "tile", 1)
    first = meet(first, "dom", 1)
    second = meet(second, "dom", -1)
    base, w_send, w_out = call(
        base_kernel,
        "base",
        [Kept(edge_f32), Kept(square), Kept(square)],
        [edge_receiver, edge_latent, edge_in, edge_out, Kept(latent)],
        [edge_index, edge_bf16, square, square, 6],
    )
    across = flip(after(far, first, second, base), "tile", 1)

    orders = exchange_orders()
    rows = 7 * feat // doms
    bits = len(orders[0])
    fine = rows % 16 == 0
    span = tiles * half // 2
    if fine:
        places = [block_places(order, rows, low) for order, low in zip(orders, (half, 0))]
    else:
        places = [
            [(at, slice(low, low + half), at * half, half) for at in range(tiles // 2)]
            for low in (half, 0)
        ]
    sum_rows = tiles * nodes
    (
        node_new,
        edge_new,
        pre_grad,
        agg_parts,
        local,
        keep_upper,
        keep_lower,
        send_upper,
        send_lower,
        own,
        opposite,
        back_first,
        back_second,
    ) = call(
        functools.partial(block_kernel, places),
        "block",
        [node_bf16, edge_bf16, edge_bf16, sds((2 * nodes, feat), BF16), Kept(node_f32)]
        + [sds((span, width), BF16)] * 2
        + [sds((span + 2 * sum_rows, width), BF16), sds((span, width), BF16)]
        + [Kept(sds((sum_rows, width), F32)), Kept(sds((sum_rows, width), BF16))]
        + [Kept(halo_bf16)] * 2,
        [edge_sender, edge_receiver]
        + [Kept(array) for array in (latent, near, far, across, first, second)]
        + [Kept(base), Kept(w_send), Kept(w_out)]
        + [edge_latent, edge_t, edge_in, node_in, node_out, node_cot, edge_cot],
        [edge_index, edge_index, sds((table_rows, feat), BF16), edge_bf16]
        + [sds((feat, edges), BF16), edge_bf16, square, sds((nodes, 2 * feat), BF16)]
        + [node_in, node_out, node_cot, edge_cot]
        + [node_bf16] * 4
        + [sds((2 * nodes, feat), BF16), node_f32, node_f32]
        + [edge_bf16] * 4
        + [edge_f32] * 3
        + [sds((edges, 1), F32), edge_f32, edge_f32]
        + [sds((tiles, 2 * half, width), BF16), sds((table_rows, feat), F32)]
        + [sds((2 * sum_rows, width), BF16)]
        + [9, 5 + 2 * sum(len(place) for place in places)],
        [where],
    )
    got_upper = flip(send_upper, "tile", 1)
    got_lower = flip(send_lower, "tile", 1)
    back_first = meet(back_first, "dom", 1)
    back_second = meet(back_second, "dom", -1)
    across = opposite.astype(F32) + got_upper[span + sum_rows :].astype(F32)
    across = flip(across.astype(BF16), "tile", 2)
    parts = []
    for order, keep, got in zip(
        orders, (keep_upper, keep_lower), (got_upper, got_lower), strict=True
    ):
        if fine:
            parts.append(Exchange([(keep, 0), (got, 0)], span, order))
            continue
        labels = axis_bits("tile")[:0:-1] + axis_bits("dom")[-2::-1]
        axes = [labels.index(label) for label in order] + [bits, bits + 1]
        values = [
            jnp.transpose(whole.reshape([2] * bits + [rows, width]), axes)
            for whole in (keep, got[:span])
        ]
        parts.append(Exchange([(v.reshape(span, width), 0) for v in values], span, order))
    sent = parts[0].cut()
    parts[0].send()
    sent = parts[1].cut(sent, back_first, back_second)
    parts[1].send()
    total = own + got_upper[span : span + sum_rows].astype(F32) + across.astype(F32)
    stay, slot_grad = call(
        node_kernel,
        "node",
        [Kept(node_bf16), Kept(slot_bf16)],
        [Kept(array) for array in (from_row, cut_row, w_send, after(local, sent), total)]
        + [Kept(back_first), Kept(back_second)],
        [sds((2 * halo, feat), BF16)],
        [where],
        SMALL_LIMIT,
    )
    back_rows = exchange(slot_grad)
    sent = cut_all(parts, slot_grad)
    send_all(parts)
    [latent_grad] = call(
        back_kernel,
        "back",
        [node_bf16],
        [Kept(pick_row), Kept(stay), Kept(after(back_rows, *sent))],
        [node_bf16, 1],
        limit=SMALL_LIMIT,
    )
    [edge_grad] = call(
        edge_grad_kernel,
        "edge_grad",
        [edge_bf16],
        [edge_receiver, after(pre_grad, latent_grad), edge_cot, edge_in, agg_parts],
        [edge_index, edge_bf16, edge_bf16, square, sds((2 * nodes, feat), BF16)]
        + [edge_f32, edge_bf16, 5, edges // ROWS],
        limit=2 * SMALL_LIMIT,
    )
    first = edge_grad
    while parts[0].order:
        cut_all(parts, first)
        send_all(parts)
        first = ()
    top = axis_bits("dom")[-1][1]
    upper = (lax.axis_index("dom") >> top) & 1
    above, below = [part.total() for part in parts]
    sent = jnp.where(upper == 1, below, above).astype(BF16)
    kept = jnp.where(upper == 1, above, below)
    weight_shard = kept + flip(sent, "dom", 1 << top).astype(F32)
    return (node_new, edge_new, latent_grad, edge_grad, weight_shard)


def solution(mesh):
    rows = P(("dom", "tile"), None)
    flat = P(("dom", "tile"))
    in_specs = (rows, rows, flat, rows, rows, flat, flat, P(), P(), P(), P(), rows, rows)
    out_specs = (rows, rows, rows, rows, P("dom", "tile"))
    return jax.shard_map(body, mesh=mesh, in_specs=in_specs, out_specs=out_specs, check_vma=False)
```

time: 275 us -> 86 us (0.31)
  waiting for transfers between devices: 158 us -> 30.5 us
  matrix products: 33.8 us -> 0 us
  local copies, waits for them, and re-layouts: 31.8 us -> 2.29 us
  Pallas kernels: 0 us -> 24.1 us
  between operations: 14.4 us -> 0.76 us
  blocking collectives: 7.34 us -> 0 us
  other arithmetic: 11.5 us -> 7.05 us
  starting transfers between devices: 17.6 us -> 20.8 us
    reduce_scatter x3 -> x0, waiting for transfers between devices: 153 us -> none  [the longest x1 127 us: body(): lax.psum_scatter(weight_terms, 'dom', scatter_dimension=0, tiled=True)]
    dot_general x26 -> x0, matrix products: 33.8 us -> none  [the longest x12 15.5 us: inner_dot(): lax.dot_general(left_mat, right_mat, (((0,), (0,)), ((), ())), preferred_...]
    pallas_call x0 -> x7, Pallas kernels: none -> 24.1 us  [call(): pl.pallas_call(kernel, out_shape=[array.array if isinstance(array, Kept)...]
    ppermute x4 -> x17, waiting for transfers between devices: 0.01 us -> 22.7 us  [the longest x13 19.6 us: flip(): return lax.ppermute(values, axis, [(i, i ^ mask) for i in range(count)])]
    gather x8 -> x0, local copies, waits for them, and re-layouts: 17.4 us -> none  [the longest x2 5.01 us: body(): jnp.take(agg_grad, edge_receiver, axis=0)]
    unnamed x93 -> x2, local copies, waits for them, and re-layouts: 11 us -> 0.01 us
    all_gather x1 -> x0, blocking collectives: 7.34 us -> none  [body(): part_rows = lax.all_gather(latent, 'tile', axis=0, tiled=True)]
    ppermute x4 -> x17, starting transfers between devices: 4.44 us -> 9.85 us  [the longest x13 6.01 us: flip(): return lax.ppermute(values, axis, [(i, i ^ mask) for i in range(count)])]
  transfers between devices with their start and end apart: 9 -> 19, of which waited for: 5 -> 11; matrix products, arithmetic and copies ran while one was open for 13% -> 10% of each run, Pallas kernels for 0% -> 10%
where the time goes in v1:
time: 86 us; the launch traced here: 85.4 us
  waiting for transfers between devices  30.5 us (35%)
  Pallas kernels  24.1 us (28%)
  starting transfers between devices  20.8 us (24%)
  other arithmetic  7.05 us (8%)
  local copies, waits for them, and re-layouts  2.29 us (3%)
    pallas_call x7, Pallas kernels, call(): pl.pallas_call(kernel, out_shape=[array.array if isinstance(array, Kept)...  24.1 us
    ppermute x13, waiting for transfers between devices, flip(): return lax.ppermute(values, axis, [(i, i ^ mask) for i in range(count)])  19.6 us
    all_to_all x2, starting transfers between devices, exchange(): lax.all_to_all(blocks, 'dom', split_axis=0, concat_axis=0, tiled=True)  10.9 us
    all_to_all x2, waiting for transfers between devices, exchange(): lax.all_to_all(blocks, 'dom', split_axis=0, concat_axis=0, tiled=True)  7.8 us
    ppermute x13, starting transfers between devices, flip(): return lax.ppermute(values, axis, [(i, i ^ mask) for i in range(count)])  6.01 us
    convert_element_type x3, other arithmetic, cut(): self.values = [(self.rows(arrays, mine * self.count).astype(BF16), 0)]  5.93 us
    ppermute x4, starting transfers between devices, meet(): return lax.ppermute(values, axis, pairs)  3.84 us
    ppermute x4, waiting for transfers between devices, meet(): return lax.ppermute(values, axis, pairs)  3.08 us
  transfers between devices with their start and end apart: 19, of which 11 were waited for; matrix products, arithmetic and copies ran while one was open for 10% of the time, Pallas kernels for 10%

profile of v1, /device:TPU:0, one launch (start us, length us, event | category | flops | bytes accessed | tf_op | source)
XLA Modules:
  0.0 85.4 jit_solution(18019463059033516812)
XLA Ops:
  0.6 1.8 %pick.1 = (bf16[128,512]{1,0:T(8,128)(2,1)}, s32[1,128]{1,0:T(1,128)S(1)}) custom-call(s32[1,128]{1,0:T(1,128)} %pick_hbm.1, bf16[128,512]{1,0:T(8,128)(2,1)} %tile_hbm.3), custom_call_target="tpu_custom_call" | custom-call | tf_op jit(solution)/shard_map/pick/pallas_call | solution.py:97
  2.5 7.3 %all-to-all-start = ((bf16[8,16,512]{2,1,0:T(8,128)(2,1)}), bf16[8,16,512]{2,1,0:T(8,128)(2,1)S(1)}, u32[]{:S(2)}, u32[]{:S(2)}) async-start(bf16[8,16,512]{2,1,0:T(8,128)(2,1)} %bitcast.3), calls=%async_computation | async-start | bytes 262144 | tf_op jit(solution)/shard_map/all_to_all | solution.py:639
  9.8 2.3 %copy.18 = bf16[768,512]{0,1:T(8,128)(2,1)} copy(bf16[768,512]{1,0:T(8,128)(2,1)} %edge_hbm.3) | data formatting | bytes 1572864 | tf_op jit(solution)/shard_map/optimization_barrier | solution.py:557
  12.0 0.1 pad_add_fusion.where_ref
  12.1 5.0 %all-to-all-done = bf16[8,16,512]{2,1,0:T(8,128)(2,1)S(1)} async-done(((bf16[8,16,512]{2,1,0:T(8,128)(2,1)}), bf16[8,16,512]{2,1,0:T(8,128)(2,1)S(1)}, u32[]{:S(2)}, u32[]{:S(2)}) %all-to-all-start) | async-done | bytes 131104 | tf_op jit(solution)/shard_map/all_to_all | solution.py:639
  17.1 1.9 %pool.1 = (bf16[128,512]{1,0:T(8,128)(2,1)S(1)}, bf16[16,512]{1,0:T(8,128)(2,1)S(1)}, bf16[16,512]{1,0:T(8,128)(2,1)S(1)}, s32[1,128]{1,0:T(1,128)S(1)}, s32[1,32]{1,0:T(1,128)S(1)}) custom-call(s32[3]{0:T(128)S(1)} %pad_add_fusion.where_ref, s32[128]{0:T(128)} %from_hbm.1, s32[1,32]{1,0:T(1,128)} %cut_hbm.1, bf16[128,512]{1,0:T(8,128)(2,1)} %tile_hbm.3, ...), custom_call_target="tpu_custom_call" | custom-call | tf_op jit(solution)/shard_map/pool/pallas_call | solution.py:97
  19.0 1.6 %collective-permute-start.1 = (bf16[128,512]{1,0:T(8,128)(2,1)S(1)}, bf16[128,512]{1,0:T(8,128)(2,1)S(1)}, u32[]{:S(2)}, u32[]{:S(2)}) collective-permute-start(bf16[128,512]{1,0:T(8,128)(2,1)S(1)} %get-tuple-element.51.latent_ref), channel_id=1, source_target_pairs={{0,2},{1,3},{2,0},{3,1},{4,6},{5,7},{6,4},{7,5},{8,10},{9,11},{10,... | collective-permute-start | bytes 393224 | tf_op jit(solution)/shard_map/ppermute | solution.py:522
  20.6 0.2 collective-permute-start.2
  20.8 1.8 %collective-permute-start.3 = (bf16[16,512]{1,0:T(8,128)(2,1)S(1)}, bf16[16,512]{1,0:T(8,128)(2,1)S(1)}, u32[]{:S(2)}, u32[]{:S(2)}) collective-permute-start(bf16[16,512]{1,0:T(8,128)(2,1)S(1)} %get-tuple-element.53), channel_id=1, source_target_pairs={{0,28},{4,8},{8,4},{12,16},{16,12},{20,24},{24,20},{28,0},{1,29},{... | collective-permute-start | bytes 49160 | tf_op jit(solution)/shard_map/ppermute | solution.py:528
  22.6 0.0 collective-permute-start
  22.6 3.0 %base.1 = (f32[768,512]{1,0:T(8,128)S(1)}, bf16[512,512]{1,0:T(8,128)(2,1)S(1)}, bf16[512,512]{1,0:T(8,128)(2,1)S(1)}) custom-call(s32[768]{0:T(1024)} %receiver_hbm.5, bf16[768,512]{1,0:T(8,128)(2,1)} %edge_hbm.3, bf16[1536,512]{1,0:T(8,128)(2,1)} %w_hbm.1, bf16[512,512]{1,0:T(8,128)(2,1)} %edge_out_hbm.1, bf16[128,512]{1,0:T(8,128)(2,1)S(1)} %get-tuple-element.51.latent_ref), custom_call_target="tpu_custom_call" | custom-call | tf_op jit(solution)/shard_map/base/pallas_call | solution.py:97
  25.6 0.0 collective-permute-done.2.first_ref
  25.6 1.6 %collective-permute-done.3.second_ref = bf16[16,512]{1,0:T(8,128)(2,1)S(1)} collective-permute-done((bf16[16,512]{1,0:T(8,128)(2,1)S(1)}, bf16[16,512]{1,0:T(8,128)(2,1)S(1)}, u32[]{:S(2)}, u32[]{:S(2)}) %collective-permute-start.3) | collective-permute-done | bytes 16416 | tf_op jit(solution)/shard_map/ppermute | solution.py:528
  27.2 0.0 collective-permute-done.1.far_ref
  27.2 0.0 collective-permute-done.near_ref
  27.2 1.3 %collective-permute-done.4.cross_ref = bf16[128,512]{1,0:T(8,128)(2,1)S(1)} collective-permute-done((bf16[128,512]{1,0:T(8,128)(2,1)S(1)}, bf16[128,512]{1,0:T(8,128)(2,1)S(1)}, u32[]{:S(2)}, u32[]{:S(2)}) %collective-permute-start.4) | collective-permute-done | bytes 131104 | tf_op jit(solution)/shard_map/ppermute | solution.py:522
  28.6 11.5 %block.1 = (bf16[128,512]{1,0:T(8,128)(2,1)}, bf16[768,512]{1,0:T(8,128)(2,1)}, bf16[768,512]{1,0:T(8,128)(2,1)}, bf16[256,512]{1,0:T(8,128)(2,1)}, f32[128,512]...) custom-call(s32[3]{0:T(128)S(1)} %pad_add_fusion.where_ref, ...), custom_call_target="tpu_custom_call" | custom-call | tf_op jit(solution)/shard_map/block/pallas_call | solution.py:97
  40.0 0.2 collective-permute-start.6
  40.2 0.4 collective-permute-start.5
  40.6 0.0 collective-permute-start.7
  40.6 1.8 %collective-permute-start.8 = (bf16[16,512]{1,0:T(8,128)(2,1)S(1)}, bf16[16,512]{1,0:T(8,128)(2,1)S(1)}, u32[]{:S(2)}, u32[]{:S(2)}) collective-permute-start(bf16[16,512]{1,0:T(8,128)(2,1)S(1)} %get-tuple-element.71), channel_id=1, source_target_pairs={{0,28},{4,8},{8,4},{12,16},{16,12},{20,24},{24,20},{28,0},{1,29},{... | collective-permute-start | bytes 49160 | tf_op jit(solution)/shard_map/ppermute | solution.py:528
  42.4 0.9 %collective-permute-done.6 = bf16[4608,128]{1,0:T(8,128)(2,1)S(1)} collective-permute-done((bf16[4608,128]{1,0:T(8,128)(2,1)}, bf16[4608,128]{1,0:T(8,128)(2,1)S(1)}, u32[]{:S(2)}, u32[]{:S(2)}) %collective-permute-start.6) | collective-permute-done | bytes 1179680 | tf_op jit(solution)/shard_map/ppermute | solution.py:522
  43.4 2.2 %add_convert_fusion.1 = (bf16[1792,128]{1,0:T(8,128)(2,1)S(1)}, bf16[1792,128]{1,0:T(8,128)(2,1)}) fusion(bf16[4608,128]{1,0:T(8,128)(2,1)S(1)} %collective-permute-done.6, s32[]{:T(128)S(6)} %select_n.81, bf16[3584,128]{1,0:T(8,128)(2,1)} %get-tuple-element.68, s32[]{:T(128)S(6)} %select_n.80, s32[]{:T(128)S(6)} %select_n.78, s32[]{:T(128)S(6)} %select_n.77), kind=kLoop, calls=%fused_computation.1 | loop fusion | flops 1835008 | bytes 2752528 | tf_op jit(solution)/shard_map/convert_element_type | solution.py:584
  45.6 0.0 collective-permute-start.10
  45.6 0.0 collective-permute-done.7.first_ref
  45.6 1.4 %collective-permute-done.8.second_ref = bf16[16,512]{1,0:T(8,128)(2,1)S(1)} collective-permute-done((bf16[16,512]{1,0:T(8,128)(2,1)S(1)}, bf16[16,512]{1,0:T(8,128)(2,1)S(1)}, u32[]{:S(2)}, u32[]{:S(2)}) %collective-permute-start.8) | collective-permute-done | bytes 16416 | tf_op jit(solution)/shard_map/ppermute | solution.py:528
  47.1 0.0 collective-permute-done.5
  47.1 2.2 %add_convert_fusion = (bf16[1792,128]{1,0:T(8,128)(2,1)S(1)}, bf16[1792,128]{1,0:T(8,128)(2,1)}) fusion(bf16[3584,128]{1,0:T(8,128)(2,1)} %collective-permute-done.5, s32[]{:T(128)S(6)} %select_n.83, bf16[3584,128]{1,0:T(8,128)(2,1)S(1)} %copy-done, s32[]{:T(128)S(6)} %select_n.79), kind=kLoop, calls=%fused_computation | loop fusion | flops 1835008 | bytes 2752520 | tf_op jit(solution)/shard_map/convert_element_type | solution.py:584
  49.3 0.6 collective-permute-start.9
  49.9 4.4 %collective-permute-done.9 = bf16[512,128]{1,0:T(8,128)(2,1)S(1)} collective-permute-done((bf16[512,128]{1,0:T(8,128)(2,1)S(1)}, bf16[512,128]{1,0:T(8,128)(2,1)S(1)}, u32[]{:S(2)}, u32[]{:S(2)}) %collective-permute-start.9) | collective-permute-done | bytes 131104 | tf_op jit(solution)/shard_map/ppermute | solution.py:522
  54.3 1.9 %node.1 = (bf16[128,512]{1,0:T(8,128)(2,1)S(1)}, bf16[128,512]{1,0:T(8,128)(2,1)}) custom-call(s32[3]{0:T(128)S(1)} %pad_add_fusion.where_ref, s32[1,128]{1,0:T(1,128)S(1)} %get-tuple-element.61.from_ref, s32[1,32]{1,0:T(1,128)S(1)} %get-tuple-element.62.cut_ref, bf16[512,512]{1,0:T(8,128)(2,1)S(1)} %get-tuple-element.56.w_send.w_send_ref, ...), custom_call_target="tpu_custom_call" | custom-call | tf_op jit(solution)/shard_map/node/pallas_call | solution.py:97
  56.3 3.6 %all-to-all-start.1 = ((bf16[8,16,512]{2,1,0:T(8,128)(2,1)}), bf16[8,16,512]{2,1,0:T(8,128)(2,1)S(1)}, u32[]{:S(2)}, u32[]{:S(2)}) async-start(bf16[8,16,512]{2,1,0:T(8,128)(2,1)} %bitcast.6), calls=%async_computation.1 | async-start | bytes 262144 | tf_op jit(solution)/shard_map/all_to_all | solution.py:639
  59.9 1.0 %collective-permute-done.11 = bf16[1792,128]{1,0:T(8,128)(2,1)} collective-permute-done((bf16[1792,128]{1,0:T(8,128)(2,1)}, bf16[1792,128]{1,0:T(8,128)(2,1)}, u32[]{:S(2)}, u32[]{:S(2)}) %collective-permute-start.11) | collective-permute-done | bytes 458784 | tf_op jit(solution)/shard_map/ppermute | solution.py:522
  61.0 1.5 %add_convert_fusion.4 = (bf16[896,128]{1,0:T(8,128)(2,1)S(1)}, bf16[896,128]{1,0:T(8,128)(2,1)S(1)}, bf16[896,128]{1,0:T(8,128)(2,1)S(1)}, bf16[896,128]{1,0:T(8,128)(2,1)S(1)}) fusion(bf16[1792,128]{1,0:T(8,128)(2,1)} %collective-permute-done.11, s32[]{:T(128)S(6)} %select_n.89, bf16[1792,128]{1,0:T(8,128)(2,1)S(1)} %get-tuple-element.81, s32[]{:T(128)S(6)} %select_n.84, ...), kind=kLoop, calls=%fused_computation.4 | loop fusion | flops 1835008 | bytes 2752528 | tf_op jit(solution)/shard_map/convert_element_type | solution.py:584
  62.5 1.5 %collective-permute-start.14 = (bf16[896,128]{1,0:T(8,128)(2,1)S(1)}, bf16[896,128]{1,0:T(8,128)(2,1)S(1)}, u32[]{:S(2)}, u32[]{:S(2)}) collective-permute-start(bf16[896,128]{1,0:T(8,128)(2,1)S(1)} %get-tuple-element.96), channel_id=1, source_target_pairs={{0,4},{4,0},{8,12},{12,8},{16,20},{20,16},{24,28},{28,24},{1,5},{5... | collective-permute-start | bytes 688136 | tf_op jit(solution)/shard_map/ppermute | solution.py:522
  64.0 0.5 collective-permute-start.12
  64.5 2.8 %all-to-all-done.1 = bf16[8,16,512]{2,1,0:T(8,128)(2,1)S(1)} async-done(((bf16[8,16,512]{2,1,0:T(8,128)(2,1)}), bf16[8,16,512]{2,1,0:T(8,128)(2,1)S(1)}, u32[]{:S(2)}, u32[]{:S(2)}) %all-to-all-start.1) | async-done | bytes 131104 | tf_op jit(solution)/shard_map/all_to_all | solution.py:639
  67.4 0.8 back.1
  68.2 3.2 %edge_grad.1 = bf16[768,512]{1,0:T(8,128)(2,1)} custom-call(s32[768]{0:T(1024)} %receiver_hbm.5, bf16[768,512]{1,0:T(8,128)(2,1)} %get-tuple-element.85.pre_grad_hbm, bf16[768,512]{1,0:T(8,128)(2,1)} %edge_cot_hbm.3, bf16[1536,512]{1,0:T(8,128)(2,1)} %w_hbm.1, bf16[256,512]{1,0:T(8,128)(2,1)} %get-tuple-element.86.agg_parts_hbm), custom_call_target="tpu_custom_call" | custom-call | tf_op jit(solution)/shard_map/edge_grad/pallas_call | solution.py:97
  71.4 0.0 collective-permute-done.14
  71.5 0.6 collective-permute-start.15
  72.1 0.1 collective-permute-start.13
  72.2 4.1 %collective-permute-done.15 = bf16[448,128]{1,0:T(8,128)(2,1)S(1)} collective-permute-done((bf16[448,128]{1,0:T(8,128)(2,1)S(1)}, bf16[448,128]{1,0:T(8,128)(2,1)S(1)}, u32[]{:S(2)}, u32[]{:S(2)}) %collective-permute-start.15) | collective-permute-done | bytes 114720 | tf_op jit(solution)/shard_map/ppermute | solution.py:522
  76.3 1.2 %collective-permute-done.13 = bf16[448,128]{1,0:T(8,128)(2,1)S(1)} collective-permute-done((bf16[448,128]{1,0:T(8,128)(2,1)S(1)}, bf16[448,128]{1,0:T(8,128)(2,1)S(1)}, u32[]{:S(2)}, u32[]{:S(2)}) %collective-permute-start.13) | collective-permute-done | bytes 114720 | tf_op jit(solution)/shard_map/ppermute | solution.py:522
  77.6 0.1 select_convert_fusion
  77.7 0.5 collective-permute-start.16
  78.2 6.5 %collective-permute-done.16 = bf16[448,128]{1,0:T(8,128)(2,1)S(1)} collective-permute-done((bf16[448,128]{1,0:T(8,128)(2,1)S(1)}, bf16[448,128]{1,0:T(8,128)(2,1)S(1)}, u32[]{:S(2)}, u32[]{:S(2)}) %collective-permute-start.16) | collective-permute-done | bytes 114720 | tf_op jit(solution)/shard_map/ppermute | solution.py:522
  84.6 0.8 convert_add_fusion.1
  (10 shorter events, 0.2 us)
Async XLA Ops:
  2.5 14.6 %all-to-all-start = ((bf16[8,16,512]{2,1,0:T(8,128)(2,1)}), bf16[8,16,512]{2,1,0:T(8,128)(2,1)S(1)}, u32[]{:S(2)}, u32[]{:S(2)}) async-start(bf16[8,16,512]{2,1,0:T(8,128)(2,1)} %bitcast.3), calls=%async_computation | async-start | bytes 262144 | tf_op jit(solution)/shard_map/all_to_all | solution.py:639
  19.0 8.2 %collective-permute-start.1 = (bf16[128,512]{1,0:T(8,128)(2,1)S(1)}, bf16[128,512]{1,0:T(8,128)(2,1)S(1)}, u32[]{:S(2)}, u32[]{:S(2)}) collective-permute-start(bf16[128,512]{1,0:T(8,128)(2,1)S(1)} %get-tuple-element.51.latent_ref), channel_id=1, source_target_pairs={{0,2},{1,3},{2,0},{3,1},{4,6},{5,7},{6,4},{7,5},{8,10},{9,11},{10,... | collective-permute-start | bytes 393224 | tf_op jit(solution)/shard_map/ppermute | solution.py:522
  20.6 5.0 %collective-permute-start.2 = (bf16[16,512]{1,0:T(8,128)(2,1)S(1)}, bf16[16,512]{1,0:T(8,128)(2,1)S(1)}, u32[]{:S(2)}, u32[]{:S(2)}) collective-permute-start(bf16[16,512]{1,0:T(8,128)(2,1)S(1)} %get-tuple-element.52), channel_id=1, source_target_pairs={{0,4},{4,0},{8,12},{12,8},{16,20},{20,16},{24,28},{28,24},{1,5},{5... | collective-permute-start | bytes 49160 | tf_op jit(solution)/shard_map/ppermute | solution.py:528
  20.8 6.4 %collective-permute-start.3 = (bf16[16,512]{1,0:T(8,128)(2,1)S(1)}, bf16[16,512]{1,0:T(8,128)(2,1)S(1)}, u32[]{:S(2)}, u32[]{:S(2)}) collective-permute-start(bf16[16,512]{1,0:T(8,128)(2,1)S(1)} %get-tuple-element.53), channel_id=1, source_target_pairs={{0,28},{4,8},{8,4},{12,16},{16,12},{20,24},{24,20},{28,0},{1,29},{... | collective-permute-start | bytes 49160 | tf_op jit(solution)/shard_map/ppermute | solution.py:528
  22.6 4.6 %collective-permute-start = (bf16[128,512]{1,0:T(8,128)(2,1)S(1)}, bf16[128,512]{1,0:T(8,128)(2,1)S(1)}, u32[]{:S(2)}, u32[]{:S(2)}) collective-permute-start(bf16[128,512]{1,0:T(8,128)(2,1)S(1)} %get-tuple-element.51.latent_ref), channel_id=1, source_target_pairs={{0,1},{1,0},{2,3},{3,2},{4,5},{5,4},{6,7},{7,6},{8,9},{9,8},{10,11... | collective-permute-start | bytes 393224 | tf_op jit(solution)/shard_map/ppermute | solution.py:522
  27.2 1.3 %collective-permute-start.4 = (bf16[128,512]{1,0:T(8,128)(2,1)S(1)}, bf16[128,512]{1,0:T(8,128)(2,1)S(1)}, u32[]{:S(2)}, u32[]{:S(2)}) collective-permute-start(bf16[128,512]{1,0:T(8,128)(2,1)S(1)} %collective-permute-done.1.far_ref), channel_id=1, source_target_pairs={{0,1},{1,0},{2,3},{3,2},{4,5},{5,4},{6,7},{7,6},{8,9},{9,8},{10,11... | collective-permute-start | bytes 393224 | tf_op jit(solution)/shard_map/ppermute | solution.py:522
  40.0 3.3 %collective-permute-start.6 = (bf16[4608,128]{1,0:T(8,128)(2,1)}, bf16[4608,128]{1,0:T(8,128)(2,1)S(1)}, u32[]{:S(2)}, u32[]{:S(2)}) collective-permute-start(bf16[4608,128]{1,0:T(8,128)(2,1)} %get-tuple-element.67), channel_id=1, source_target_pairs={{0,1},{1,0},{2,3},{3,2},{4,5},{5,4},{6,7},{7,6},{8,9},{9,8},{10,11... | collective-permute-start | bytes 3538952 | tf_op jit(solution)/shard_map/ppermute | solution.py:522
  40.2 6.8 %collective-permute-start.5 = (bf16[3584,128]{1,0:T(8,128)(2,1)}, bf16[3584,128]{1,0:T(8,128)(2,1)}, u32[]{:S(2)}, u32[]{:S(2)}) collective-permute-start(bf16[3584,128]{1,0:T(8,128)(2,1)} %get-tuple-element.65), channel_id=1, source_target_pairs={{0,1},{1,0},{2,3},{3,2},{4,5},{5,4},{6,7},{7,6},{8,9},{9,8},{10,11... | collective-permute-start | bytes 2752520 | tf_op jit(solution)/shard_map/ppermute | solution.py:522
  40.6 5.0 %collective-permute-start.7 = (bf16[16,512]{1,0:T(8,128)(2,1)S(1)}, bf16[16,512]{1,0:T(8,128)(2,1)S(1)}, u32[]{:S(2)}, u32[]{:S(2)}) collective-permute-start(bf16[16,512]{1,0:T(8,128)(2,1)S(1)} %get-tuple-element.70), channel_id=1, source_target_pairs={{0,4},{4,0},{8,12},{12,8},{16,20},{20,16},{24,28},{28,24},{1,5},{5... | collective-permute-start | bytes 49160 | tf_op jit(solution)/shard_map/ppermute | solution.py:528
  40.6 6.4 %collective-permute-start.8 = (bf16[16,512]{1,0:T(8,128)(2,1)S(1)}, bf16[16,512]{1,0:T(8,128)(2,1)S(1)}, u32[]{:S(2)}, u32[]{:S(2)}) collective-permute-start(bf16[16,512]{1,0:T(8,128)(2,1)S(1)} %get-tuple-element.71), channel_id=1, source_target_pairs={{0,28},{4,8},{8,4},{12,16},{16,12},{20,24},{24,20},{28,0},{1,29},{... | collective-permute-start | bytes 49160 | tf_op jit(solution)/shard_map/ppermute | solution.py:528
  43.4 3.7 %copy-start = (bf16[3584,128]{1,0:T(8,128)(2,1)S(1)}, bf16[3584,128]{1,0:T(8,128)(2,1)}, u32[]{:S(2)}) copy-start(bf16[3584,128]{1,0:T(8,128)(2,1)} %get-tuple-element.72) | copy-start | bytes 2752516
  45.6 14.3 %collective-permute-start.10 = (bf16[1792,128]{1,0:T(8,128)(2,1)}, bf16[1792,128]{1,0:T(8,128)(2,1)}, u32[]{:S(2)}, u32[]{:S(2)}) collective-permute-start(bf16[1792,128]{1,0:T(8,128)(2,1)} %get-tuple-element.92), channel_id=1, source_target_pairs={{0,4},{4,0},{8,12},{12,8},{16,20},{20,16},{24,28},{28,24},{1,5},{5... | collective-permute-start | bytes 1376264 | tf_op jit(solution)/shard_map/ppermute | solution.py:522
  49.2 11.7 %collective-permute-start.11 = (bf16[1792,128]{1,0:T(8,128)(2,1)}, bf16[1792,128]{1,0:T(8,128)(2,1)}, u32[]{:S(2)}, u32[]{:S(2)}) collective-permute-start(bf16[1792,128]{1,0:T(8,128)(2,1)} %get-tuple-element.94), channel_id=1, source_target_pairs={{0,8},{4,12},{8,0},{12,4},{16,24},{20,28},{24,16},{28,20},{1,9},{5... | collective-permute-start | bytes 1376264 | tf_op jit(solution)/shard_map/ppermute | solution.py:522
  49.3 5.0 %collective-permute-start.9 = (bf16[512,128]{1,0:T(8,128)(2,1)S(1)}, bf16[512,128]{1,0:T(8,128)(2,1)S(1)}, u32[]{:S(2)}, u32[]{:S(2)}) collective-permute-start(bf16[512,128]{1,0:T(8,128)(2,1)S(1)} %add_convert_fusion.8), channel_id=1, source_target_pairs={{0,2},{1,3},{2,0},{3,1},{4,6},{5,7},{6,4},{7,5},{8,10},{9,11},{10,... | collective-permute-start | bytes 393224 | tf_op jit(solution)/shard_map/ppermute | solution.py:522
  56.3 11.1 %all-to-all-start.1 = ((bf16[8,16,512]{2,1,0:T(8,128)(2,1)}), bf16[8,16,512]{2,1,0:T(8,128)(2,1)S(1)}, u32[]{:S(2)}, u32[]{:S(2)}) async-start(bf16[8,16,512]{2,1,0:T(8,128)(2,1)} %bitcast.6), calls=%async_computation.1 | async-start | bytes 262144 | tf_op jit(solution)/shard_map/all_to_all | solution.py:639
  62.5 8.9 %collective-permute-start.14 = (bf16[896,128]{1,0:T(8,128)(2,1)S(1)}, bf16[896,128]{1,0:T(8,128)(2,1)S(1)}, u32[]{:S(2)}, u32[]{:S(2)}) collective-permute-start(bf16[896,128]{1,0:T(8,128)(2,1)S(1)} %get-tuple-element.96), channel_id=1, source_target_pairs={{0,4},{4,0},{8,12},{12,8},{16,20},{20,16},{24,28},{28,24},{1,5},{5... | collective-permute-start | bytes 688136 | tf_op jit(solution)/shard_map/ppermute | solution.py:522
  64.0 8.1 %collective-permute-start.12 = (bf16[896,128]{1,0:T(8,128)(2,1)S(1)}, bf16[896,128]{1,0:T(8,128)(2,1)S(1)}, u32[]{:S(2)}, u32[]{:S(2)}) collective-permute-start(bf16[896,128]{1,0:T(8,128)(2,1)S(1)} %get-tuple-element.99), channel_id=1, source_target_pairs={{0,2},{1,3},{2,0},{3,1},{4,6},{5,7},{6,4},{7,5},{8,10},{9,11},{10,... | collective-permute-start | bytes 688136 | tf_op jit(solution)/shard_map/ppermute | solution.py:522
  71.5 4.9 %collective-permute-start.15 = (bf16[448,128]{1,0:T(8,128)(2,1)S(1)}, bf16[448,128]{1,0:T(8,128)(2,1)S(1)}, u32[]{:S(2)}, u32[]{:S(2)}) collective-permute-start(bf16[448,128]{1,0:T(8,128)(2,1)S(1)} %add_convert_fusion.9), channel_id=1, source_target_pairs={{0,2},{1,3},{2,0},{3,1},{4,6},{5,7},{6,4},{7,5},{8,10},{9,11},{10,... | collective-permute-start | bytes 344072 | tf_op jit(solution)/shard_map/ppermute | solution.py:522
  72.1 5.5 %collective-permute-start.13 = (bf16[448,128]{1,0:T(8,128)(2,1)S(1)}, bf16[448,128]{1,0:T(8,128)(2,1)S(1)}, u32[]{:S(2)}, u32[]{:S(2)}) collective-permute-start(bf16[448,128]{1,0:T(8,128)(2,1)S(1)} %add_convert_fusion.11), channel_id=1, source_target_pairs={{0,8},{4,12},{8,0},{12,4},{16,24},{20,28},{24,16},{28,20},{1,9},{5... | collective-permute-start | bytes 344072 | tf_op jit(solution)/shard_map/ppermute | solution.py:522
  77.7 7.0 %collective-permute-start.16 = (bf16[448,128]{1,0:T(8,128)(2,1)S(1)}, bf16[448,128]{1,0:T(8,128)(2,1)S(1)}, u32[]{:S(2)}, u32[]{:S(2)}) collective-permute-start(bf16[448,128]{1,0:T(8,128)(2,1)S(1)} %select_convert_fusion), channel_id=1, source_target_pairs={{0,16},{4,20},{8,24},{12,28},{16,0},{20,4},{24,8},{28,12},{1,17},{... | collective-permute-start | bytes 344072 | tf_op jit(solution)/shard_map/ppermute | solution.py:522

commit v2 on v1

--- a/solution.py
+++ b/solution.py
@@ -394,10 +394,30 @@
     taken = flat_dot(receiver_rows, pre_grad[...])
 
     def give(which, keep_ref, send_ref):
-        for source, rows, first, count in places[which]:
-            to = pl.ds(first, count)
-            stores.start(weights.at[2 * source + core, rows], keep_ref.at[to])
-            stores.start(weights.at[2 * source + 1 - core, rows], send_ref.at[to])
+        order, low = places[which]
+        half = keep_ref.shape[0] // (tiles // 2)
+        if order is None:
+            for upper in range(tiles // 2):
+                to = pl.ds(upper * half, half)
+                rows = slice(low, low + half)
+                stores.start(weights.at[2 * upper + core, rows], keep_ref.at[to])
+                stores.start(weights.at[2 * upper + 1 - core, rows], send_ref.at[to])
+            return
+        here = {"tile": tile, "dom": where_ref[3]}
+        rows = keep_ref.shape[0] >> len(order)
+        for index in range(1 << len(order)):
+            upper = block = 0
+            for at, (axis, bit) in enumerate(order):
+                flipped = 1 - ((index >> (len(order) - 1 - at)) & 1)
+                value = ((here[axis] >> bit) & 1) ^ flipped
+                if axis == "tile":
+                    upper = upper + (value << (bit - 1))
+                else:
+                    block = block + (value << bit)
+            source = pl.ds(pl.multiple_of(low + block * rows, 16), rows)
+            to = pl.ds(index * rows, rows)
+            stores.start(weights.at[2 * upper + core, source], keep_ref.at[to])
+            stores.start(weights.at[2 * upper + 1 - core, source], send_ref.at[to])
 
     part_rows = sums.shape[0] // 2
     for start in (0, part_rows):
@@ -538,21 +558,6 @@
     return side + cross + line, line + side + cross
 
 
-def block_places(order, rows, low):
-    found = []
-    for index in range(1 << len(order)):
-        upper = block = 0
-        for at, (axis, bit) in enumerate(order):
-            value = (index >> (len(order) - 1 - at)) & 1
-            if axis == "tile":
-                upper |= value << (bit - 1)
-            else:
-                block |= value << bit
-        start = low + block * rows
-        found.append((upper, slice(start, start + rows), index * rows, rows))
-    return found
-
-
 def after(values, *others):
     return lax.optimization_barrier((values, others))[0]
 
@@ -562,34 +567,38 @@
 
 
 class Exchange:
-    def __init__(self, values, count, order):
+    def __init__(self, values, count, order, relative):
         self.values = values
         self.count = count
         self.order = list(order)
+        self.relative = relative
         self.outgoing = None
 
-    def rows(self, arrays, skip):
-        found = [
-            lax.dynamic_slice_in_dim(array, row + skip, self.count, 0)
-            for array, (_, row) in zip(arrays, self.values)
-        ]
-        return total_of(found)
-
     def cut(self, *others):
-        arrays = after([array for array, _ in self.values], *others)
+        arrays = after(self.values, *others)
         self.count //= 2
         axis, bit = self.order[0]
         mine = (lax.axis_index(axis) >> bit) & 1
-        self.outgoing = self.rows(arrays, (1 - mine) * self.count).astype(BF16)
-        self.values = [(self.rows(arrays, mine * self.count).astype(BF16), 0)]
+
+        def half(second):
+            if self.relative:
+                first = int(second) * self.count
+                return total_of([a[first : first + self.count] for a in arrays]).astype(BF16)
+            first = (mine if second else 1 - mine) * self.count
+            return total_of(
+                [lax.dynamic_slice_in_dim(a, first, self.count, 0) for a in arrays]
+            ).astype(BF16)
+
+        self.outgoing = half(False)
+        self.values = [half(True)]
         return self.outgoing
 
     def send(self):
         axis, bit = self.order.pop(0)
-        self.values.append((flip(self.outgoing, axis, 1 << bit), 0))
+        self.values.append(flip(self.outgoing, axis, 1 << bit))
 
     def total(self):
-        return self.rows([array for array, _ in self.values], 0)
+        return total_of(self.values)
 
 
 def cut_all(parts, *others):
@@ -642,7 +651,7 @@
 
     tile = lax.axis_index("tile")
     turn = jnp.where(lax.axis_index("dom") % 2 == 0, halo, 0)
-    where = jnp.stack([tile & 1, tile, turn]).astype(jnp.int32)
+    where = jnp.stack([tile & 1, tile, turn, lax.axis_index("dom")]).astype(jnp.int32)
     outgoing, pick_row = call(
         pick_kernel,
         "pick",
@@ -681,13 +690,8 @@
     bits = len(orders[0])
     fine = rows % 16 == 0
     span = tiles * half // 2
-    if fine:
-        places = [block_places(order, rows, low) for order, low in zip(orders, (half, 0))]
-    else:
-        places = [
-            [(at, slice(low, low + half), at * half, half) for at in range(tiles // 2)]
-            for low in (half, 0)
-        ]
+    places = [(order if fine else None, low) for order, low in zip(orders, (half, 0))]
+    copies = 2 * sum(1 << len(order) if fine else tiles // 2 for order in orders)
     sum_rows = tiles * nodes
     (
         node_new,
@@ -725,21 +729,21 @@
         + [sds((edges, 1), F32), edge_f32, edge_f32]
         + [sds((tiles, 2 * half, width), BF16), sds((table_rows, feat), F32)]
         + [sds((2 * sum_rows, width), BF16)]
-        + [9, 5 + 2 * sum(len(place) for place in places)],
+        + [9, 5 + copies],
         [where],
     )
     got_upper = flip(send_upper, "tile", 1)
     got_lower = flip(send_lower, "tile", 1)
     back_first = meet(back_first, "dom", 1)
     back_second = meet(back_second, "dom", -1)
-    across = opposite.astype(F32) + got_upper[span + sum_rows :].astype(F32)
-    across = flip(across.astype(BF16), "tile", 2)
+    leaving = (opposite.astype(F32) + got_upper[span + sum_rows :].astype(F32)).astype(BF16)
+    across = flip(leaving, "tile", 2)
     parts = []
     for order, keep, got in zip(
         orders, (keep_upper, keep_lower), (got_upper, got_lower), strict=True
     ):
         if fine:
-            parts.append(Exchange([(keep, 0), (got, 0)], span, order))
+            parts.append(Exchange([keep, got], span, order, True))
             continue
         labels = axis_bits("tile")[:0:-1] + axis_bits("dom")[-2::-1]
         axes = [labels.index(label) for label in order] + [bits, bits + 1]
@@ -747,10 +751,10 @@
             jnp.transpose(whole.reshape([2] * bits + [rows, width]), axes)
             for whole in (keep, got[:span])
         ]
-        parts.append(Exchange([(v.reshape(span, width), 0) for v in values], span, order))
-    sent = parts[0].cut()
+        parts.append(Exchange([v.reshape(span, width) for v in values], span, order, False))
+    sent = parts[0].cut(leaving)
     parts[0].send()
-    sent = parts[1].cut(sent, back_first, back_second)
+    sent = parts[1].cut(sent, back_first, back_second, across)
     parts[1].send()
     total = own + got_upper[span : span + sum_rows].astype(F32) + across.astype(F32)
     stay, slot_grad = call(

time: 86 us -> 83.8 us (0.974)
  other arithmetic: 7.05 us -> 3.06 us
  waiting for transfers between devices: 30.5 us -> 33.7 us
  starting transfers between devices: 20.8 us -> 19.2 us
    ppermute x13, waiting for transfers between devices: 19.6 us -> 25.4 us  [flip(): return lax.ppermute(values, axis, [(i, i ^ mask) for i in range(count)])]
    convert_element_type x6, other arithmetic: 6.05 us -> 2.06 us  [the longest x5 2.03 us: half(): return total_of([a[first:first + self.count] for a in arrays]).astype(BF16)]
    all_to_all x2, waiting for transfers between devices: 7.8 us -> 4.98 us  [exchange(): lax.all_to_all(blocks, 'dom', split_axis=0, concat_axis=0, tiled=True)]
    ppermute x13, starting transfers between devices: 6.01 us -> 4.67 us  [flip(): return lax.ppermute(values, axis, [(i, i ^ mask) for i in range(count)])]
  transfers between devices with their start and end apart: 19 -> 19, of which waited for: 11 -> 13; matrix products, arithmetic and copies ran while one was open for 10% -> 5% of each run, Pallas kernels for 10% -> 11%
where the time goes in v2:
time: 83.8 us; the launch traced here: 83.3 us
  waiting for transfers between devices  33.7 us (40%)
  Pallas kernels  24.2 us (29%)
  starting transfers between devices  19.2 us (23%)
  other arithmetic  3.06 us (4%)
  local copies, waits for them, and re-layouts  2.29 us (3%)
    ppermute x13, waiting for transfers between devices, flip(): return lax.ppermute(values, axis, [(i, i ^ mask) for i in range(count)])  25.4 us
    pallas_call x7, Pallas kernels, call(): pl.pallas_call(kernel, out_shape=[array.array if isinstance(array, Kept)...  24.2 us
    all_to_all x2, starting transfers between devices, exchange(): lax.all_to_all(blocks, 'dom', split_axis=0, concat_axis=0, tiled=True)  10.7 us
    all_to_all x2, waiting for transfers between devices, exchange(): lax.all_to_all(blocks, 'dom', split_axis=0, concat_axis=0, tiled=True)  4.98 us
    ppermute x13, starting transfers between devices, flip(): return lax.ppermute(values, axis, [(i, i ^ mask) for i in range(count)])  4.67 us
    ppermute x4, starting transfers between devices, meet(): return lax.ppermute(values, axis, pairs)  3.85 us
    ppermute x4, waiting for transfers between devices, meet(): return lax.ppermute(values, axis, pairs)  3.34 us
    optimization_barrier x1, local copies, waits for them, and re-layouts, after(): return lax.optimization_barrier((values, others))[0]  2.29 us
  transfers between devices with their start and end apart: 19, of which 13 were waited for; matrix products, arithmetic and copies ran while one was open for 5% of the time, Pallas kernels for 11%

profile of v2, /device:TPU:0, one launch (start us, length us, event | category | flops | bytes accessed | tf_op | source)
XLA Modules:
  0.0 83.3 jit_solution(1931965219803738178)
XLA Ops:
  0.6 1.8 %pick.1 = (bf16[128,512]{1,0:T(8,128)(2,1)}, s32[1,128]{1,0:T(1,128)S(1)}) custom-call(s32[1,128]{1,0:T(1,128)} %pick_hbm.1, bf16[128,512]{1,0:T(8,128)(2,1)} %tile_hbm.3), custom_call_target="tpu_custom_call" | custom-call | tf_op jit(solution)/shard_map/pick/pallas_call | solution.py:97
  2.5 7.3 %all-to-all-start = ((bf16[8,16,512]{2,1,0:T(8,128)(2,1)}), bf16[8,16,512]{2,1,0:T(8,128)(2,1)S(1)}, u32[]{:S(2)}, u32[]{:S(2)}) async-start(bf16[8,16,512]{2,1,0:T(8,128)(2,1)} %bitcast.4), calls=%async_computation | async-start | bytes 262144 | tf_op jit(solution)/shard_map/all_to_all | solution.py:648
  9.8 2.3 %copy.18 = bf16[768,512]{0,1:T(8,128)(2,1)} copy(bf16[768,512]{1,0:T(8,128)(2,1)} %edge_hbm.3) | data formatting | bytes 1572864 | tf_op jit(solution)/shard_map/optimization_barrier | solution.py:562
  12.0 0.1 pad_add_fusion.where_ref
  12.1 5.0 %all-to-all-done = bf16[8,16,512]{2,1,0:T(8,128)(2,1)S(1)} async-done(((bf16[8,16,512]{2,1,0:T(8,128)(2,1)}), bf16[8,16,512]{2,1,0:T(8,128)(2,1)S(1)}, u32[]{:S(2)}, u32[]{:S(2)}) %all-to-all-start) | async-done | bytes 131104 | tf_op jit(solution)/shard_map/all_to_all | solution.py:648
  17.1 1.9 %pool.1 = (bf16[128,512]{1,0:T(8,128)(2,1)S(1)}, bf16[16,512]{1,0:T(8,128)(2,1)S(1)}, bf16[16,512]{1,0:T(8,128)(2,1)S(1)}, s32[1,128]{1,0:T(1,128)S(1)}, s32[1,32]{1,0:T(1,128)S(1)}) custom-call(s32[4]{0:T(128)S(1)} %pad_add_fusion.where_ref, s32[128]{0:T(128)} %from_hbm.1, s32[1,32]{1,0:T(1,128)} %cut_hbm.1, bf16[128,512]{1,0:T(8,128)(2,1)} %tile_hbm.3, ...), custom_call_target="tpu_custom_call" | custom-call | tf_op jit(solution)/shard_map/pool/pallas_call | solution.py:97
  19.0 1.6 %collective-permute-start.1 = (bf16[128,512]{1,0:T(8,128)(2,1)S(1)}, bf16[128,512]{1,0:T(8,128)(2,1)S(1)}, u32[]{:S(2)}, u32[]{:S(2)}) collective-permute-start(bf16[128,512]{1,0:T(8,128)(2,1)S(1)} %get-tuple-element.51.latent_ref), channel_id=1, source_target_pairs={{0,2},{1,3},{2,0},{3,1},{4,6},{5,7},{6,4},{7,5},{8,10},{9,11},{10,... | collective-permute-start | bytes 393224 | tf_op jit(solution)/shard_map/ppermute | solution.py:542
  20.6 0.2 collective-permute-start.2
  20.8 1.8 %collective-permute-start.3 = (bf16[16,512]{1,0:T(8,128)(2,1)S(1)}, bf16[16,512]{1,0:T(8,128)(2,1)S(1)}, u32[]{:S(2)}, u32[]{:S(2)}) collective-permute-start(bf16[16,512]{1,0:T(8,128)(2,1)S(1)} %get-tuple-element.53), channel_id=1, source_target_pairs={{0,28},{4,8},{8,4},{12,16},{16,12},{20,24},{24,20},{28,0},{1,29},{... | collective-permute-start | bytes 49160 | tf_op jit(solution)/shard_map/ppermute | solution.py:548
  22.6 3.0 %base.1 = (f32[768,512]{1,0:T(8,128)S(1)}, bf16[512,512]{1,0:T(8,128)(2,1)S(1)}, bf16[512,512]{1,0:T(8,128)(2,1)S(1)}) custom-call(s32[768]{0:T(1024)} %receiver_hbm.5, bf16[768,512]{1,0:T(8,128)(2,1)} %edge_hbm.3, bf16[1536,512]{1,0:T(8,128)(2,1)} %w_hbm.1, bf16[512,512]{1,0:T(8,128)(2,1)} %edge_out_hbm.1, bf16[128,512]{1,0:T(8,128)(2,1)S(1)} %get-tuple-element.51.latent_ref), custom_call_target="tpu_custom_call" | custom-call | tf_op jit(solution)/shard_map/base/pallas_call | solution.py:97
  25.6 0.0 collective-permute-done.2.first_ref
  25.6 1.6 %collective-permute-done.3.second_ref = bf16[16,512]{1,0:T(8,128)(2,1)S(1)} collective-permute-done((bf16[16,512]{1,0:T(8,128)(2,1)S(1)}, bf16[16,512]{1,0:T(8,128)(2,1)S(1)}, u32[]{:S(2)}, u32[]{:S(2)}) %collective-permute-start.3) | collective-permute-done | bytes 16416 | tf_op jit(solution)/shard_map/ppermute | solution.py:548
  27.2 0.0 collective-permute-done.1.far_ref
  27.2 0.0 collective-permute-start.4
  27.2 0.0 collective-permute-done.near_ref
  27.2 1.3 %collective-permute-done.4.cross_ref = bf16[128,512]{1,0:T(8,128)(2,1)S(1)} collective-permute-done((bf16[128,512]{1,0:T(8,128)(2,1)S(1)}, bf16[128,512]{1,0:T(8,128)(2,1)S(1)}, u32[]{:S(2)}, u32[]{:S(2)}) %collective-permute-start.4) | collective-permute-done | bytes 131104 | tf_op jit(solution)/shard_map/ppermute | solution.py:542
  28.6 11.6 %block.1 = (bf16[128,512]{1,0:T(8,128)(2,1)}, bf16[768,512]{1,0:T(8,128)(2,1)}, bf16[768,512]{1,0:T(8,128)(2,1)}, bf16[256,512]{1,0:T(8,128)(2,1)}, f32[128,512]...) custom-call(s32[4]{0:T(128)S(1)} %pad_add_fusion.where_ref, ...), custom_call_target="tpu_custom_call" | custom-call | tf_op jit(solution)/shard_map/block/pallas_call | solution.py:97
  40.1 0.2 collective-permute-start.6
  40.4 0.4 collective-permute-start.5
  40.7 0.0 collective-permute-start.7
  40.7 1.8 %collective-permute-start.8 = (bf16[16,512]{1,0:T(8,128)(2,1)S(1)}, bf16[16,512]{1,0:T(8,128)(2,1)S(1)}, u32[]{:S(2)}, u32[]{:S(2)}) collective-permute-start(bf16[16,512]{1,0:T(8,128)(2,1)S(1)} %get-tuple-element.72), channel_id=1, source_target_pairs={{0,28},{4,8},{8,4},{12,16},{16,12},{20,24},{24,20},{28,0},{1,29},{... | collective-permute-start | bytes 49160 | tf_op jit(solution)/shard_map/ppermute | solution.py:548
  42.5 0.7 collective-permute-done.6
  43.3 0.6 collective-permute-start.9
  43.9 1.5 %add_convert_fusion.1 = (bf16[1792,128]{1,0:T(8,128)(2,1)S(1)}, bf16[1792,128]{1,0:T(8,128)(2,1)S(1)}) fusion(bf16[4608,128]{1,0:T(8,128)(2,1)S(1)} %collective-permute-done.6, bf16[3584,128]{1,0:T(8,128)(2,1)} %get-tuple-element.69), kind=kLoop, calls=%fused_computation.1 | loop fusion | flops 1835008 | bytes 2752512 | tf_op jit(solution)/shard_map/convert_element_type | solution.py:586
  45.4 0.1 collective-permute-start.10
  45.5 1.7 %collective-permute-done.8.second_ref = bf16[16,512]{1,0:T(8,128)(2,1)S(1)} collective-permute-done((bf16[16,512]{1,0:T(8,128)(2,1)S(1)}, bf16[16,512]{1,0:T(8,128)(2,1)S(1)}, u32[]{:S(2)}, u32[]{:S(2)}) %collective-permute-start.8) | collective-permute-done | bytes 16416 | tf_op jit(solution)/shard_map/ppermute | solution.py:548
  47.2 1.7 %collective-permute-done.9 = bf16[512,128]{1,0:T(8,128)(2,1)S(1)} collective-permute-done((bf16[512,128]{1,0:T(8,128)(2,1)S(1)}, bf16[512,128]{1,0:T(8,128)(2,1)S(1)}, u32[]{:S(2)}, u32[]{:S(2)}) %collective-permute-start.9) | collective-permute-done | bytes 131104 | tf_op jit(solution)/shard_map/ppermute | solution.py:542
  48.9 0.2 add_convert_fusion
  49.2 0.5 collective-permute-start.11
  49.7 1.9 %node.1 = (bf16[128,512]{1,0:T(8,128)(2,1)S(1)}, bf16[128,512]{1,0:T(8,128)(2,1)}) custom-call(s32[4]{0:T(128)S(1)} %pad_add_fusion.where_ref, s32[1,128]{1,0:T(1,128)S(1)} %get-tuple-element.61.from_ref, s32[1,32]{1,0:T(1,128)S(1)} %get-tuple-element.62.cut_ref, bf16[512,512]{1,0:T(8,128)(2,1)S(1)} %get-tuple-element.56.w_send.w_send_ref, ...), custom_call_target="tpu_custom_call" | custom-call | tf_op jit(solution)/shard_map/node/pallas_call | solution.py:97
  51.6 3.4 %all-to-all-start.1 = ((bf16[8,16,512]{2,1,0:T(8,128)(2,1)}), bf16[8,16,512]{2,1,0:T(8,128)(2,1)S(1)}, u32[]{:S(2)}, u32[]{:S(2)}) async-start(bf16[8,16,512]{2,1,0:T(8,128)(2,1)} %bitcast.7), calls=%async_computation.1 | async-start | bytes 262144 | tf_op jit(solution)/shard_map/all_to_all | solution.py:648
  55.0 3.0 %collective-permute-done.10 = bf16[1792,128]{1,0:T(8,128)(2,1)S(1)} collective-permute-done((bf16[1792,128]{1,0:T(8,128)(2,1)S(1)}, bf16[1792,128]{1,0:T(8,128)(2,1)S(1)}, u32[]{:S(2)}, u32[]{:S(2)}) %collective-permute-start.10) | collective-permute-done | bytes 458784 | tf_op jit(solution)/shard_map/ppermute | solution.py:542
  57.9 4.8 %collective-permute-done.11 = bf16[1792,128]{1,0:T(8,128)(2,1)S(1)} collective-permute-done((bf16[1792,128]{1,0:T(8,128)(2,1)S(1)}, bf16[1792,128]{1,0:T(8,128)(2,1)S(1)}, u32[]{:S(2)}, u32[]{:S(2)}) %collective-permute-start.11) | collective-permute-done | bytes 458784 | tf_op jit(solution)/shard_map/ppermute | solution.py:542
  62.7 0.2 add_convert_fusion.4
  63.0 0.1 collective-permute-start.14
  63.1 0.6 collective-permute-start.12
  63.7 0.8 %back.1 = bf16[128,512]{1,0:T(8,128)(2,1)} custom-call(s32[1,128]{1,0:T(1,128)S(1)} %get-tuple-element.60.pick_ref, bf16[128,512]{1,0:T(8,128)(2,1)S(1)} %get-tuple-element.77.stay_ref, bf16[128,512]{1,0:T(8,128)(2,1)S(1)} %bitcast.10), custom_call_target="tpu_custom_call" | custom-call | tf_op jit(solution)/shard_map/back/pallas_call | solution.py:97
  64.5 3.2 %edge_grad.1 = bf16[768,512]{1,0:T(8,128)(2,1)} custom-call(s32[768]{0:T(1024)} %receiver_hbm.5, bf16[768,512]{1,0:T(8,128)(2,1)} %get-tuple-element.85.pre_grad_hbm, bf16[768,512]{1,0:T(8,128)(2,1)} %edge_cot_hbm.3, bf16[1536,512]{1,0:T(8,128)(2,1)} %w_hbm.1, bf16[256,512]{1,0:T(8,128)(2,1)} %get-tuple-element.86.agg_parts_hbm), custom_call_target="tpu_custom_call" | custom-call | tf_op jit(solution)/shard_map/edge_grad/pallas_call | solution.py:97
  67.7 1.3 %collective-permute-done.14 = bf16[896,128]{1,0:T(8,128)(2,1)S(1)} collective-permute-done((bf16[896,128]{1,0:T(8,128)(2,1)S(1)}, bf16[896,128]{1,0:T(8,128)(2,1)S(1)}, u32[]{:S(2)}, u32[]{:S(2)}) %collective-permute-start.14) | collective-permute-done | bytes 229408 | tf_op jit(solution)/shard_map/ppermute | solution.py:542
  69.1 0.6 collective-permute-start.15
  69.7 0.6 collective-permute-done.12
  70.3 0.1 collective-permute-start.13
  70.4 3.5 %collective-permute-done.15 = bf16[448,128]{1,0:T(8,128)(2,1)S(1)} collective-permute-done((bf16[448,128]{1,0:T(8,128)(2,1)S(1)}, bf16[448,128]{1,0:T(8,128)(2,1)S(1)}, u32[]{:S(2)}, u32[]{:S(2)}) %collective-permute-start.15) | collective-permute-done | bytes 114720 | tf_op jit(solution)/shard_map/ppermute | solution.py:542
  74.0 2.5 %collective-permute-done.13 = bf16[448,128]{1,0:T(8,128)(2,1)S(1)} collective-permute-done((bf16[448,128]{1,0:T(8,128)(2,1)S(1)}, bf16[448,128]{1,0:T(8,128)(2,1)S(1)}, u32[]{:S(2)}, u32[]{:S(2)}) %collective-permute-start.13) | collective-permute-done | bytes 114720 | tf_op jit(solution)/shard_map/ppermute | solution.py:542
  76.4 0.1 select_convert_fusion
  76.5 0.1 collective-permute-start.16
  76.6 5.9 %collective-permute-done.16 = bf16[448,128]{1,0:T(8,128)(2,1)S(1)} collective-permute-done((bf16[448,128]{1,0:T(8,128)(2,1)S(1)}, bf16[448,128]{1,0:T(8,128)(2,1)S(1)}, u32[]{:S(2)}, u32[]{:S(2)}) %collective-permute-start.16) | collective-permute-done | bytes 114720 | tf_op jit(solution)/shard_map/ppermute | solution.py:542
  82.5 0.8 convert_add_fusion.1
  (10 shorter events, 0.2 us)
Async XLA Ops:
  2.5 14.6 %all-to-all-start = ((bf16[8,16,512]{2,1,0:T(8,128)(2,1)}), bf16[8,16,512]{2,1,0:T(8,128)(2,1)S(1)}, u32[]{:S(2)}, u32[]{:S(2)}) async-start(bf16[8,16,512]{2,1,0:T(8,128)(2,1)} %bitcast.4), calls=%async_computation | async-start | bytes 262144 | tf_op jit(solution)/shard_map/all_to_all | solution.py:648
  19.0 8.2 %collective-permute-start.1 = (bf16[128,512]{1,0:T(8,128)(2,1)S(1)}, bf16[128,512]{1,0:T(8,128)(2,1)S(1)}, u32[]{:S(2)}, u32[]{:S(2)}) collective-permute-start(bf16[128,512]{1,0:T(8,128)(2,1)S(1)} %get-tuple-element.51.latent_ref), channel_id=1, source_target_pairs={{0,2},{1,3},{2,0},{3,1},{4,6},{5,7},{6,4},{7,5},{8,10},{9,11},{10,... | collective-permute-start | bytes 393224 | tf_op jit(solution)/shard_map/ppermute | solution.py:542
  20.6 5.0 %collective-permute-start.2 = (bf16[16,512]{1,0:T(8,128)(2,1)S(1)}, bf16[16,512]{1,0:T(8,128)(2,1)S(1)}, u32[]{:S(2)}, u32[]{:S(2)}) collective-permute-start(bf16[16,512]{1,0:T(8,128)(2,1)S(1)} %get-tuple-element.52), channel_id=1, source_target_pairs={{0,4},{4,0},{8,12},{12,8},{16,20},{20,16},{24,28},{28,24},{1,5},{5... | collective-permute-start | bytes 49160 | tf_op jit(solution)/shard_map/ppermute | solution.py:548
  20.8 6.4 %collective-permute-start.3 = (bf16[16,512]{1,0:T(8,128)(2,1)S(1)}, bf16[16,512]{1,0:T(8,128)(2,1)S(1)}, u32[]{:S(2)}, u32[]{:S(2)}) collective-permute-start(bf16[16,512]{1,0:T(8,128)(2,1)S(1)} %get-tuple-element.53), channel_id=1, source_target_pairs={{0,28},{4,8},{8,4},{12,16},{16,12},{20,24},{24,20},{28,0},{1,29},{... | collective-permute-start | bytes 49160 | tf_op jit(solution)/shard_map/ppermute | solution.py:548
  22.6 4.6 %collective-permute-start = (bf16[128,512]{1,0:T(8,128)(2,1)S(1)}, bf16[128,512]{1,0:T(8,128)(2,1)S(1)}, u32[]{:S(2)}, u32[]{:S(2)}) collective-permute-start(bf16[128,512]{1,0:T(8,128)(2,1)S(1)} %get-tuple-element.51.latent_ref), channel_id=1, source_target_pairs={{0,1},{1,0},{2,3},{3,2},{4,5},{5,4},{6,7},{7,6},{8,9},{9,8},{10,11... | collective-permute-start | bytes 393224 | tf_op jit(solution)/shard_map/ppermute | solution.py:542
  27.2 1.3 %collective-permute-start.4 = (bf16[128,512]{1,0:T(8,128)(2,1)S(1)}, bf16[128,512]{1,0:T(8,128)(2,1)S(1)}, u32[]{:S(2)}, u32[]{:S(2)}) collective-permute-start(bf16[128,512]{1,0:T(8,128)(2,1)S(1)} %collective-permute-done.1.far_ref), channel_id=1, source_target_pairs={{0,1},{1,0},{2,3},{3,2},{4,5},{5,4},{6,7},{7,6},{8,9},{9,8},{10,11... | collective-permute-start | bytes 393224 | tf_op jit(solution)/shard_map/ppermute | solution.py:542
  40.1 3.1 %collective-permute-start.6 = (bf16[4608,128]{1,0:T(8,128)(2,1)}, bf16[4608,128]{1,0:T(8,128)(2,1)S(1)}, u32[]{:S(2)}, u32[]{:S(2)}) collective-permute-start(bf16[4608,128]{1,0:T(8,128)(2,1)} %get-tuple-element.67), channel_id=1, source_target_pairs={{0,1},{1,0},{2,3},{3,2},{4,5},{5,4},{6,7},{7,6},{8,9},{9,8},{10,11... | collective-permute-start | bytes 3538952 | tf_op jit(solution)/shard_map/ppermute | solution.py:542
  40.4 6.8 %collective-permute-start.5 = (bf16[3584,128]{1,0:T(8,128)(2,1)}, bf16[3584,128]{1,0:T(8,128)(2,1)S(1)}, u32[]{:S(2)}, u32[]{:S(2)}) collective-permute-start(bf16[3584,128]{1,0:T(8,128)(2,1)} %get-tuple-element.65), channel_id=1, source_target_pairs={{0,1},{1,0},{2,3},{3,2},{4,5},{5,4},{6,7},{7,6},{8,9},{9,8},{10,11... | collective-permute-start | bytes 2752520 | tf_op jit(solution)/shard_map/ppermute | solution.py:542
  40.7 4.8 %collective-permute-start.7 = (bf16[16,512]{1,0:T(8,128)(2,1)S(1)}, bf16[16,512]{1,0:T(8,128)(2,1)S(1)}, u32[]{:S(2)}, u32[]{:S(2)}) collective-permute-start(bf16[16,512]{1,0:T(8,128)(2,1)S(1)} %get-tuple-element.71), channel_id=1, source_target_pairs={{0,4},{4,0},{8,12},{12,8},{16,20},{20,16},{24,28},{28,24},{1,5},{5... | collective-permute-start | bytes 49160 | tf_op jit(solution)/shard_map/ppermute | solution.py:548
  40.7 6.4 %collective-permute-start.8 = (bf16[16,512]{1,0:T(8,128)(2,1)S(1)}, bf16[16,512]{1,0:T(8,128)(2,1)S(1)}, u32[]{:S(2)}, u32[]{:S(2)}) collective-permute-start(bf16[16,512]{1,0:T(8,128)(2,1)S(1)} %get-tuple-element.72), channel_id=1, source_target_pairs={{0,28},{4,8},{8,4},{12,16},{16,12},{20,24},{24,20},{28,0},{1,29},{... | collective-permute-start | bytes 49160 | tf_op jit(solution)/shard_map/ppermute | solution.py:548
  43.3 5.6 %collective-permute-start.9 = (bf16[512,128]{1,0:T(8,128)(2,1)S(1)}, bf16[512,128]{1,0:T(8,128)(2,1)S(1)}, u32[]{:S(2)}, u32[]{:S(2)}) collective-permute-start(bf16[512,128]{1,0:T(8,128)(2,1)S(1)} %add_convert_fusion.8), channel_id=1, source_target_pairs={{0,2},{1,3},{2,0},{3,1},{4,6},{5,7},{6,4},{7,5},{8,10},{9,11},{10,... | collective-permute-start | bytes 393224 | tf_op jit(solution)/shard_map/ppermute | solution.py:542
  43.9 5.0 %copy-start = (bf16[3584,128]{1,0:T(8,128)(2,1)S(1)}, bf16[3584,128]{1,0:T(8,128)(2,1)}, u32[]{:S(2)}) copy-start(bf16[3584,128]{1,0:T(8,128)(2,1)} %get-tuple-element.73) | copy-start | bytes 2752516
  45.4 12.5 %collective-permute-start.10 = (bf16[1792,128]{1,0:T(8,128)(2,1)S(1)}, bf16[1792,128]{1,0:T(8,128)(2,1)S(1)}, u32[]{:S(2)}, u32[]{:S(2)}) collective-permute-start(bf16[1792,128]{1,0:T(8,128)(2,1)S(1)} %get-tuple-element.92), channel_id=1, source_target_pairs={{0,4},{4,0},{8,12},{12,8},{16,20},{20,16},{24,28},{28,24},{1,5},{5... | collective-permute-start | bytes 1376264 | tf_op jit(solution)/shard_map/ppermute | solution.py:542
  49.2 13.6 %collective-permute-start.11 = (bf16[1792,128]{1,0:T(8,128)(2,1)S(1)}, bf16[1792,128]{1,0:T(8,128)(2,1)S(1)}, u32[]{:S(2)}, u32[]{:S(2)}) collective-permute-start(bf16[1792,128]{1,0:T(8,128)(2,1)S(1)} %get-tuple-element.94), channel_id=1, source_target_pairs={{0,8},{4,12},{8,0},{12,4},{16,24},{20,28},{24,16},{28,20},{1,9},{5... | collective-permute-start | bytes 1376264 | tf_op jit(solution)/shard_map/ppermute | solution.py:542
  51.6 12.1 %all-to-all-start.1 = ((bf16[8,16,512]{2,1,0:T(8,128)(2,1)}), bf16[8,16,512]{2,1,0:T(8,128)(2,1)S(1)}, u32[]{:S(2)}, u32[]{:S(2)}) async-start(bf16[8,16,512]{2,1,0:T(8,128)(2,1)} %bitcast.7), calls=%async_computation.1 | async-start | bytes 262144 | tf_op jit(solution)/shard_map/all_to_all | solution.py:648
  63.0 6.1 %collective-permute-start.14 = (bf16[896,128]{1,0:T(8,128)(2,1)S(1)}, bf16[896,128]{1,0:T(8,128)(2,1)S(1)}, u32[]{:S(2)}, u32[]{:S(2)}) collective-permute-start(bf16[896,128]{1,0:T(8,128)(2,1)S(1)} %get-tuple-element.96), channel_id=1, source_target_pairs={{0,4},{4,0},{8,12},{12,8},{16,20},{20,16},{24,28},{28,24},{1,5},{5... | collective-permute-start | bytes 688136 | tf_op jit(solution)/shard_map/ppermute | solution.py:542
  63.1 7.2 %collective-permute-start.12 = (bf16[896,128]{1,0:T(8,128)(2,1)S(1)}, bf16[896,128]{1,0:T(8,128)(2,1)S(1)}, u32[]{:S(2)}, u32[]{:S(2)}) collective-permute-start(bf16[896,128]{1,0:T(8,128)(2,1)S(1)} %get-tuple-element.99), channel_id=1, source_target_pairs={{0,2},{1,3},{2,0},{3,1},{4,6},{5,7},{6,4},{7,5},{8,10},{9,11},{10,... | collective-permute-start | bytes 688136 | tf_op jit(solution)/shard_map/ppermute | solution.py:542
  69.1 4.9 %collective-permute-start.15 = (bf16[448,128]{1,0:T(8,128)(2,1)S(1)}, bf16[448,128]{1,0:T(8,128)(2,1)S(1)}, u32[]{:S(2)}, u32[]{:S(2)}) collective-permute-start(bf16[448,128]{1,0:T(8,128)(2,1)S(1)} %add_convert_fusion.9), channel_id=1, source_target_pairs={{0,2},{1,3},{2,0},{3,1},{4,6},{5,7},{6,4},{7,5},{8,10},{9,11},{10,... | collective-permute-start | bytes 344072 | tf_op jit(solution)/shard_map/ppermute | solution.py:542
  70.3 6.1 %collective-permute-start.13 = (bf16[448,128]{1,0:T(8,128)(2,1)S(1)}, bf16[448,128]{1,0:T(8,128)(2,1)S(1)}, u32[]{:S(2)}, u32[]{:S(2)}) collective-permute-start(bf16[448,128]{1,0:T(8,128)(2,1)S(1)} %add_convert_fusion.11), channel_id=1, source_target_pairs={{0,8},{4,12},{8,0},{12,4},{16,24},{20,28},{24,16},{28,20},{1,9},{5... | collective-permute-start | bytes 344072 | tf_op jit(solution)/shard_map/ppermute | solution.py:542
  76.5 6.0 %collective-permute-start.16 = (bf16[448,128]{1,0:T(8,128)(2,1)S(1)}, bf16[448,128]{1,0:T(8,128)(2,1)S(1)}, u32[]{:S(2)}, u32[]{:S(2)}) collective-permute-start(bf16[448,128]{1,0:T(8,128)(2,1)S(1)} %select_convert_fusion), channel_id=1, source_target_pairs={{0,16},{4,20},{8,24},{12,28},{16,0},{20,4},{24,8},{28,12},{1,17},{... | collective-permute-start | bytes 344072 | tf_op jit(solution)/shard_map/ppermute | solution.py:542

commit v3 on v2

--- a/solution.py
+++ b/solution.py
@@ -555,7 +555,7 @@
 def exchange_orders():
     cross, dom_bits = axis_bits("tile")[1:], axis_bits("dom")
     side, line = dom_bits[:1], dom_bits[1:-1]
-    return side + cross + line, line + side + cross
+    return cross + side + line, line + cross + side
 
 
 def after(values, *others):
@@ -768,7 +768,16 @@
         SMALL_LIMIT,
     )
     back_rows = exchange(slot_grad)
-    sent = cut_all(parts, slot_grad)
+    [edge_grad] = call(
+        edge_grad_kernel,
+        "edge_grad",
+        [edge_bf16],
+        [edge_receiver, after(pre_grad, slot_grad), edge_cot, edge_in, agg_parts],
+        [edge_index, edge_bf16, edge_bf16, square, sds((2 * nodes, feat), BF16)]
+        + [edge_f32, edge_bf16, 5, edges // ROWS],
+        limit=2 * SMALL_LIMIT,
+    )
+    sent = cut_all(parts, edge_grad)
     send_all(parts)
     [latent_grad] = call(
         back_kernel,
@@ -778,16 +787,7 @@
         [node_bf16, 1],
         limit=SMALL_LIMIT,
     )
-    [edge_grad] = call(
-        edge_grad_kernel,
-        "edge_grad",
-        [edge_bf16],
-        [edge_receiver, after(pre_grad, latent_grad), edge_cot, edge_in, agg_parts],
-        [edge_index, edge_bf16, edge_bf16, square, sds((2 * nodes, feat), BF16)]
-        + [edge_f32, edge_bf16, 5, edges // ROWS],
-        limit=2 * SMALL_LIMIT,
-    )
-    first = edge_grad
+    first = latent_grad
     while parts[0].order:
         cut_all(parts, first)
         send_all(parts)

time: 83.8 us -> 83.6 us (level)
  waiting for transfers between devices: 33.7 us -> 32.4 us
  starting transfers between devices: 19.2 us -> 20.4 us
    ppermute x4, waiting for transfers between devices: 3.34 us -> 1.87 us  [meet(): return lax.ppermute(values, axis, pairs)]
    ppermute x13, starting transfers between devices: 4.67 us -> 5.85 us  [flip(): return lax.ppermute(values, axis, [(i, i ^ mask) for i in range(count)])]
  transfers between devices with their start and end apart: 19 -> 19, of which waited for: 13 -> 12; matrix products, arithmetic and copies ran while one was open for 5% -> 5% of each run, Pallas kernels for 11% -> 11%
where the time goes in v3:
time: 83.6 us; the launch traced here: 83.1 us
  waiting for transfers between devices  32.4 us (39%)
  Pallas kernels  24.2 us (29%)
  starting transfers between devices  20.4 us (24%)
  other arithmetic  3.06 us (4%)
  local copies, waits for them, and re-layouts  2.29 us (3%)
    ppermute x13, waiting for transfers between devices, flip(): return lax.ppermute(values, axis, [(i, i ^ mask) for i in range(count)])  25.5 us
    pallas_call x7, Pallas kernels, call(): pl.pallas_call(kernel, out_shape=[array.array if isinstance(array, Kept)...  24.2 us
    all_to_all x2, starting transfers between devices, exchange(): lax.all_to_all(blocks, 'dom', split_axis=0, concat_axis=0, tiled=True)  10.7 us
    ppermute x13, starting transfers between devices, flip(): return lax.ppermute(values, axis, [(i, i ^ mask) for i in range(count)])  5.85 us
    all_to_all x2, waiting for transfers between devices, exchange(): lax.all_to_all(blocks, 'dom', split_axis=0, concat_axis=0, tiled=True)  4.98 us
    ppermute x4, starting transfers between devices, meet(): return lax.ppermute(values, axis, pairs)  3.85 us
    optimization_barrier x1, local copies, waits for them, and re-layouts, after(): return lax.optimization_barrier((values, others))[0]  2.29 us
    convert_element_type x5, other arithmetic, half(): return total_of([a[first:first + self.count] for a in arrays]).astype(BF16)  2.03 us
  transfers between devices with their start and end apart: 19, of which 12 were waited for; matrix products, arithmetic and copies ran while one was open for 5% of the time, Pallas kernels for 11%

profile of v3, /device:TPU:0, one launch (start us, length us, event | category | flops | bytes accessed | tf_op | source)
XLA Modules:
  0.0 83.1 jit_solution(7296123174146820648)
XLA Ops:
  0.6 1.8 %pick.1 = (bf16[128,512]{1,0:T(8,128)(2,1)}, s32[1,128]{1,0:T(1,128)S(1)}) custom-call(s32[1,128]{1,0:T(1,128)} %pick_hbm.1, bf16[128,512]{1,0:T(8,128)(2,1)} %tile_hbm.3), custom_call_target="tpu_custom_call" | custom-call | tf_op jit(solution)/shard_map/pick/pallas_call | solution.py:97
  2.5 7.3 %all-to-all-start = ((bf16[8,16,512]{2,1,0:T(8,128)(2,1)}), bf16[8,16,512]{2,1,0:T(8,128)(2,1)S(1)}, u32[]{:S(2)}, u32[]{:S(2)}) async-start(bf16[8,16,512]{2,1,0:T(8,128)(2,1)} %bitcast.4), calls=%async_computation | async-start | bytes 262144 | tf_op jit(solution)/shard_map/all_to_all | solution.py:648
  9.8 2.3 %copy.18 = bf16[768,512]{0,1:T(8,128)(2,1)} copy(bf16[768,512]{1,0:T(8,128)(2,1)} %edge_hbm.3) | data formatting | bytes 1572864 | tf_op jit(solution)/shard_map/optimization_barrier | solution.py:562
  12.0 0.1 pad_add_fusion.where_ref
  12.1 5.0 %all-to-all-done = bf16[8,16,512]{2,1,0:T(8,128)(2,1)S(1)} async-done(((bf16[8,16,512]{2,1,0:T(8,128)(2,1)}), bf16[8,16,512]{2,1,0:T(8,128)(2,1)S(1)}, u32[]{:S(2)}, u32[]{:S(2)}) %all-to-all-start) | async-done | bytes 131104 | tf_op jit(solution)/shard_map/all_to_all | solution.py:648
  17.1 1.9 %pool.1 = (bf16[128,512]{1,0:T(8,128)(2,1)S(1)}, bf16[16,512]{1,0:T(8,128)(2,1)S(1)}, bf16[16,512]{1,0:T(8,128)(2,1)S(1)}, s32[1,128]{1,0:T(1,128)S(1)}, s32[1,32]{1,0:T(1,128)S(1)}) custom-call(s32[4]{0:T(128)S(1)} %pad_add_fusion.where_ref, s32[128]{0:T(128)} %from_hbm.1, s32[1,32]{1,0:T(1,128)} %cut_hbm.1, bf16[128,512]{1,0:T(8,128)(2,1)} %tile_hbm.3, ...), custom_call_target="tpu_custom_call" | custom-call | tf_op jit(solution)/shard_map/pool/pallas_call | solution.py:97
  19.0 1.6 %collective-permute-start.1 = (bf16[128,512]{1,0:T(8,128)(2,1)S(1)}, bf16[128,512]{1,0:T(8,128)(2,1)S(1)}, u32[]{:S(2)}, u32[]{:S(2)}) collective-permute-start(bf16[128,512]{1,0:T(8,128)(2,1)S(1)} %get-tuple-element.51.latent_ref), channel_id=1, source_target_pairs={{0,2},{1,3},{2,0},{3,1},{4,6},{5,7},{6,4},{7,5},{8,10},{9,11},{10,... | collective-permute-start | bytes 393224 | tf_op jit(solution)/shard_map/ppermute | solution.py:542
  20.6 0.2 collective-permute-start.2
  20.8 1.8 %collective-permute-start.3 = (bf16[16,512]{1,0:T(8,128)(2,1)S(1)}, bf16[16,512]{1,0:T(8,128)(2,1)S(1)}, u32[]{:S(2)}, u32[]{:S(2)}) collective-permute-start(bf16[16,512]{1,0:T(8,128)(2,1)S(1)} %get-tuple-element.53), channel_id=1, source_target_pairs={{0,28},{4,8},{8,4},{12,16},{16,12},{20,24},{24,20},{28,0},{1,29},{... | collective-permute-start | bytes 49160 | tf_op jit(solution)/shard_map/ppermute | solution.py:548
  22.6 0.0 collective-permute-start
  22.6 3.0 %base.1 = (f32[768,512]{1,0:T(8,128)S(1)}, bf16[512,512]{1,0:T(8,128)(2,1)S(1)}, bf16[512,512]{1,0:T(8,128)(2,1)S(1)}) custom-call(s32[768]{0:T(1024)} %receiver_hbm.5, bf16[768,512]{1,0:T(8,128)(2,1)} %edge_hbm.3, bf16[1536,512]{1,0:T(8,128)(2,1)} %w_hbm.1, bf16[512,512]{1,0:T(8,128)(2,1)} %edge_out_hbm.1, bf16[128,512]{1,0:T(8,128)(2,1)S(1)} %get-tuple-element.51.latent_ref), custom_call_target="tpu_custom_call" | custom-call | tf_op jit(solution)/shard_map/base/pallas_call | solution.py:97
  25.6 0.0 collective-permute-done.2.first_ref
  25.6 1.6 %collective-permute-done.3.second_ref = bf16[16,512]{1,0:T(8,128)(2,1)S(1)} collective-permute-done((bf16[16,512]{1,0:T(8,128)(2,1)S(1)}, bf16[16,512]{1,0:T(8,128)(2,1)S(1)}, u32[]{:S(2)}, u32[]{:S(2)}) %collective-permute-start.3) | collective-permute-done | bytes 16416 | tf_op jit(solution)/shard_map/ppermute | solution.py:548
  27.2 0.0 collective-permute-done.1.far_ref
  27.2 1.3 %collective-permute-done.4.cross_ref = bf16[128,512]{1,0:T(8,128)(2,1)S(1)} collective-permute-done((bf16[128,512]{1,0:T(8,128)(2,1)S(1)}, bf16[128,512]{1,0:T(8,128)(2,1)S(1)}, u32[]{:S(2)}, u32[]{:S(2)}) %collective-permute-start.4) | collective-permute-done | bytes 131104 | tf_op jit(solution)/shard_map/ppermute | solution.py:542
  28.6 11.6 %block.1 = (bf16[128,512]{1,0:T(8,128)(2,1)}, bf16[768,512]{1,0:T(8,128)(2,1)}, bf16[768,512]{1,0:T(8,128)(2,1)}, bf16[256,512]{1,0:T(8,128)(2,1)}, f32[128,512]...) custom-call(s32[4]{0:T(128)S(1)} %pad_add_fusion.where_ref, ...), custom_call_target="tpu_custom_call" | custom-call | tf_op jit(solution)/shard_map/block/pallas_call | solution.py:97
  40.1 0.2 collective-permute-start.6
  40.4 0.4 collective-permute-start.5
  40.7 0.0 collective-permute-start.7
  40.7 1.8 %collective-permute-start.8 = (bf16[16,512]{1,0:T(8,128)(2,1)S(1)}, bf16[16,512]{1,0:T(8,128)(2,1)S(1)}, u32[]{:S(2)}, u32[]{:S(2)}) collective-permute-start(bf16[16,512]{1,0:T(8,128)(2,1)S(1)} %get-tuple-element.72), channel_id=1, source_target_pairs={{0,28},{4,8},{8,4},{12,16},{16,12},{20,24},{24,20},{28,0},{1,29},{... | collective-permute-start | bytes 49160 | tf_op jit(solution)/shard_map/ppermute | solution.py:548
  42.5 0.7 collective-permute-done.6
  43.3 0.6 collective-permute-start.9
  43.9 1.5 %add_convert_fusion.1 = (bf16[1792,128]{1,0:T(8,128)(2,1)S(1)}, bf16[1792,128]{1,0:T(8,128)(2,1)S(1)}) fusion(bf16[4608,128]{1,0:T(8,128)(2,1)S(1)} %collective-permute-done.6, bf16[3584,128]{1,0:T(8,128)(2,1)} %get-tuple-element.69), kind=kLoop, calls=%fused_computation.1 | loop fusion | flops 1835008 | bytes 2752512 | tf_op jit(solution)/shard_map/convert_element_type | solution.py:586
  45.4 1.6 %collective-permute-start.10 = (bf16[1792,128]{1,0:T(8,128)(2,1)S(1)}, bf16[1792,128]{1,0:T(8,128)(2,1)S(1)}, u32[]{:S(2)}, u32[]{:S(2)}) collective-permute-start(bf16[1792,128]{1,0:T(8,128)(2,1)S(1)} %get-tuple-element.92), channel_id=1, source_target_pairs={{0,2},{1,3},{2,0},{3,1},{4,6},{5,7},{6,4},{7,5},{8,10},{9,11},{10,... | collective-permute-start | bytes 1376264 | tf_op jit(solution)/shard_map/ppermute | solution.py:542
  46.9 0.0 collective-permute-done.7.first_ref
  46.9 0.2 collective-permute-done.8.second_ref
  47.2 0.0 collective-permute-done.5
  47.2 2.5 %collective-permute-done.9 = bf16[512,128]{1,0:T(8,128)(2,1)S(1)} collective-permute-done((bf16[512,128]{1,0:T(8,128)(2,1)S(1)}, bf16[512,128]{1,0:T(8,128)(2,1)S(1)}, u32[]{:S(2)}, u32[]{:S(2)}) %collective-permute-start.9) | collective-permute-done | bytes 131104 | tf_op jit(solution)/shard_map/ppermute | solution.py:542
  49.7 0.2 add_convert_fusion
  50.0 0.8 collective-permute-start.11
  50.7 1.9 %node.1 = (bf16[128,512]{1,0:T(8,128)(2,1)S(1)}, bf16[128,512]{1,0:T(8,128)(2,1)}) custom-call(s32[4]{0:T(128)S(1)} %pad_add_fusion.where_ref, s32[1,128]{1,0:T(1,128)S(1)} %get-tuple-element.61.from_ref, s32[1,32]{1,0:T(1,128)S(1)} %get-tuple-element.62.cut_ref, bf16[512,512]{1,0:T(8,128)(2,1)S(1)} %get-tuple-element.56.w_send.w_send_ref, ...), custom_call_target="tpu_custom_call" | custom-call | tf_op jit(solution)/shard_map/node/pallas_call | solution.py:97
  52.7 3.4 %all-to-all-start.1 = ((bf16[8,16,512]{2,1,0:T(8,128)(2,1)}), bf16[8,16,512]{2,1,0:T(8,128)(2,1)S(1)}, u32[]{:S(2)}, u32[]{:S(2)}) async-start(bf16[8,16,512]{2,1,0:T(8,128)(2,1)} %bitcast.7), calls=%async_computation.1 | async-start | bytes 262144 | tf_op jit(solution)/shard_map/all_to_all | solution.py:648
  56.0 3.2 %edge_grad.1 = bf16[768,512]{1,0:T(8,128)(2,1)} custom-call(s32[768]{0:T(1024)} %receiver_hbm.5, bf16[768,512]{1,0:T(8,128)(2,1)} %get-tuple-element.80.pre_grad_hbm, bf16[768,512]{1,0:T(8,128)(2,1)} %edge_cot_hbm.3, bf16[1536,512]{1,0:T(8,128)(2,1)} %w_hbm.1, bf16[256,512]{1,0:T(8,128)(2,1)} %get-tuple-element.81.agg_parts_hbm), custom_call_target="tpu_custom_call" | custom-call | tf_op jit(solution)/shard_map/edge_grad/pallas_call | solution.py:97
  59.3 3.5 %collective-permute-done.11 = bf16[1792,128]{1,0:T(8,128)(2,1)S(1)} collective-permute-done((bf16[1792,128]{1,0:T(8,128)(2,1)S(1)}, bf16[1792,128]{1,0:T(8,128)(2,1)S(1)}, u32[]{:S(2)}, u32[]{:S(2)}) %collective-permute-start.11) | collective-permute-done | bytes 458784 | tf_op jit(solution)/shard_map/ppermute | solution.py:542
  62.7 0.2 add_convert_fusion.4
  63.0 0.6 collective-permute-start.14
  63.6 0.0 collective-permute-start.12
  63.6 0.8 %back.1 = bf16[128,512]{1,0:T(8,128)(2,1)} custom-call(s32[1,128]{1,0:T(1,128)S(1)} %get-tuple-element.60.pick_ref, bf16[128,512]{1,0:T(8,128)(2,1)S(1)} %get-tuple-element.77.stay_ref, bf16[128,512]{1,0:T(8,128)(2,1)S(1)} %bitcast.10), custom_call_target="tpu_custom_call" | custom-call | tf_op jit(solution)/shard_map/back/pallas_call | solution.py:97
  64.4 4.6 %collective-permute-done.14 = bf16[896,128]{1,0:T(8,128)(2,1)S(1)} collective-permute-done((bf16[896,128]{1,0:T(8,128)(2,1)S(1)}, bf16[896,128]{1,0:T(8,128)(2,1)S(1)}, u32[]{:S(2)}, u32[]{:S(2)}) %collective-permute-start.14) | collective-permute-done | bytes 229408 | tf_op jit(solution)/shard_map/ppermute | solution.py:542
  69.1 0.1 collective-permute-start.15
  69.2 1.3 %collective-permute-done.12 = bf16[896,128]{1,0:T(8,128)(2,1)S(1)} collective-permute-done((bf16[896,128]{1,0:T(8,128)(2,1)S(1)}, bf16[896,128]{1,0:T(8,128)(2,1)S(1)}, u32[]{:S(2)}, u32[]{:S(2)}) %collective-permute-start.12) | collective-permute-done | bytes 229408 | tf_op jit(solution)/shard_map/ppermute | solution.py:542
  70.5 0.1 collective-permute-start.13
  70.6 3.3 %collective-permute-done.15 = bf16[448,128]{1,0:T(8,128)(2,1)S(1)} collective-permute-done((bf16[448,128]{1,0:T(8,128)(2,1)S(1)}, bf16[448,128]{1,0:T(8,128)(2,1)S(1)}, u32[]{:S(2)}, u32[]{:S(2)}) %collective-permute-start.15) | collective-permute-done | bytes 114720 | tf_op jit(solution)/shard_map/ppermute | solution.py:542
  74.0 2.2 %collective-permute-done.13 = bf16[448,128]{1,0:T(8,128)(2,1)S(1)} collective-permute-done((bf16[448,128]{1,0:T(8,128)(2,1)S(1)}, bf16[448,128]{1,0:T(8,128)(2,1)S(1)}, u32[]{:S(2)}, u32[]{:S(2)}) %collective-permute-start.13) | collective-permute-done | bytes 114720 | tf_op jit(solution)/shard_map/ppermute | solution.py:542
  76.2 0.1 select_convert_fusion
  76.3 0.1 collective-permute-start.16
  76.4 5.9 %collective-permute-done.16 = bf16[448,128]{1,0:T(8,128)(2,1)S(1)} collective-permute-done((bf16[448,128]{1,0:T(8,128)(2,1)S(1)}, bf16[448,128]{1,0:T(8,128)(2,1)S(1)}, u32[]{:S(2)}, u32[]{:S(2)}) %collective-permute-start.16) | collective-permute-done | bytes 114720 | tf_op jit(solution)/shard_map/ppermute | solution.py:542
  82.3 0.8 convert_add_fusion.1
  (10 shorter events, 0.2 us)
Async XLA Ops:
  2.5 14.6 %all-to-all-start = ((bf16[8,16,512]{2,1,0:T(8,128)(2,1)}), bf16[8,16,512]{2,1,0:T(8,128)(2,1)S(1)}, u32[]{:S(2)}, u32[]{:S(2)}) async-start(bf16[8,16,512]{2,1,0:T(8,128)(2,1)} %bitcast.4), calls=%async_computation | async-start | bytes 262144 | tf_op jit(solution)/shard_map/all_to_all | solution.py:648
  19.0 8.2 %collective-permute-start.1 = (bf16[128,512]{1,0:T(8,128)(2,1)S(1)}, bf16[128,512]{1,0:T(8,128)(2,1)S(1)}, u32[]{:S(2)}, u32[]{:S(2)}) collective-permute-start(bf16[128,512]{1,0:T(8,128)(2,1)S(1)} %get-tuple-element.51.latent_ref), channel_id=1, source_target_pairs={{0,2},{1,3},{2,0},{3,1},{4,6},{5,7},{6,4},{7,5},{8,10},{9,11},{10,... | collective-permute-start | bytes 393224 | tf_op jit(solution)/shard_map/ppermute | solution.py:542
  20.6 5.0 %collective-permute-start.2 = (bf16[16,512]{1,0:T(8,128)(2,1)S(1)}, bf16[16,512]{1,0:T(8,128)(2,1)S(1)}, u32[]{:S(2)}, u32[]{:S(2)}) collective-permute-start(bf16[16,512]{1,0:T(8,128)(2,1)S(1)} %get-tuple-element.52), channel_id=1, source_target_pairs={{0,4},{4,0},{8,12},{12,8},{16,20},{20,16},{24,28},{28,24},{1,5},{5... | collective-permute-start | bytes 49160 | tf_op jit(solution)/shard_map/ppermute | solution.py:548
  20.8 6.4 %collective-permute-start.3 = (bf16[16,512]{1,0:T(8,128)(2,1)S(1)}, bf16[16,512]{1,0:T(8,128)(2,1)S(1)}, u32[]{:S(2)}, u32[]{:S(2)}) collective-permute-start(bf16[16,512]{1,0:T(8,128)(2,1)S(1)} %get-tuple-element.53), channel_id=1, source_target_pairs={{0,28},{4,8},{8,4},{12,16},{16,12},{20,24},{24,20},{28,0},{1,29},{... | collective-permute-start | bytes 49160 | tf_op jit(solution)/shard_map/ppermute | solution.py:548
  22.6 4.6 %collective-permute-start = (bf16[128,512]{1,0:T(8,128)(2,1)S(1)}, bf16[128,512]{1,0:T(8,128)(2,1)S(1)}, u32[]{:S(2)}, u32[]{:S(2)}) collective-permute-start(bf16[128,512]{1,0:T(8,128)(2,1)S(1)} %get-tuple-element.51.latent_ref), channel_id=1, source_target_pairs={{0,1},{1,0},{2,3},{3,2},{4,5},{5,4},{6,7},{7,6},{8,9},{9,8},{10,11... | collective-permute-start | bytes 393224 | tf_op jit(solution)/shard_map/ppermute | solution.py:542
  27.2 1.3 %collective-permute-start.4 = (bf16[128,512]{1,0:T(8,128)(2,1)S(1)}, bf16[128,512]{1,0:T(8,128)(2,1)S(1)}, u32[]{:S(2)}, u32[]{:S(2)}) collective-permute-start(bf16[128,512]{1,0:T(8,128)(2,1)S(1)} %collective-permute-done.1.far_ref), channel_id=1, source_target_pairs={{0,1},{1,0},{2,3},{3,2},{4,5},{5,4},{6,7},{7,6},{8,9},{9,8},{10,11... | collective-permute-start | bytes 393224 | tf_op jit(solution)/shard_map/ppermute | solution.py:542
  40.1 3.1 %collective-permute-start.6 = (bf16[4608,128]{1,0:T(8,128)(2,1)}, bf16[4608,128]{1,0:T(8,128)(2,1)S(1)}, u32[]{:S(2)}, u32[]{:S(2)}) collective-permute-start(bf16[4608,128]{1,0:T(8,128)(2,1)} %get-tuple-element.67), channel_id=1, source_target_pairs={{0,1},{1,0},{2,3},{3,2},{4,5},{5,4},{6,7},{7,6},{8,9},{9,8},{10,11... | collective-permute-start | bytes 3538952 | tf_op jit(solution)/shard_map/ppermute | solution.py:542
  40.4 6.8 %collective-permute-start.5 = (bf16[3584,128]{1,0:T(8,128)(2,1)}, bf16[3584,128]{1,0:T(8,128)(2,1)S(1)}, u32[]{:S(2)}, u32[]{:S(2)}) collective-permute-start(bf16[3584,128]{1,0:T(8,128)(2,1)} %get-tuple-element.65), channel_id=1, source_target_pairs={{0,1},{1,0},{2,3},{3,2},{4,5},{5,4},{6,7},{7,6},{8,9},{9,8},{10,11... | collective-permute-start | bytes 2752520 | tf_op jit(solution)/shard_map/ppermute | solution.py:542
  40.7 6.2 %collective-permute-start.7 = (bf16[16,512]{1,0:T(8,128)(2,1)S(1)}, bf16[16,512]{1,0:T(8,128)(2,1)S(1)}, u32[]{:S(2)}, u32[]{:S(2)}) collective-permute-start(bf16[16,512]{1,0:T(8,128)(2,1)S(1)} %get-tuple-element.71), channel_id=1, source_target_pairs={{0,4},{4,0},{8,12},{12,8},{16,20},{20,16},{24,28},{28,24},{1,5},{5... | collective-permute-start | bytes 49160 | tf_op jit(solution)/shard_map/ppermute | solution.py:548
  40.7 6.4 %collective-permute-start.8 = (bf16[16,512]{1,0:T(8,128)(2,1)S(1)}, bf16[16,512]{1,0:T(8,128)(2,1)S(1)}, u32[]{:S(2)}, u32[]{:S(2)}) collective-permute-start(bf16[16,512]{1,0:T(8,128)(2,1)S(1)} %get-tuple-element.72), channel_id=1, source_target_pairs={{0,28},{4,8},{8,4},{12,16},{16,12},{20,24},{24,20},{28,0},{1,29},{... | collective-permute-start | bytes 49160 | tf_op jit(solution)/shard_map/ppermute | solution.py:548
  43.3 6.4 %collective-permute-start.9 = (bf16[512,128]{1,0:T(8,128)(2,1)S(1)}, bf16[512,128]{1,0:T(8,128)(2,1)S(1)}, u32[]{:S(2)}, u32[]{:S(2)}) collective-permute-start(bf16[512,128]{1,0:T(8,128)(2,1)S(1)} %add_convert_fusion.8), channel_id=1, source_target_pairs={{0,2},{1,3},{2,0},{3,1},{4,6},{5,7},{6,4},{7,5},{8,10},{9,11},{10,... | collective-permute-start | bytes 393224 | tf_op jit(solution)/shard_map/ppermute | solution.py:542
  43.9 5.8 %copy-start = (bf16[3584,128]{1,0:T(8,128)(2,1)S(1)}, bf16[3584,128]{1,0:T(8,128)(2,1)}, u32[]{:S(2)}) copy-start(bf16[3584,128]{1,0:T(8,128)(2,1)} %get-tuple-element.73) | copy-start | bytes 2752516
  45.4 13.9 %collective-permute-start.10 = (bf16[1792,128]{1,0:T(8,128)(2,1)S(1)}, bf16[1792,128]{1,0:T(8,128)(2,1)S(1)}, u32[]{:S(2)}, u32[]{:S(2)}) collective-permute-start(bf16[1792,128]{1,0:T(8,128)(2,1)S(1)} %get-tuple-element.92), channel_id=1, source_target_pairs={{0,2},{1,3},{2,0},{3,1},{4,6},{5,7},{6,4},{7,5},{8,10},{9,11},{10,... | collective-permute-start | bytes 1376264 | tf_op jit(solution)/shard_map/ppermute | solution.py:542
  50.0 12.8 %collective-permute-start.11 = (bf16[1792,128]{1,0:T(8,128)(2,1)S(1)}, bf16[1792,128]{1,0:T(8,128)(2,1)S(1)}, u32[]{:S(2)}, u32[]{:S(2)}) collective-permute-start(bf16[1792,128]{1,0:T(8,128)(2,1)S(1)} %get-tuple-element.94), channel_id=1, source_target_pairs={{0,8},{4,12},{8,0},{12,4},{16,24},{20,28},{24,16},{28,20},{1,9},{5... | collective-permute-start | bytes 1376264 | tf_op jit(solution)/shard_map/ppermute | solution.py:542
  52.7 10.9 %all-to-all-start.1 = ((bf16[8,16,512]{2,1,0:T(8,128)(2,1)}), bf16[8,16,512]{2,1,0:T(8,128)(2,1)S(1)}, u32[]{:S(2)}, u32[]{:S(2)}) async-start(bf16[8,16,512]{2,1,0:T(8,128)(2,1)} %bitcast.7), calls=%async_computation.1 | async-start | bytes 262144 | tf_op jit(solution)/shard_map/all_to_all | solution.py:648
  63.0 6.1 %collective-permute-start.14 = (bf16[896,128]{1,0:T(8,128)(2,1)S(1)}, bf16[896,128]{1,0:T(8,128)(2,1)S(1)}, u32[]{:S(2)}, u32[]{:S(2)}) collective-permute-start(bf16[896,128]{1,0:T(8,128)(2,1)S(1)} %get-tuple-element.96), channel_id=1, source_target_pairs={{0,2},{1,3},{2,0},{3,1},{4,6},{5,7},{6,4},{7,5},{8,10},{9,11},{10,... | collective-permute-start | bytes 688136 | tf_op jit(solution)/shard_map/ppermute | solution.py:542
  63.6 6.9 %collective-permute-start.12 = (bf16[896,128]{1,0:T(8,128)(2,1)S(1)}, bf16[896,128]{1,0:T(8,128)(2,1)S(1)}, u32[]{:S(2)}, u32[]{:S(2)}) collective-permute-start(bf16[896,128]{1,0:T(8,128)(2,1)S(1)} %get-tuple-element.99), channel_id=1, source_target_pairs={{0,4},{4,0},{8,12},{12,8},{16,20},{20,16},{24,28},{28,24},{1,5},{5... | collective-permute-start | bytes 688136 | tf_op jit(solution)/shard_map/ppermute | solution.py:542
  69.1 4.9 %collective-permute-start.15 = (bf16[448,128]{1,0:T(8,128)(2,1)S(1)}, bf16[448,128]{1,0:T(8,128)(2,1)S(1)}, u32[]{:S(2)}, u32[]{:S(2)}) collective-permute-start(bf16[448,128]{1,0:T(8,128)(2,1)S(1)} %add_convert_fusion.9), channel_id=1, source_target_pairs={{0,4},{4,0},{8,12},{12,8},{16,20},{20,16},{24,28},{28,24},{1,5},{5... | collective-permute-start | bytes 344072 | tf_op jit(solution)/shard_map/ppermute | solution.py:542
  70.5 5.7 %collective-permute-start.13 = (bf16[448,128]{1,0:T(8,128)(2,1)S(1)}, bf16[448,128]{1,0:T(8,128)(2,1)S(1)}, u32[]{:S(2)}, u32[]{:S(2)}) collective-permute-start(bf16[448,128]{1,0:T(8,128)(2,1)S(1)} %add_convert_fusion.11), channel_id=1, source_target_pairs={{0,8},{4,12},{8,0},{12,4},{16,24},{20,28},{24,16},{28,20},{1,9},{5... | collective-permute-start | bytes 344072 | tf_op jit(solution)/shard_map/ppermute | solution.py:542
  76.3 6.0 %collective-permute-start.16 = (bf16[448,128]{1,0:T(8,128)(2,1)S(1)}, bf16[448,128]{1,0:T(8,128)(2,1)S(1)}, u32[]{:S(2)}, u32[]{:S(2)}) collective-permute-start(bf16[448,128]{1,0:T(8,128)(2,1)S(1)} %select_convert_fusion), channel_id=1, source_target_pairs={{0,16},{4,20},{8,24},{12,28},{16,0},{20,4},{24,8},{28,12},{1,17},{... | collective-permute-start | bytes 344072 | tf_op jit(solution)/shard_map/ppermute | solution.py:542

commit v4 on v2

--- a/solution.py
+++ b/solution.py
@@ -752,9 +752,9 @@
             for whole in (keep, got[:span])
         ]
         parts.append(Exchange([v.reshape(span, width) for v in values], span, order, False))
-    sent = parts[0].cut(leaving)
+    sent = parts[0].cut()
     parts[0].send()
-    sent = parts[1].cut(sent, back_first, back_second, across)
+    sent = parts[1].cut(sent, back_first, back_second)
     parts[1].send()
     total = own + got_upper[span : span + sum_rows].astype(F32) + across.astype(F32)
     stay, slot_grad = call(

time: 83.8 us -> 83.8 us (level)
  waiting for transfers between devices: 33.7 us -> 32.4 us
  starting transfers between devices: 19.2 us -> 20.5 us
    ppermute x13, waiting for transfers between devices: 25.4 us -> 18.9 us  [flip(): return lax.ppermute(values, axis, [(i, i ^ mask) for i in range(count)])]
    all_to_all x2, waiting for transfers between devices: 4.98 us -> 9.56 us  [exchange(): lax.all_to_all(blocks, 'dom', split_axis=0, concat_axis=0, tiled=True)]
    ppermute x13, starting transfers between devices: 4.67 us -> 5.74 us  [flip(): return lax.ppermute(values, axis, [(i, i ^ mask) for i in range(count)])]
  transfers between devices with their start and end apart: 19 -> 19, of which waited for: 13 -> 11; matrix products, arithmetic and copies ran while one was open for 5% -> 5% of each run, Pallas kernels for 11% -> 11%
where the time goes in v4:
time: 83.8 us; the launch traced here: 83.3 us
  waiting for transfers between devices  32.4 us (39%)
  Pallas kernels  24.2 us (29%)
  starting transfers between devices  20.5 us (24%)
  other arithmetic  3.06 us (4%)
  local copies, waits for them, and re-layouts  2.29 us (3%)
    pallas_call x7, Pallas kernels, call(): pl.pallas_call(kernel, out_shape=[array.array if isinstance(array, Kept)...  24.2 us
    ppermute x13, waiting for transfers between devices, flip(): return lax.ppermute(values, axis, [(i, i ^ mask) for i in range(count)])  18.9 us
    all_to_all x2, starting transfers between devices, exchange(): lax.all_to_all(blocks, 'dom', split_axis=0, concat_axis=0, tiled=True)  10.9 us
    all_to_all x2, waiting for transfers between devices, exchange(): lax.all_to_all(blocks, 'dom', split_axis=0, concat_axis=0, tiled=True)  9.56 us
    ppermute x13, starting transfers between devices, flip(): return lax.ppermute(values, axis, [(i, i ^ mask) for i in range(count)])  5.74 us
    ppermute x4, waiting for transfers between devices, meet(): return lax.ppermute(values, axis, pairs)  3.98 us
    ppermute x4, starting transfers between devices, meet(): return lax.ppermute(values, axis, pairs)  3.85 us
    optimization_barrier x1, local copies, waits for them, and re-layouts, after(): return lax.optimization_barrier((values, others))[0]  2.29 us
  transfers between devices with their start and end apart: 19, of which 11 were waited for; matrix products, arithmetic and copies ran while one was open for 5% of the time, Pallas kernels for 11%

profile of v4, /device:TPU:0, one launch (start us, length us, event | category | flops | bytes accessed | tf_op | source)
XLA Modules:
  0.0 83.3 jit_solution(17361330525822691023)
XLA Ops:
  0.6 1.8 %pick.1 = (bf16[128,512]{1,0:T(8,128)(2,1)}, s32[1,128]{1,0:T(1,128)S(1)}) custom-call(s32[1,128]{1,0:T(1,128)} %pick_hbm.1, bf16[128,512]{1,0:T(8,128)(2,1)} %tile_hbm.3), custom_call_target="tpu_custom_call" | custom-call | tf_op jit(solution)/shard_map/pick/pallas_call | solution.py:97
  2.5 7.3 %all-to-all-start = ((bf16[8,16,512]{2,1,0:T(8,128)(2,1)}), bf16[8,16,512]{2,1,0:T(8,128)(2,1)S(1)}, u32[]{:S(2)}, u32[]{:S(2)}) async-start(bf16[8,16,512]{2,1,0:T(8,128)(2,1)} %bitcast.4), calls=%async_computation | async-start | bytes 262144 | tf_op jit(solution)/shard_map/all_to_all | solution.py:648
  9.8 2.3 %copy.18 = bf16[768,512]{0,1:T(8,128)(2,1)} copy(bf16[768,512]{1,0:T(8,128)(2,1)} %edge_hbm.3) | data formatting | bytes 1572864 | tf_op jit(solution)/shard_map/optimization_barrier | solution.py:562
  12.0 0.1 pad_add_fusion.where_ref
  12.1 5.0 %all-to-all-done = bf16[8,16,512]{2,1,0:T(8,128)(2,1)S(1)} async-done(((bf16[8,16,512]{2,1,0:T(8,128)(2,1)}), bf16[8,16,512]{2,1,0:T(8,128)(2,1)S(1)}, u32[]{:S(2)}, u32[]{:S(2)}) %all-to-all-start) | async-done | bytes 131104 | tf_op jit(solution)/shard_map/all_to_all | solution.py:648
  17.1 1.9 %pool.1 = (bf16[128,512]{1,0:T(8,128)(2,1)S(1)}, bf16[16,512]{1,0:T(8,128)(2,1)S(1)}, bf16[16,512]{1,0:T(8,128)(2,1)S(1)}, s32[1,128]{1,0:T(1,128)S(1)}, s32[1,32]{1,0:T(1,128)S(1)}) custom-call(s32[4]{0:T(128)S(1)} %pad_add_fusion.where_ref, s32[128]{0:T(128)} %from_hbm.1, s32[1,32]{1,0:T(1,128)} %cut_hbm.1, bf16[128,512]{1,0:T(8,128)(2,1)} %tile_hbm.3, ...), custom_call_target="tpu_custom_call" | custom-call | tf_op jit(solution)/shard_map/pool/pallas_call | solution.py:97
  19.0 1.6 %collective-permute-start.1 = (bf16[128,512]{1,0:T(8,128)(2,1)S(1)}, bf16[128,512]{1,0:T(8,128)(2,1)S(1)}, u32[]{:S(2)}, u32[]{:S(2)}) collective-permute-start(bf16[128,512]{1,0:T(8,128)(2,1)S(1)} %get-tuple-element.51.latent_ref), channel_id=1, source_target_pairs={{0,2},{1,3},{2,0},{3,1},{4,6},{5,7},{6,4},{7,5},{8,10},{9,11},{10,... | collective-permute-start | bytes 393224 | tf_op jit(solution)/shard_map/ppermute | solution.py:542
  20.6 0.2 collective-permute-start.2
  20.8 1.8 %collective-permute-start.3 = (bf16[16,512]{1,0:T(8,128)(2,1)S(1)}, bf16[16,512]{1,0:T(8,128)(2,1)S(1)}, u32[]{:S(2)}, u32[]{:S(2)}) collective-permute-start(bf16[16,512]{1,0:T(8,128)(2,1)S(1)} %get-tuple-element.53), channel_id=1, source_target_pairs={{0,28},{4,8},{8,4},{12,16},{16,12},{20,24},{24,20},{28,0},{1,29},{... | collective-permute-start | bytes 49160 | tf_op jit(solution)/shard_map/ppermute | solution.py:548
  22.6 0.0 collective-permute-start
  22.6 3.0 %base.1 = (f32[768,512]{1,0:T(8,128)S(1)}, bf16[512,512]{1,0:T(8,128)(2,1)S(1)}, bf16[512,512]{1,0:T(8,128)(2,1)S(1)}) custom-call(s32[768]{0:T(1024)} %receiver_hbm.5, bf16[768,512]{1,0:T(8,128)(2,1)} %edge_hbm.3, bf16[1536,512]{1,0:T(8,128)(2,1)} %w_hbm.1, bf16[512,512]{1,0:T(8,128)(2,1)} %edge_out_hbm.1, bf16[128,512]{1,0:T(8,128)(2,1)S(1)} %get-tuple-element.51.latent_ref), custom_call_target="tpu_custom_call" | custom-call | tf_op jit(solution)/shard_map/base/pallas_call | solution.py:97
  25.6 0.0 collective-permute-done.2.first_ref
  25.6 1.6 %collective-permute-done.3.second_ref = bf16[16,512]{1,0:T(8,128)(2,1)S(1)} collective-permute-done((bf16[16,512]{1,0:T(8,128)(2,1)S(1)}, bf16[16,512]{1,0:T(8,128)(2,1)S(1)}, u32[]{:S(2)}, u32[]{:S(2)}) %collective-permute-start.3) | collective-permute-done | bytes 16416 | tf_op jit(solution)/shard_map/ppermute | solution.py:548
  27.2 0.0 collective-permute-done.1.far_ref
  27.2 0.0 collective-permute-done.near_ref
  27.2 1.3 %collective-permute-done.4.cross_ref = bf16[128,512]{1,0:T(8,128)(2,1)S(1)} collective-permute-done((bf16[128,512]{1,0:T(8,128)(2,1)S(1)}, bf16[128,512]{1,0:T(8,128)(2,1)S(1)}, u32[]{:S(2)}, u32[]{:S(2)}) %collective-permute-start.4) | collective-permute-done | bytes 131104 | tf_op jit(solution)/shard_map/ppermute | solution.py:542
  28.6 11.6 %block.1 = (bf16[128,512]{1,0:T(8,128)(2,1)}, bf16[768,512]{1,0:T(8,128)(2,1)}, bf16[768,512]{1,0:T(8,128)(2,1)}, bf16[256,512]{1,0:T(8,128)(2,1)}, f32[128,512]...) custom-call(s32[4]{0:T(128)S(1)} %pad_add_fusion.where_ref, ...), custom_call_target="tpu_custom_call" | custom-call | tf_op jit(solution)/shard_map/block/pallas_call | solution.py:97
  40.1 0.2 collective-permute-start.6
  40.4 0.4 collective-permute-start.5
  40.7 0.0 collective-permute-start.7
  40.7 1.8 %collective-permute-start.8 = (bf16[16,512]{1,0:T(8,128)(2,1)S(1)}, bf16[16,512]{1,0:T(8,128)(2,1)S(1)}, u32[]{:S(2)}, u32[]{:S(2)}) collective-permute-start(bf16[16,512]{1,0:T(8,128)(2,1)S(1)} %get-tuple-element.71), channel_id=1, source_target_pairs={{0,28},{4,8},{8,4},{12,16},{16,12},{20,24},{24,20},{28,0},{1,29},{... | collective-permute-start | bytes 49160 | tf_op jit(solution)/shard_map/ppermute | solution.py:548
  42.5 0.7 collective-permute-done.6
  43.3 1.5 %add_convert_fusion.1 = (bf16[1792,128]{1,0:T(8,128)(2,1)S(1)}, bf16[1792,128]{1,0:T(8,128)(2,1)S(1)}) fusion(bf16[4608,128]{1,0:T(8,128)(2,1)S(1)} %collective-permute-done.6, bf16[3584,128]{1,0:T(8,128)(2,1)} %get-tuple-element.68), kind=kLoop, calls=%fused_computation.1 | loop fusion | flops 1835008 | bytes 2752512 | tf_op jit(solution)/shard_map/convert_element_type | solution.py:586
  44.7 0.1 collective-permute-start.10
  44.8 2.3 %collective-permute-done.8.second_ref = bf16[16,512]{1,0:T(8,128)(2,1)S(1)} collective-permute-done((bf16[16,512]{1,0:T(8,128)(2,1)S(1)}, bf16[16,512]{1,0:T(8,128)(2,1)S(1)}, u32[]{:S(2)}, u32[]{:S(2)}) %collective-permute-start.8) | collective-permute-done | bytes 16416 | tf_op jit(solution)/shard_map/ppermute | solution.py:548
  47.2 0.2 add_convert_fusion
  47.4 0.1 collective-permute-start.11
  47.5 0.6 collective-permute-start.9
  48.1 4.4 %collective-permute-done.9 = bf16[512,128]{1,0:T(8,128)(2,1)S(1)} collective-permute-done((bf16[512,128]{1,0:T(8,128)(2,1)S(1)}, bf16[512,128]{1,0:T(8,128)(2,1)S(1)}, u32[]{:S(2)}, u32[]{:S(2)}) %collective-permute-start.9) | collective-permute-done | bytes 131104 | tf_op jit(solution)/shard_map/ppermute | solution.py:542
  52.6 1.9 %node.1 = (bf16[128,512]{1,0:T(8,128)(2,1)S(1)}, bf16[128,512]{1,0:T(8,128)(2,1)}) custom-call(s32[4]{0:T(128)S(1)} %pad_add_fusion.where_ref, s32[1,128]{1,0:T(1,128)S(1)} %get-tuple-element.61.from_ref, s32[1,32]{1,0:T(1,128)S(1)} %get-tuple-element.62.cut_ref, bf16[512,512]{1,0:T(8,128)(2,1)S(1)} %get-tuple-element.56.w_send.w_send_ref, ...), custom_call_target="tpu_custom_call" | custom-call | tf_op jit(solution)/shard_map/node/pallas_call | solution.py:97
  54.5 3.6 %all-to-all-start.1 = ((bf16[8,16,512]{2,1,0:T(8,128)(2,1)}), bf16[8,16,512]{2,1,0:T(8,128)(2,1)S(1)}, u32[]{:S(2)}, u32[]{:S(2)}) async-start(bf16[8,16,512]{2,1,0:T(8,128)(2,1)} %bitcast.7), calls=%async_computation.1 | async-start | bytes 262144 | tf_op jit(solution)/shard_map/all_to_all | solution.py:648
  58.2 0.8 collective-permute-done.11
  59.0 0.2 add_convert_fusion.4
  59.2 1.3 %collective-permute-start.14 = (bf16[896,128]{1,0:T(8,128)(2,1)S(1)}, bf16[896,128]{1,0:T(8,128)(2,1)S(1)}, u32[]{:S(2)}, u32[]{:S(2)}) collective-permute-start(bf16[896,128]{1,0:T(8,128)(2,1)S(1)} %get-tuple-element.96), channel_id=1, source_target_pairs={{0,4},{4,0},{8,12},{12,8},{16,20},{20,16},{24,28},{28,24},{1,5},{5... | collective-permute-start | bytes 688136 | tf_op jit(solution)/shard_map/ppermute | solution.py:542
  60.5 0.5 collective-permute-start.12
  61.0 4.6 %all-to-all-done.1 = bf16[8,16,512]{2,1,0:T(8,128)(2,1)S(1)} async-done(((bf16[8,16,512]{2,1,0:T(8,128)(2,1)}), bf16[8,16,512]{2,1,0:T(8,128)(2,1)S(1)}, u32[]{:S(2)}, u32[]{:S(2)}) %all-to-all-start.1) | async-done | bytes 131104 | tf_op jit(solution)/shard_map/all_to_all | solution.py:648
  65.6 0.8 %back.1 = bf16[128,512]{1,0:T(8,128)(2,1)} custom-call(s32[1,128]{1,0:T(1,128)S(1)} %get-tuple-element.60.pick_ref, bf16[128,512]{1,0:T(8,128)(2,1)S(1)} %get-tuple-element.77.stay_ref, bf16[128,512]{1,0:T(8,128)(2,1)S(1)} %bitcast.10), custom_call_target="tpu_custom_call" | custom-call | tf_op jit(solution)/shard_map/back/pallas_call | solution.py:97
  66.5 3.2 %edge_grad.1 = bf16[768,512]{1,0:T(8,128)(2,1)} custom-call(s32[768]{0:T(1024)} %receiver_hbm.5, bf16[768,512]{1,0:T(8,128)(2,1)} %get-tuple-element.85.pre_grad_hbm, bf16[768,512]{1,0:T(8,128)(2,1)} %edge_cot_hbm.3, bf16[1536,512]{1,0:T(8,128)(2,1)} %w_hbm.1, bf16[256,512]{1,0:T(8,128)(2,1)} %get-tuple-element.86.agg_parts_hbm), custom_call_target="tpu_custom_call" | custom-call | tf_op jit(solution)/shard_map/edge_grad/pallas_call | solution.py:97
  69.7 0.0 collective-permute-done.14
  69.7 0.6 collective-permute-start.15
  70.3 0.0 collective-permute-done.12
  70.4 0.1 collective-permute-start.13
  70.4 4.1 %collective-permute-done.15 = bf16[448,128]{1,0:T(8,128)(2,1)S(1)} collective-permute-done((bf16[448,128]{1,0:T(8,128)(2,1)S(1)}, bf16[448,128]{1,0:T(8,128)(2,1)S(1)}, u32[]{:S(2)}, u32[]{:S(2)}) %collective-permute-start.15) | collective-permute-done | bytes 114720 | tf_op jit(solution)/shard_map/ppermute | solution.py:542
  74.6 1.8 %collective-permute-done.13 = bf16[448,128]{1,0:T(8,128)(2,1)S(1)} collective-permute-done((bf16[448,128]{1,0:T(8,128)(2,1)S(1)}, bf16[448,128]{1,0:T(8,128)(2,1)S(1)}, u32[]{:S(2)}, u32[]{:S(2)}) %collective-permute-start.13) | collective-permute-done | bytes 114720 | tf_op jit(solution)/shard_map/ppermute | solution.py:542
  76.3 0.1 select_convert_fusion
  76.4 0.4 collective-permute-start.16
  76.8 5.7 %collective-permute-done.16 = bf16[448,128]{1,0:T(8,128)(2,1)S(1)} collective-permute-done((bf16[448,128]{1,0:T(8,128)(2,1)S(1)}, bf16[448,128]{1,0:T(8,128)(2,1)S(1)}, u32[]{:S(2)}, u32[]{:S(2)}) %collective-permute-start.16) | collective-permute-done | bytes 114720 | tf_op jit(solution)/shard_map/ppermute | solution.py:542
  82.5 0.8 convert_add_fusion.1
  (10 shorter events, 0.2 us)
Async XLA Ops:
  2.5 14.6 %all-to-all-start = ((bf16[8,16,512]{2,1,0:T(8,128)(2,1)}), bf16[8,16,512]{2,1,0:T(8,128)(2,1)S(1)}, u32[]{:S(2)}, u32[]{:S(2)}) async-start(bf16[8,16,512]{2,1,0:T(8,128)(2,1)} %bitcast.4), calls=%async_computation | async-start | bytes 262144 | tf_op jit(solution)/shard_map/all_to_all | solution.py:648
  19.0 8.2 %collective-permute-start.1 = (bf16[128,512]{1,0:T(8,128)(2,1)S(1)}, bf16[128,512]{1,0:T(8,128)(2,1)S(1)}, u32[]{:S(2)}, u32[]{:S(2)}) collective-permute-start(bf16[128,512]{1,0:T(8,128)(2,1)S(1)} %get-tuple-element.51.latent_ref), channel_id=1, source_target_pairs={{0,2},{1,3},{2,0},{3,1},{4,6},{5,7},{6,4},{7,5},{8,10},{9,11},{10,... | collective-permute-start | bytes 393224 | tf_op jit(solution)/shard_map/ppermute | solution.py:542
  20.6 5.0 %collective-permute-start.2 = (bf16[16,512]{1,0:T(8,128)(2,1)S(1)}, bf16[16,512]{1,0:T(8,128)(2,1)S(1)}, u32[]{:S(2)}, u32[]{:S(2)}) collective-permute-start(bf16[16,512]{1,0:T(8,128)(2,1)S(1)} %get-tuple-element.52), channel_id=1, source_target_pairs={{0,4},{4,0},{8,12},{12,8},{16,20},{20,16},{24,28},{28,24},{1,5},{5... | collective-permute-start | bytes 49160 | tf_op jit(solution)/shard_map/ppermute | solution.py:548
  20.8 6.4 %collective-permute-start.3 = (bf16[16,512]{1,0:T(8,128)(2,1)S(1)}, bf16[16,512]{1,0:T(8,128)(2,1)S(1)}, u32[]{:S(2)}, u32[]{:S(2)}) collective-permute-start(bf16[16,512]{1,0:T(8,128)(2,1)S(1)} %get-tuple-element.53), channel_id=1, source_target_pairs={{0,28},{4,8},{8,4},{12,16},{16,12},{20,24},{24,20},{28,0},{1,29},{... | collective-permute-start | bytes 49160 | tf_op jit(solution)/shard_map/ppermute | solution.py:548
  22.6 4.6 %collective-permute-start = (bf16[128,512]{1,0:T(8,128)(2,1)S(1)}, bf16[128,512]{1,0:T(8,128)(2,1)S(1)}, u32[]{:S(2)}, u32[]{:S(2)}) collective-permute-start(bf16[128,512]{1,0:T(8,128)(2,1)S(1)} %get-tuple-element.51.latent_ref), channel_id=1, source_target_pairs={{0,1},{1,0},{2,3},{3,2},{4,5},{5,4},{6,7},{7,6},{8,9},{9,8},{10,11... | collective-permute-start | bytes 393224 | tf_op jit(solution)/shard_map/ppermute | solution.py:542
  27.2 1.3 %collective-permute-start.4 = (bf16[128,512]{1,0:T(8,128)(2,1)S(1)}, bf16[128,512]{1,0:T(8,128)(2,1)S(1)}, u32[]{:S(2)}, u32[]{:S(2)}) collective-permute-start(bf16[128,512]{1,0:T(8,128)(2,1)S(1)} %collective-permute-done.1.far_ref), channel_id=1, source_target_pairs={{0,1},{1,0},{2,3},{3,2},{4,5},{5,4},{6,7},{7,6},{8,9},{9,8},{10,11... | collective-permute-start | bytes 393224 | tf_op jit(solution)/shard_map/ppermute | solution.py:542
  40.1 3.1 %collective-permute-start.6 = (bf16[4608,128]{1,0:T(8,128)(2,1)}, bf16[4608,128]{1,0:T(8,128)(2,1)S(1)}, u32[]{:S(2)}, u32[]{:S(2)}) collective-permute-start(bf16[4608,128]{1,0:T(8,128)(2,1)} %get-tuple-element.67), channel_id=1, source_target_pairs={{0,1},{1,0},{2,3},{3,2},{4,5},{5,4},{6,7},{7,6},{8,9},{9,8},{10,11... | collective-permute-start | bytes 3538952 | tf_op jit(solution)/shard_map/ppermute | solution.py:542
  40.4 6.8 %collective-permute-start.5 = (bf16[3584,128]{1,0:T(8,128)(2,1)}, bf16[3584,128]{1,0:T(8,128)(2,1)S(1)}, u32[]{:S(2)}, u32[]{:S(2)}) collective-permute-start(bf16[3584,128]{1,0:T(8,128)(2,1)} %get-tuple-element.65), channel_id=1, source_target_pairs={{0,1},{1,0},{2,3},{3,2},{4,5},{5,4},{6,7},{7,6},{8,9},{9,8},{10,11... | collective-permute-start | bytes 2752520 | tf_op jit(solution)/shard_map/ppermute | solution.py:542
  40.7 4.1 %collective-permute-start.7 = (bf16[16,512]{1,0:T(8,128)(2,1)S(1)}, bf16[16,512]{1,0:T(8,128)(2,1)S(1)}, u32[]{:S(2)}, u32[]{:S(2)}) collective-permute-start(bf16[16,512]{1,0:T(8,128)(2,1)S(1)} %get-tuple-element.70), channel_id=1, source_target_pairs={{0,4},{4,0},{8,12},{12,8},{16,20},{20,16},{24,28},{28,24},{1,5},{5... | collective-permute-start | bytes 49160 | tf_op jit(solution)/shard_map/ppermute | solution.py:548
  40.7 6.4 %collective-permute-start.8 = (bf16[16,512]{1,0:T(8,128)(2,1)S(1)}, bf16[16,512]{1,0:T(8,128)(2,1)S(1)}, u32[]{:S(2)}, u32[]{:S(2)}) collective-permute-start(bf16[16,512]{1,0:T(8,128)(2,1)S(1)} %get-tuple-element.71), channel_id=1, source_target_pairs={{0,28},{4,8},{8,4},{12,16},{16,12},{20,24},{24,20},{28,0},{1,29},{... | collective-permute-start | bytes 49160 | tf_op jit(solution)/shard_map/ppermute | solution.py:548
  43.3 3.9 %copy-start = (bf16[3584,128]{1,0:T(8,128)(2,1)S(1)}, bf16[3584,128]{1,0:T(8,128)(2,1)}, u32[]{:S(2)}) copy-start(bf16[3584,128]{1,0:T(8,128)(2,1)} %get-tuple-element.72) | copy-start | bytes 2752516
  44.7 14.2 %collective-permute-start.10 = (bf16[1792,128]{1,0:T(8,128)(2,1)S(1)}, bf16[1792,128]{1,0:T(8,128)(2,1)S(1)}, u32[]{:S(2)}, u32[]{:S(2)}) collective-permute-start(bf16[1792,128]{1,0:T(8,128)(2,1)S(1)} %get-tuple-element.92), channel_id=1, source_target_pairs={{0,4},{4,0},{8,12},{12,8},{16,20},{20,16},{24,28},{28,24},{1,5},{5... | collective-permute-start | bytes 1376264 | tf_op jit(solution)/shard_map/ppermute | solution.py:542
  47.4 11.5 %collective-permute-start.11 = (bf16[1792,128]{1,0:T(8,128)(2,1)S(1)}, bf16[1792,128]{1,0:T(8,128)(2,1)S(1)}, u32[]{:S(2)}, u32[]{:S(2)}) collective-permute-start(bf16[1792,128]{1,0:T(8,128)(2,1)S(1)} %get-tuple-element.94), channel_id=1, source_target_pairs={{0,8},{4,12},{8,0},{12,4},{16,24},{20,28},{24,16},{28,20},{1,9},{5... | collective-permute-start | bytes 1376264 | tf_op jit(solution)/shard_map/ppermute | solution.py:542
  47.5 5.0 %collective-permute-start.9 = (bf16[512,128]{1,0:T(8,128)(2,1)S(1)}, bf16[512,128]{1,0:T(8,128)(2,1)S(1)}, u32[]{:S(2)}, u32[]{:S(2)}) collective-permute-start(bf16[512,128]{1,0:T(8,128)(2,1)S(1)} %add_convert_fusion.8), channel_id=1, source_target_pairs={{0,2},{1,3},{2,0},{3,1},{4,6},{5,7},{6,4},{7,5},{8,10},{9,11},{10,... | collective-permute-start | bytes 393224 | tf_op jit(solution)/shard_map/ppermute | solution.py:542
  54.5 11.1 %all-to-all-start.1 = ((bf16[8,16,512]{2,1,0:T(8,128)(2,1)}), bf16[8,16,512]{2,1,0:T(8,128)(2,1)S(1)}, u32[]{:S(2)}, u32[]{:S(2)}) async-start(bf16[8,16,512]{2,1,0:T(8,128)(2,1)} %bitcast.7), calls=%async_computation.1 | async-start | bytes 262144 | tf_op jit(solution)/shard_map/all_to_all | solution.py:648
  59.2 10.5 %collective-permute-start.14 = (bf16[896,128]{1,0:T(8,128)(2,1)S(1)}, bf16[896,128]{1,0:T(8,128)(2,1)S(1)}, u32[]{:S(2)}, u32[]{:S(2)}) collective-permute-start(bf16[896,128]{1,0:T(8,128)(2,1)S(1)} %get-tuple-element.96), channel_id=1, source_target_pairs={{0,4},{4,0},{8,12},{12,8},{16,20},{20,16},{24,28},{28,24},{1,5},{5... | collective-permute-start | bytes 688136 | tf_op jit(solution)/shard_map/ppermute | solution.py:542
  60.5 9.8 %collective-permute-start.12 = (bf16[896,128]{1,0:T(8,128)(2,1)S(1)}, bf16[896,128]{1,0:T(8,128)(2,1)S(1)}, u32[]{:S(2)}, u32[]{:S(2)}) collective-permute-start(bf16[896,128]{1,0:T(8,128)(2,1)S(1)} %get-tuple-element.99), channel_id=1, source_target_pairs={{0,2},{1,3},{2,0},{3,1},{4,6},{5,7},{6,4},{7,5},{8,10},{9,11},{10,... | collective-permute-start | bytes 688136 | tf_op jit(solution)/shard_map/ppermute | solution.py:542
  69.7 4.9 %collective-permute-start.15 = (bf16[448,128]{1,0:T(8,128)(2,1)S(1)}, bf16[448,128]{1,0:T(8,128)(2,1)S(1)}, u32[]{:S(2)}, u32[]{:S(2)}) collective-permute-start(bf16[448,128]{1,0:T(8,128)(2,1)S(1)} %add_convert_fusion.9), channel_id=1, source_target_pairs={{0,2},{1,3},{2,0},{3,1},{4,6},{5,7},{6,4},{7,5},{8,10},{9,11},{10,... | collective-permute-start | bytes 344072 | tf_op jit(solution)/shard_map/ppermute | solution.py:542
  70.4 6.0 %collective-permute-start.13 = (bf16[448,128]{1,0:T(8,128)(2,1)S(1)}, bf16[448,128]{1,0:T(8,128)(2,1)S(1)}, u32[]{:S(2)}, u32[]{:S(2)}) collective-permute-start(bf16[448,128]{1,0:T(8,128)(2,1)S(1)} %add_convert_fusion.11), channel_id=1, source_target_pairs={{0,8},{4,12},{8,0},{12,4},{16,24},{20,28},{24,16},{28,20},{1,9},{5... | collective-permute-start | bytes 344072 | tf_op jit(solution)/shard_map/ppermute | solution.py:542
  76.4 6.0 %collective-permute-start.16 = (bf16[448,128]{1,0:T(8,128)(2,1)S(1)}, bf16[448,128]{1,0:T(8,128)(2,1)S(1)}, u32[]{:S(2)}, u32[]{:S(2)}) collective-permute-start(bf16[448,128]{1,0:T(8,128)(2,1)S(1)} %select_convert_fusion), channel_id=1, source_target_pairs={{0,16},{4,20},{8,24},{12,28},{16,0},{20,4},{24,8},{28,12},{1,17},{... | collective-permute-start | bytes 344072 | tf_op jit(solution)/shard_map/ppermute | solution.py:542

commit v5 on v4

--- a/solution.py
+++ b/solution.py
@@ -778,20 +778,22 @@
         [node_bf16, 1],
         limit=SMALL_LIMIT,
     )
+    first = latent_grad
+    while parts[0].order:
+        sent = cut_all(parts, first)
+        send_all(parts)
+        first = ()
     [edge_grad] = call(
         edge_grad_kernel,
         "edge_grad",
         [edge_bf16],
-        [edge_receiver, after(pre_grad, latent_grad), edge_cot, edge_in, agg_parts],
+        [edge_receiver, after(pre_grad, *sent), edge_cot, edge_in, agg_parts],
         [edge_index, edge_bf16, edge_bf16, square, sds((2 * nodes, feat), BF16)]
         + [edge_f32, edge_bf16, 5, edges // ROWS],
         limit=2 * SMALL_LIMIT,
     )
-    first = edge_grad
-    while parts[0].order:
-        cut_all(parts, first)
-        send_all(parts)
-        first = ()
+    for part in parts:
+        part.values = after(part.values, edge_grad)
     top = axis_bits("dom")[-1][1]
     upper = (lax.axis_index("dom") >> top) & 1
     above, below = [part.total() for part in parts]

time: 83.8 us -> 80.4 us (0.959)
  waiting for transfers between devices: 32.4 us -> 25.2 us
  starting transfers between devices: 20.5 us -> 24.4 us
    ppermute x13, waiting for transfers between devices: 18.9 us -> 11.6 us  [flip(): return lax.ppermute(values, axis, [(i, i ^ mask) for i in range(count)])]
    ppermute x13, starting transfers between devices: 5.74 us -> 9.6 us  [flip(): return lax.ppermute(values, axis, [(i, i ^ mask) for i in range(count)])]
  transfers between devices with their start and end apart: 19 -> 19, of which waited for: 11 -> 10; matrix products, arithmetic and copies ran while one was open for 5% -> 6% of each run, Pallas kernels for 11% -> 11%
where the time goes in v5:
time: 80.4 us; the launch traced here: 79.9 us
  waiting for transfers between devices  25.2 us (31%)
  starting transfers between devices  24.4 us (30%)
  Pallas kernels  24.2 us (30%)
  other arithmetic  3.07 us (4%)
  local copies, waits for them, and re-layouts  2.29 us (3%)
    pallas_call x7, Pallas kernels, call(): pl.pallas_call(kernel, out_shape=[array.array if isinstance(array, Kept)...  24.2 us
    ppermute x13, waiting for transfers between devices, flip(): return lax.ppermute(values, axis, [(i, i ^ mask) for i in range(count)])  11.6 us
    all_to_all x2, starting transfers between devices, exchange(): lax.all_to_all(blocks, 'dom', split_axis=0, concat_axis=0, tiled=True)  10.9 us
    ppermute x13, starting transfers between devices, flip(): return lax.ppermute(values, axis, [(i, i ^ mask) for i in range(count)])  9.6 us
    all_to_all x2, waiting for transfers between devices, exchange(): lax.all_to_all(blocks, 'dom', split_axis=0, concat_axis=0, tiled=True)  9.56 us
    ppermute x4, waiting for transfers between devices, meet(): return lax.ppermute(values, axis, pairs)  3.98 us
    ppermute x4, starting transfers between devices, meet(): return lax.ppermute(values, axis, pairs)  3.85 us
    optimization_barrier x1, local copies, waits for them, and re-layouts, after(): return lax.optimization_barrier((values, others))[0]  2.29 us
  transfers between devices with their start and end apart: 19, of which 10 were waited for; matrix products, arithmetic and copies ran while one was open for 6% of the time, Pallas kernels for 11%

profile of v5, /device:TPU:0, one launch (start us, length us, event | category | flops | bytes accessed | tf_op | source)
XLA Modules:
  0.0 79.9 jit_solution(4577429144278284739)
XLA Ops:
  0.6 1.8 %pick.1 = (bf16[128,512]{1,0:T(8,128)(2,1)}, s32[1,128]{1,0:T(1,128)S(1)}) custom-call(s32[1,128]{1,0:T(1,128)} %pick_hbm.1, bf16[128,512]{1,0:T(8,128)(2,1)} %tile_hbm.3), custom_call_target="tpu_custom_call" | custom-call | tf_op jit(solution)/shard_map/pick/pallas_call | solution.py:97
  2.5 7.3 %all-to-all-start = ((bf16[8,16,512]{2,1,0:T(8,128)(2,1)}), bf16[8,16,512]{2,1,0:T(8,128)(2,1)S(1)}, u32[]{:S(2)}, u32[]{:S(2)}) async-start(bf16[8,16,512]{2,1,0:T(8,128)(2,1)} %bitcast.4), calls=%async_computation | async-start | bytes 262144 | tf_op jit(solution)/shard_map/all_to_all | solution.py:648
  9.8 2.3 %copy.18 = bf16[768,512]{0,1:T(8,128)(2,1)} copy(bf16[768,512]{1,0:T(8,128)(2,1)} %edge_hbm.3) | data formatting | bytes 1572864 | tf_op jit(solution)/shard_map/optimization_barrier | solution.py:562
  12.0 0.1 pad_add_fusion.where_ref
  12.1 5.0 %all-to-all-done = bf16[8,16,512]{2,1,0:T(8,128)(2,1)S(1)} async-done(((bf16[8,16,512]{2,1,0:T(8,128)(2,1)}), bf16[8,16,512]{2,1,0:T(8,128)(2,1)S(1)}, u32[]{:S(2)}, u32[]{:S(2)}) %all-to-all-start) | async-done | bytes 131104 | tf_op jit(solution)/shard_map/all_to_all | solution.py:648
  17.1 1.9 %pool.1 = (bf16[128,512]{1,0:T(8,128)(2,1)S(1)}, bf16[16,512]{1,0:T(8,128)(2,1)S(1)}, bf16[16,512]{1,0:T(8,128)(2,1)S(1)}, s32[1,128]{1,0:T(1,128)S(1)}, s32[1,32]{1,0:T(1,128)S(1)}) custom-call(s32[4]{0:T(128)S(1)} %pad_add_fusion.where_ref, s32[128]{0:T(128)} %from_hbm.1, s32[1,32]{1,0:T(1,128)} %cut_hbm.1, bf16[128,512]{1,0:T(8,128)(2,1)} %tile_hbm.3, ...), custom_call_target="tpu_custom_call" | custom-call | tf_op jit(solution)/shard_map/pool/pallas_call | solution.py:97
  19.0 1.6 %collective-permute-start.1 = (bf16[128,512]{1,0:T(8,128)(2,1)S(1)}, bf16[128,512]{1,0:T(8,128)(2,1)S(1)}, u32[]{:S(2)}, u32[]{:S(2)}) collective-permute-start(bf16[128,512]{1,0:T(8,128)(2,1)S(1)} %get-tuple-element.55.latent_ref), channel_id=1, source_target_pairs={{0,2},{1,3},{2,0},{3,1},{4,6},{5,7},{6,4},{7,5},{8,10},{9,11},{10,... | collective-permute-start | bytes 393224 | tf_op jit(solution)/shard_map/ppermute | solution.py:542
  20.6 0.2 collective-permute-start.2
  20.8 1.8 %collective-permute-start.3 = (bf16[16,512]{1,0:T(8,128)(2,1)S(1)}, bf16[16,512]{1,0:T(8,128)(2,1)S(1)}, u32[]{:S(2)}, u32[]{:S(2)}) collective-permute-start(bf16[16,512]{1,0:T(8,128)(2,1)S(1)} %get-tuple-element.57), channel_id=1, source_target_pairs={{0,28},{4,8},{8,4},{12,16},{16,12},{20,24},{24,20},{28,0},{1,29},{... | collective-permute-start | bytes 49160 | tf_op jit(solution)/shard_map/ppermute | solution.py:548
  22.6 0.0 collective-permute-start
  22.6 3.0 %base.1 = (f32[768,512]{1,0:T(8,128)S(1)}, bf16[512,512]{1,0:T(8,128)(2,1)S(1)}, bf16[512,512]{1,0:T(8,128)(2,1)S(1)}) custom-call(s32[768]{0:T(1024)} %receiver_hbm.5, bf16[768,512]{1,0:T(8,128)(2,1)} %edge_hbm.3, bf16[1536,512]{1,0:T(8,128)(2,1)} %w_hbm.1, bf16[512,512]{1,0:T(8,128)(2,1)} %edge_out_hbm.1, bf16[128,512]{1,0:T(8,128)(2,1)S(1)} %get-tuple-element.55.latent_ref), custom_call_target="tpu_custom_call" | custom-call | tf_op jit(solution)/shard_map/base/pallas_call | solution.py:97
  25.6 1.6 %collective-permute-done.3.second_ref = bf16[16,512]{1,0:T(8,128)(2,1)S(1)} collective-permute-done((bf16[16,512]{1,0:T(8,128)(2,1)S(1)}, bf16[16,512]{1,0:T(8,128)(2,1)S(1)}, u32[]{:S(2)}, u32[]{:S(2)}) %collective-permute-start.3) | collective-permute-done | bytes 16416 | tf_op jit(solution)/shard_map/ppermute | solution.py:548
  27.2 0.0 collective-permute-start.4
  27.2 0.0 collective-permute-done.near_ref
  27.2 1.3 %collective-permute-done.4.cross_ref = bf16[128,512]{1,0:T(8,128)(2,1)S(1)} collective-permute-done((bf16[128,512]{1,0:T(8,128)(2,1)S(1)}, bf16[128,512]{1,0:T(8,128)(2,1)S(1)}, u32[]{:S(2)}, u32[]{:S(2)}) %collective-permute-start.4) | collective-permute-done | bytes 131104 | tf_op jit(solution)/shard_map/ppermute | solution.py:542
  28.6 11.6 %block.1 = (bf16[128,512]{1,0:T(8,128)(2,1)}, bf16[768,512]{1,0:T(8,128)(2,1)}, bf16[768,512]{1,0:T(8,128)(2,1)}, bf16[256,512]{1,0:T(8,128)(2,1)}, f32[128,512]...) custom-call(s32[4]{0:T(128)S(1)} %pad_add_fusion.where_ref, ...), custom_call_target="tpu_custom_call" | custom-call | tf_op jit(solution)/shard_map/block/pallas_call | solution.py:97
  40.1 0.2 collective-permute-start.6
  40.4 0.4 collective-permute-start.5
  40.7 0.0 collective-permute-start.7
  40.7 1.8 %collective-permute-start.8 = (bf16[16,512]{1,0:T(8,128)(2,1)S(1)}, bf16[16,512]{1,0:T(8,128)(2,1)S(1)}, u32[]{:S(2)}, u32[]{:S(2)}) collective-permute-start(bf16[16,512]{1,0:T(8,128)(2,1)S(1)} %get-tuple-element.75), channel_id=1, source_target_pairs={{0,28},{4,8},{8,4},{12,16},{16,12},{20,24},{24,20},{28,0},{1,29},{... | collective-permute-start | bytes 49160 | tf_op jit(solution)/shard_map/ppermute | solution.py:548
  42.5 0.7 collective-permute-done.6
  43.3 1.5 %add_convert_fusion.1 = (bf16[1792,128]{1,0:T(8,128)(2,1)S(1)}, bf16[1792,128]{1,0:T(8,128)(2,1)S(1)}) fusion(bf16[4608,128]{1,0:T(8,128)(2,1)S(1)} %collective-permute-done.6, bf16[3584,128]{1,0:T(8,128)(2,1)} %get-tuple-element.72), kind=kLoop, calls=%fused_computation.1 | loop fusion | flops 1835008 | bytes 2752512 | tf_op jit(solution)/shard_map/convert_element_type | solution.py:586
  44.8 0.1 collective-permute-start.10
  44.8 0.0 collective-permute-done.7.first_ref
  44.8 2.3 %collective-permute-done.8.second_ref = bf16[16,512]{1,0:T(8,128)(2,1)S(1)} collective-permute-done((bf16[16,512]{1,0:T(8,128)(2,1)S(1)}, bf16[16,512]{1,0:T(8,128)(2,1)S(1)}, u32[]{:S(2)}, u32[]{:S(2)}) %collective-permute-start.8) | collective-permute-done | bytes 16416 | tf_op jit(solution)/shard_map/ppermute | solution.py:548
  47.2 0.0 collective-permute-done.5
  47.2 0.2 add_convert_fusion
  47.4 0.1 collective-permute-start.11
  47.6 0.6 collective-permute-start.9
  48.2 4.4 %collective-permute-done.9 = bf16[512,128]{1,0:T(8,128)(2,1)S(1)} collective-permute-done((bf16[512,128]{1,0:T(8,128)(2,1)S(1)}, bf16[512,128]{1,0:T(8,128)(2,1)S(1)}, u32[]{:S(2)}, u32[]{:S(2)}) %collective-permute-start.9) | collective-permute-done | bytes 131104 | tf_op jit(solution)/shard_map/ppermute | solution.py:542
  52.6 1.9 %node.1 = (bf16[128,512]{1,0:T(8,128)(2,1)S(1)}, bf16[128,512]{1,0:T(8,128)(2,1)}) custom-call(s32[4]{0:T(128)S(1)} %pad_add_fusion.where_ref, s32[1,128]{1,0:T(1,128)S(1)} %get-tuple-element.65.from_ref, s32[1,32]{1,0:T(1,128)S(1)} %get-tuple-element.66.cut_ref, bf16[512,512]{1,0:T(8,128)(2,1)S(1)} %get-tuple-element.60.w_send.w_send_ref, ...), custom_call_target="tpu_custom_call" | custom-call | tf_op jit(solution)/shard_map/node/pallas_call | solution.py:97
  54.5 3.6 %all-to-all-start.1 = ((bf16[8,16,512]{2,1,0:T(8,128)(2,1)}), bf16[8,16,512]{2,1,0:T(8,128)(2,1)S(1)}, u32[]{:S(2)}, u32[]{:S(2)}) async-start(bf16[8,16,512]{2,1,0:T(8,128)(2,1)} %bitcast.7), calls=%async_computation.1 | async-start | bytes 262144 | tf_op jit(solution)/shard_map/all_to_all | solution.py:648
  58.2 0.8 %collective-permute-done.11 = bf16[1792,128]{1,0:T(8,128)(2,1)S(1)} collective-permute-done((bf16[1792,128]{1,0:T(8,128)(2,1)S(1)}, bf16[1792,128]{1,0:T(8,128)(2,1)S(1)}, u32[]{:S(2)}, u32[]{:S(2)}) %collective-permute-start.11) | collective-permute-done | bytes 458784 | tf_op jit(solution)/shard_map/ppermute | solution.py:542
  59.0 0.2 add_convert_fusion.4
  59.2 1.3 %collective-permute-start.13 = (bf16[896,128]{1,0:T(8,128)(2,1)S(1)}, bf16[896,128]{1,0:T(8,128)(2,1)S(1)}, u32[]{:S(2)}, u32[]{:S(2)}) collective-permute-start(bf16[896,128]{1,0:T(8,128)(2,1)S(1)} %get-tuple-element.104), channel_id=1, source_target_pairs={{0,4},{4,0},{8,12},{12,8},{16,20},{20,16},{24,28},{28,24},{1,5},{5... | collective-permute-start | bytes 688136 | tf_op jit(solution)/shard_map/ppermute | solution.py:542
  60.5 0.5 collective-permute-start.12
  61.0 4.6 %all-to-all-done.1 = bf16[8,16,512]{2,1,0:T(8,128)(2,1)S(1)} async-done(((bf16[8,16,512]{2,1,0:T(8,128)(2,1)}), bf16[8,16,512]{2,1,0:T(8,128)(2,1)S(1)}, u32[]{:S(2)}, u32[]{:S(2)}) %all-to-all-start.1) | async-done | bytes 131104 | tf_op jit(solution)/shard_map/all_to_all | solution.py:648
  65.6 0.8 %back.1 = bf16[128,512]{1,0:T(8,128)(2,1)} custom-call(s32[1,128]{1,0:T(1,128)S(1)} %get-tuple-element.64.pick_ref, bf16[128,512]{1,0:T(8,128)(2,1)S(1)} %get-tuple-element.81.stay_ref, bf16[128,512]{1,0:T(8,128)(2,1)S(1)} %bitcast.10), custom_call_target="tpu_custom_call" | custom-call | tf_op jit(solution)/shard_map/back/pallas_call | solution.py:97
  66.5 0.1 add_convert_fusion.9
  66.5 0.6 collective-permute-start.15
  67.1 0.1 add_convert_fusion.10
  67.2 2.1 %collective-permute-start.14 = (bf16[448,128]{1,0:T(8,128)(2,1)S(1)}, bf16[448,128]{1,0:T(8,128)(2,1)S(1)}, u32[]{:S(2)}, u32[]{:S(2)}) collective-permute-start(bf16[448,128]{1,0:T(8,128)(2,1)S(1)} %get-tuple-element.110), channel_id=1, source_target_pairs={{0,8},{4,12},{8,0},{12,4},{16,24},{20,28},{24,16},{28,20},{1,9},{5... | collective-permute-start | bytes 344072 | tf_op jit(solution)/shard_map/ppermute | solution.py:542
  69.4 3.2 %edge_grad.1 = bf16[768,512]{1,0:T(8,128)(2,1)} custom-call(s32[768]{0:T(1024)} %receiver_hbm.5, bf16[768,512]{1,0:T(8,128)(2,1)} %get-tuple-element.93.pre_grad_hbm, bf16[768,512]{1,0:T(8,128)(2,1)} %edge_cot_hbm.3, bf16[1536,512]{1,0:T(8,128)(2,1)} %w_hbm.1, bf16[256,512]{1,0:T(8,128)(2,1)} %get-tuple-element.94.agg_parts_hbm), custom_call_target="tpu_custom_call" | custom-call | tf_op jit(solution)/shard_map/edge_grad/pallas_call | solution.py:97
  72.6 0.7 collective-permute-done.14
  73.3 0.1 select_convert_fusion
  73.3 2.1 %collective-permute-start.16 = (bf16[448,128]{1,0:T(8,128)(2,1)S(1)}, bf16[448,128]{1,0:T(8,128)(2,1)S(1)}, u32[]{:S(2)}, u32[]{:S(2)}) collective-permute-start(bf16[448,128]{1,0:T(8,128)(2,1)S(1)} %select_convert_fusion), channel_id=1, source_target_pairs={{0,16},{4,20},{8,24},{12,28},{16,0},{20,4},{24,8},{28,12},{1,17},{... | collective-permute-start | bytes 344072 | tf_op jit(solution)/shard_map/ppermute | solution.py:542
  75.5 3.6 %collective-permute-done.16 = bf16[448,128]{1,0:T(8,128)(2,1)S(1)} collective-permute-done((bf16[448,128]{1,0:T(8,128)(2,1)S(1)}, bf16[448,128]{1,0:T(8,128)(2,1)S(1)}, u32[]{:S(2)}, u32[]{:S(2)}) %collective-permute-start.16) | collective-permute-done | bytes 114720 | tf_op jit(solution)/shard_map/ppermute | solution.py:542
  79.1 0.8 convert_add_fusion.1
  (10 shorter events, 0.1 us)
Async XLA Ops:
  2.5 14.6 %all-to-all-start = ((bf16[8,16,512]{2,1,0:T(8,128)(2,1)}), bf16[8,16,512]{2,1,0:T(8,128)(2,1)S(1)}, u32[]{:S(2)}, u32[]{:S(2)}) async-start(bf16[8,16,512]{2,1,0:T(8,128)(2,1)} %bitcast.4), calls=%async_computation | async-start | bytes 262144 | tf_op jit(solution)/shard_map/all_to_all | solution.py:648
  19.0 8.2 %collective-permute-start.1 = (bf16[128,512]{1,0:T(8,128)(2,1)S(1)}, bf16[128,512]{1,0:T(8,128)(2,1)S(1)}, u32[]{:S(2)}, u32[]{:S(2)}) collective-permute-start(bf16[128,512]{1,0:T(8,128)(2,1)S(1)} %get-tuple-element.55.latent_ref), channel_id=1, source_target_pairs={{0,2},{1,3},{2,0},{3,1},{4,6},{5,7},{6,4},{7,5},{8,10},{9,11},{10,... | collective-permute-start | bytes 393224 | tf_op jit(solution)/shard_map/ppermute | solution.py:542
  20.6 5.0 %collective-permute-start.2 = (bf16[16,512]{1,0:T(8,128)(2,1)S(1)}, bf16[16,512]{1,0:T(8,128)(2,1)S(1)}, u32[]{:S(2)}, u32[]{:S(2)}) collective-permute-start(bf16[16,512]{1,0:T(8,128)(2,1)S(1)} %get-tuple-element.56), channel_id=1, source_target_pairs={{0,4},{4,0},{8,12},{12,8},{16,20},{20,16},{24,28},{28,24},{1,5},{5... | collective-permute-start | bytes 49160 | tf_op jit(solution)/shard_map/ppermute | solution.py:548
  20.8 6.4 %collective-permute-start.3 = (bf16[16,512]{1,0:T(8,128)(2,1)S(1)}, bf16[16,512]{1,0:T(8,128)(2,1)S(1)}, u32[]{:S(2)}, u32[]{:S(2)}) collective-permute-start(bf16[16,512]{1,0:T(8,128)(2,1)S(1)} %get-tuple-element.57), channel_id=1, source_target_pairs={{0,28},{4,8},{8,4},{12,16},{16,12},{20,24},{24,20},{28,0},{1,29},{... | collective-permute-start | bytes 49160 | tf_op jit(solution)/shard_map/ppermute | solution.py:548
  22.6 4.6 %collective-permute-start = (bf16[128,512]{1,0:T(8,128)(2,1)S(1)}, bf16[128,512]{1,0:T(8,128)(2,1)S(1)}, u32[]{:S(2)}, u32[]{:S(2)}) collective-permute-start(bf16[128,512]{1,0:T(8,128)(2,1)S(1)} %get-tuple-element.55.latent_ref), channel_id=1, source_target_pairs={{0,1},{1,0},{2,3},{3,2},{4,5},{5,4},{6,7},{7,6},{8,9},{9,8},{10,11... | collective-permute-start | bytes 393224 | tf_op jit(solution)/shard_map/ppermute | solution.py:542
  27.2 1.3 %collective-permute-start.4 = (bf16[128,512]{1,0:T(8,128)(2,1)S(1)}, bf16[128,512]{1,0:T(8,128)(2,1)S(1)}, u32[]{:S(2)}, u32[]{:S(2)}) collective-permute-start(bf16[128,512]{1,0:T(8,128)(2,1)S(1)} %collective-permute-done.1.far_ref), channel_id=1, source_target_pairs={{0,1},{1,0},{2,3},{3,2},{4,5},{5,4},{6,7},{7,6},{8,9},{9,8},{10,11... | collective-permute-start | bytes 393224 | tf_op jit(solution)/shard_map/ppermute | solution.py:542
  40.1 3.1 %collective-permute-start.6 = (bf16[4608,128]{1,0:T(8,128)(2,1)}, bf16[4608,128]{1,0:T(8,128)(2,1)S(1)}, u32[]{:S(2)}, u32[]{:S(2)}) collective-permute-start(bf16[4608,128]{1,0:T(8,128)(2,1)} %get-tuple-element.71), channel_id=1, source_target_pairs={{0,1},{1,0},{2,3},{3,2},{4,5},{5,4},{6,7},{7,6},{8,9},{9,8},{10,11... | collective-permute-start | bytes 3538952 | tf_op jit(solution)/shard_map/ppermute | solution.py:542
  40.4 6.8 %collective-permute-start.5 = (bf16[3584,128]{1,0:T(8,128)(2,1)}, bf16[3584,128]{1,0:T(8,128)(2,1)S(1)}, u32[]{:S(2)}, u32[]{:S(2)}) collective-permute-start(bf16[3584,128]{1,0:T(8,128)(2,1)} %get-tuple-element.69), channel_id=1, source_target_pairs={{0,1},{1,0},{2,3},{3,2},{4,5},{5,4},{6,7},{7,6},{8,9},{9,8},{10,11... | collective-permute-start | bytes 2752520 | tf_op jit(solution)/shard_map/ppermute | solution.py:542
  40.7 4.1 %collective-permute-start.7 = (bf16[16,512]{1,0:T(8,128)(2,1)S(1)}, bf16[16,512]{1,0:T(8,128)(2,1)S(1)}, u32[]{:S(2)}, u32[]{:S(2)}) collective-permute-start(bf16[16,512]{1,0:T(8,128)(2,1)S(1)} %get-tuple-element.74), channel_id=1, source_target_pairs={{0,4},{4,0},{8,12},{12,8},{16,20},{20,16},{24,28},{28,24},{1,5},{5... | collective-permute-start | bytes 49160 | tf_op jit(solution)/shard_map/ppermute | solution.py:548
  40.7 6.4 %collective-permute-start.8 = (bf16[16,512]{1,0:T(8,128)(2,1)S(1)}, bf16[16,512]{1,0:T(8,128)(2,1)S(1)}, u32[]{:S(2)}, u32[]{:S(2)}) collective-permute-start(bf16[16,512]{1,0:T(8,128)(2,1)S(1)} %get-tuple-element.75), channel_id=1, source_target_pairs={{0,28},{4,8},{8,4},{12,16},{16,12},{20,24},{24,20},{28,0},{1,29},{... | collective-permute-start | bytes 49160 | tf_op jit(solution)/shard_map/ppermute | solution.py:548
  43.3 3.9 %copy-start = (bf16[3584,128]{1,0:T(8,128)(2,1)S(1)}, bf16[3584,128]{1,0:T(8,128)(2,1)}, u32[]{:S(2)}) copy-start(bf16[3584,128]{1,0:T(8,128)(2,1)} %get-tuple-element.76) | copy-start | bytes 2752516
  44.8 14.2 %collective-permute-start.10 = (bf16[1792,128]{1,0:T(8,128)(2,1)S(1)}, bf16[1792,128]{1,0:T(8,128)(2,1)S(1)}, u32[]{:S(2)}, u32[]{:S(2)}) collective-permute-start(bf16[1792,128]{1,0:T(8,128)(2,1)S(1)} %get-tuple-element.100), channel_id=1, source_target_pairs={{0,4},{4,0},{8,12},{12,8},{16,20},{20,16},{24,28},{28,24},{1,5},{5... | collective-permute-start | bytes 1376264 | tf_op jit(solution)/shard_map/ppermute | solution.py:542
  47.4 11.5 %collective-permute-start.11 = (bf16[1792,128]{1,0:T(8,128)(2,1)S(1)}, bf16[1792,128]{1,0:T(8,128)(2,1)S(1)}, u32[]{:S(2)}, u32[]{:S(2)}) collective-permute-start(bf16[1792,128]{1,0:T(8,128)(2,1)S(1)} %get-tuple-element.102), channel_id=1, source_target_pairs={{0,8},{4,12},{8,0},{12,4},{16,24},{20,28},{24,16},{28,20},{1,9},{5... | collective-permute-start | bytes 1376264 | tf_op jit(solution)/shard_map/ppermute | solution.py:542
  47.6 5.0 %collective-permute-start.9 = (bf16[512,128]{1,0:T(8,128)(2,1)S(1)}, bf16[512,128]{1,0:T(8,128)(2,1)S(1)}, u32[]{:S(2)}, u32[]{:S(2)}) collective-permute-start(bf16[512,128]{1,0:T(8,128)(2,1)S(1)} %add_convert_fusion.8), channel_id=1, source_target_pairs={{0,2},{1,3},{2,0},{3,1},{4,6},{5,7},{6,4},{7,5},{8,10},{9,11},{10,... | collective-permute-start | bytes 393224 | tf_op jit(solution)/shard_map/ppermute | solution.py:542
  54.5 11.1 %all-to-all-start.1 = ((bf16[8,16,512]{2,1,0:T(8,128)(2,1)}), bf16[8,16,512]{2,1,0:T(8,128)(2,1)S(1)}, u32[]{:S(2)}, u32[]{:S(2)}) async-start(bf16[8,16,512]{2,1,0:T(8,128)(2,1)} %bitcast.7), calls=%async_computation.1 | async-start | bytes 262144 | tf_op jit(solution)/shard_map/all_to_all | solution.py:648
  59.2 7.2 %collective-permute-start.13 = (bf16[896,128]{1,0:T(8,128)(2,1)S(1)}, bf16[896,128]{1,0:T(8,128)(2,1)S(1)}, u32[]{:S(2)}, u32[]{:S(2)}) collective-permute-start(bf16[896,128]{1,0:T(8,128)(2,1)S(1)} %get-tuple-element.104), channel_id=1, source_target_pairs={{0,4},{4,0},{8,12},{12,8},{16,20},{20,16},{24,28},{28,24},{1,5},{5... | collective-permute-start | bytes 688136 | tf_op jit(solution)/shard_map/ppermute | solution.py:542
  60.5 6.6 %collective-permute-start.12 = (bf16[896,128]{1,0:T(8,128)(2,1)S(1)}, bf16[896,128]{1,0:T(8,128)(2,1)S(1)}, u32[]{:S(2)}, u32[]{:S(2)}) collective-permute-start(bf16[896,128]{1,0:T(8,128)(2,1)S(1)} %get-tuple-element.111), channel_id=1, source_target_pairs={{0,2},{1,3},{2,0},{3,1},{4,6},{5,7},{6,4},{7,5},{8,10},{9,11},{10,... | collective-permute-start | bytes 688136 | tf_op jit(solution)/shard_map/ppermute | solution.py:542
  66.5 6.0 %collective-permute-start.15 = (bf16[448,128]{1,0:T(8,128)(2,1)S(1)}, bf16[448,128]{1,0:T(8,128)(2,1)S(1)}, u32[]{:S(2)}, u32[]{:S(2)}) collective-permute-start(bf16[448,128]{1,0:T(8,128)(2,1)S(1)} %get-tuple-element.108), channel_id=1, source_target_pairs={{0,2},{1,3},{2,0},{3,1},{4,6},{5,7},{6,4},{7,5},{8,10},{9,11},{10,... | collective-permute-start | bytes 344072 | tf_op jit(solution)/shard_map/ppermute | solution.py:542
  67.2 6.1 %collective-permute-start.14 = (bf16[448,128]{1,0:T(8,128)(2,1)S(1)}, bf16[448,128]{1,0:T(8,128)(2,1)S(1)}, u32[]{:S(2)}, u32[]{:S(2)}) collective-permute-start(bf16[448,128]{1,0:T(8,128)(2,1)S(1)} %get-tuple-element.110), channel_id=1, source_target_pairs={{0,8},{4,12},{8,0},{12,4},{16,24},{20,28},{24,16},{28,20},{1,9},{5... | collective-permute-start | bytes 344072 | tf_op jit(solution)/shard_map/ppermute | solution.py:542
  73.3 5.8 %collective-permute-start.16 = (bf16[448,128]{1,0:T(8,128)(2,1)S(1)}, bf16[448,128]{1,0:T(8,128)(2,1)S(1)}, u32[]{:S(2)}, u32[]{:S(2)}) collective-permute-start(bf16[448,128]{1,0:T(8,128)(2,1)S(1)} %select_convert_fusion), channel_id=1, source_target_pairs={{0,16},{4,20},{8,24},{12,28},{16,0},{20,4},{24,8},{28,12},{1,17},{... | collective-permute-start | bytes 344072 | tf_op jit(solution)/shard_map/ppermute | solution.py:542

commit v6 on v5

--- a/solution.py
+++ b/solution.py
@@ -10,7 +10,7 @@
 EPSILON = 1e-05
 BF16 = jnp.bfloat16
 F32 = jnp.float32
-ROWS = 256
+ROWS = 384
 CHUNK = 32
 VMEM_LIMIT = 30 * 1024 * 1024
 SMALL_LIMIT = 8 * 1024 * 1024
@@ -126,46 +126,49 @@
             copy.wait()
 
 
-def pick_kernel(pick_hbm, tile_hbm, out_ref, pick_ref, pick, tile, in_sems):
+def pick_kernel(
+    pick_hbm,
+    tile_hbm,
+    from_hbm,
+    cut_hbm,
+    out_ref,
+    pick_ref,
+    tile_ref,
+    from_ref,
+    cut_ref,
+    at,
+    in_sems,
+):
     loads = Copies(in_sems)
-    loads.start(pick_hbm, pick)
-    loads.start(tile_hbm, tile)
-    loads.finish()
-    pick_ref[...] = pick[...]
-    rows = hot_rows(as_column(pick[...]), tile.shape[0])
-    out_ref[...] = flat_dot(rows, tile[...]).astype(BF16)
+    first = [loads.start(pick_hbm, pick_ref), loads.start(tile_hbm, tile_ref)]
+    second = [loads.start(from_hbm, at), loads.start(cut_hbm, cut_ref)]
+    for copy in first:
+        copy.wait()
+    rows = hot_rows(as_column(pick_ref[...]), tile_ref.shape[0])
+    out_ref[...] = flat_dot(rows, tile_ref[...]).astype(BF16)
+    for copy in second:
+        copy.wait()
+    from_ref[...] = at[...].reshape(from_ref.shape)
 
 
 def pool_kernel(
     where_ref,
-    from_hbm,
-    cut_hbm,
-    tile_hbm,
+    from_ref,
+    cut_ref,
+    tile_ref,
     came_ref,
     latent_ref,
     first_ref,
     second_ref,
-    from_ref,
-    cut_ref,
-    at,
-    cut,
-    tile,
     ends,
-    in_sems,
 ):
-    loads = Copies(in_sems)
-    for source, target in ((from_hbm, at), (cut_hbm, cut), (tile_hbm, tile)):
-        loads.start(source, target)
-    loads.finish()
-    from_ref[...] = at[...].reshape(from_ref.shape)
-    cut_ref[...] = cut[...]
-    nodes = tile.shape[0]
+    nodes = tile_ref.shape[0]
     halo = first_ref.shape[0]
-    rows = hot_rows(as_column(at[...]), nodes + came_ref.shape[0])
-    value = flat_dot(rows[:, :nodes], tile[...]) + flat_dot(rows[:, nodes:], came_ref[...])
+    rows = hot_rows(as_column(from_ref[...]), nodes + came_ref.shape[0])
+    value = flat_dot(rows[:, :nodes], tile_ref[...]) + flat_dot(rows[:, nodes:], came_ref[...])
     value = value.astype(BF16)
     latent_ref[...] = value
-    ends[...] = inner_dot(hot_columns(cut[...], nodes), value).astype(BF16)
+    ends[...] = inner_dot(hot_columns(cut_ref[...], nodes), value).astype(BF16)
     turn = pl.multiple_of(where_ref[2], halo)
     first_ref[...] = ends[pl.ds(turn, halo), :]
     second_ref[...] = ends[pl.ds(halo - turn, halo), :]
@@ -652,23 +655,23 @@
     tile = lax.axis_index("tile")
     turn = jnp.where(lax.axis_index("dom") % 2 == 0, halo, 0)
     where = jnp.stack([tile & 1, tile, turn, lax.axis_index("dom")]).astype(jnp.int32)
-    outgoing, pick_row = call(
+    outgoing, pick_row, tile_rows, from_row, cut_row = call(
         pick_kernel,
         "pick",
-        [Kept(slot_bf16), Kept(relay_pick)],
-        [relay_pick, tile_latent],
-        [relay_pick, tile_latent, 2],
+        [Kept(slot_bf16), Kept(relay_pick), Kept(node_bf16)]
+        + [Kept(sds((1, nodes), jnp.int32)), Kept(cut_pick)],
+        [relay_pick, tile_latent, relay_from, cut_pick],
+        [node_index, 4],
         limit=SMALL_LIMIT,
     )
     edge_t = jnp.transpose(after(edge_latent, outgoing))
     came = after(exchange(outgoing), edge_t)
-    latent, first, second, from_row, cut_row = call(
+    latent, first, second = call(
         pool_kernel,
         "pool",
-        [Kept(node_bf16), Kept(halo_bf16), Kept(halo_bf16)]
-        + [Kept(sds((1, nodes), jnp.int32)), Kept(cut_pick)],
-        [relay_from, cut_pick, tile_latent, Kept(came)],
-        [node_index, cut_pick, node_bf16, sds((2 * halo, feat), BF16), 3],
+        [Kept(node_bf16), Kept(halo_bf16), Kept(halo_bf16)],
+        [Kept(array) for array in (from_row, cut_row, tile_rows, came)],
+        [sds((2 * halo, feat), BF16)],
         [where],
         SMALL_LIMIT,
     )

time: 80.4 us -> 79.1 us (0.984)
  Pallas kernels: 24.2 us -> 22.8 us
    pallas_call x7, Pallas kernels: 24.2 us -> 22.8 us  [call(): pl.pallas_call(kernel, out_shape=[array.array if isinstance(array, Kept)...]
where the time goes in v6:
time: 79.1 us; the launch traced here: 78.6 us
  waiting for transfers between devices  25.3 us (32%)
  starting transfers between devices  24.4 us (31%)
  Pallas kernels  22.8 us (29%)
  other arithmetic  3.07 us (4%)
  local copies, waits for them, and re-layouts  2.29 us (3%)
    pallas_call x7, Pallas kernels, call(): pl.pallas_call(kernel, out_shape=[array.array if isinstance(array, Kept)...  22.8 us
    ppermute x13, waiting for transfers between devices, flip(): return lax.ppermute(values, axis, [(i, i ^ mask) for i in range(count)])  11.6 us
    all_to_all x2, starting transfers between devices, exchange(): lax.all_to_all(blocks, 'dom', split_axis=0, concat_axis=0, tiled=True)  10.9 us
    ppermute x13, starting transfers between devices, flip(): return lax.ppermute(values, axis, [(i, i ^ mask) for i in range(count)])  9.6 us
    all_to_all x2, waiting for transfers between devices, exchange(): lax.all_to_all(blocks, 'dom', split_axis=0, concat_axis=0, tiled=True)  9.55 us
    ppermute x4, waiting for transfers between devices, meet(): return lax.ppermute(values, axis, pairs)  4.14 us
    ppermute x4, starting transfers between devices, meet(): return lax.ppermute(values, axis, pairs)  3.85 us
    optimization_barrier x1, local copies, waits for them, and re-layouts, after(): return lax.optimization_barrier((values, others))[0]  2.29 us
  transfers between devices with their start and end apart: 19, of which 10 were waited for; matrix products, arithmetic and copies ran while one was open for 6% of the time, Pallas kernels for 11%

profile of v6, /device:TPU:0, one launch (start us, length us, event | category | flops | bytes accessed | tf_op | source)
XLA Modules:
  0.0 78.6 jit_solution(1332132448616029185)
XLA Ops:
  0.6 1.8 %pick.1 = (bf16[128,512]{1,0:T(8,128)(2,1)}, s32[1,128]{1,0:T(1,128)S(1)}, bf16[128,512]{1,0:T(8,128)(2,1)S(1)}, s32[1,128]{1,0:T(1,128)S(1)}, s32[1,32]{1,0:T(1,128)S(1)}) custom-call(s32[1,128]{1,0:T(1,128)} %pick_hbm.1, bf16[128,512]{1,0:T(8,128)(2,1)} %tile_hbm.1, s32[128]{0:T(128)} %from_hbm.1, s32[1,32]{1,0:T(1,128)} %cut_hbm.1), custom_call_target="tpu_custom_call" | custom-call | tf_op jit(solution)/shard_map/pick/pallas_call | solution.py:97
  2.5 7.3 %all-to-all-start = ((bf16[8,16,512]{2,1,0:T(8,128)(2,1)}), bf16[8,16,512]{2,1,0:T(8,128)(2,1)S(1)}, u32[]{:S(2)}, u32[]{:S(2)}) async-start(bf16[8,16,512]{2,1,0:T(8,128)(2,1)} %bitcast.4), calls=%async_computation | async-start | bytes 262144 | tf_op jit(solution)/shard_map/all_to_all | solution.py:651
  9.8 2.3 %copy.18 = bf16[768,512]{0,1:T(8,128)(2,1)} copy(bf16[768,512]{1,0:T(8,128)(2,1)} %edge_hbm.3) | data formatting | bytes 1572864 | tf_op jit(solution)/shard_map/optimization_barrier | solution.py:565
  12.1 0.1 pad_add_fusion.where_ref
  12.1 5.0 %all-to-all-done = bf16[8,16,512]{2,1,0:T(8,128)(2,1)S(1)} async-done(((bf16[8,16,512]{2,1,0:T(8,128)(2,1)}), bf16[8,16,512]{2,1,0:T(8,128)(2,1)S(1)}, u32[]{:S(2)}, u32[]{:S(2)}) %all-to-all-start) | async-done | bytes 131104 | tf_op jit(solution)/shard_map/all_to_all | solution.py:651
  17.1 0.9 %pool.1 = (bf16[128,512]{1,0:T(8,128)(2,1)S(1)}, bf16[16,512]{1,0:T(8,128)(2,1)S(1)}, bf16[16,512]{1,0:T(8,128)(2,1)S(1)}) custom-call(s32[4]{0:T(128)S(1)} %pad_add_fusion.where_ref, s32[1,128]{1,0:T(1,128)S(1)} %get-tuple-element.53.from_ref, s32[1,32]{1,0:T(1,128)S(1)} %get-tuple-element.54.cut_ref, bf16[128,512]{1,0:T(8,128)(2,1)S(1)} %get-tuple-element.55.tile_ref, ...), custom_call_target="tpu_custom_call" | custom-call | tf_op jit(solution)/shard_map/pool/pallas_call | solution.py:97
  18.0 1.6 %collective-permute-start.1 = (bf16[128,512]{1,0:T(8,128)(2,1)S(1)}, bf16[128,512]{1,0:T(8,128)(2,1)S(1)}, u32[]{:S(2)}, u32[]{:S(2)}) collective-permute-start(bf16[128,512]{1,0:T(8,128)(2,1)S(1)} %get-tuple-element.59.latent_ref), channel_id=1, source_target_pairs={{0,2},{1,3},{2,0},{3,1},{4,6},{5,7},{6,4},{7,5},{8,10},{9,11},{10,... | collective-permute-start | bytes 393224 | tf_op jit(solution)/shard_map/ppermute | solution.py:545
  19.6 0.2 collective-permute-start.2
  19.8 1.8 %collective-permute-start.3 = (bf16[16,512]{1,0:T(8,128)(2,1)S(1)}, bf16[16,512]{1,0:T(8,128)(2,1)S(1)}, u32[]{:S(2)}, u32[]{:S(2)}) collective-permute-start(bf16[16,512]{1,0:T(8,128)(2,1)S(1)} %get-tuple-element.61), channel_id=1, source_target_pairs={{0,28},{4,8},{8,4},{12,16},{16,12},{20,24},{24,20},{28,0},{1,29},{... | collective-permute-start | bytes 49160 | tf_op jit(solution)/shard_map/ppermute | solution.py:551
  21.6 0.0 collective-permute-start
  21.6 2.8 %base.1 = (f32[768,512]{1,0:T(8,128)S(1)}, bf16[512,512]{1,0:T(8,128)(2,1)S(1)}, bf16[512,512]{1,0:T(8,128)(2,1)S(1)}) custom-call(s32[768]{0:T(1024)} %receiver_hbm.5, bf16[768,512]{1,0:T(8,128)(2,1)} %edge_hbm.3, bf16[1536,512]{1,0:T(8,128)(2,1)} %w_hbm.1, bf16[512,512]{1,0:T(8,128)(2,1)} %edge_out_hbm.1, bf16[128,512]{1,0:T(8,128)(2,1)S(1)} %get-tuple-element.59.latent_ref), custom_call_target="tpu_custom_call" | custom-call | tf_op jit(solution)/shard_map/base/pallas_call | solution.py:97
  24.4 0.0 collective-permute-done.2.first_ref
  24.5 1.8 %collective-permute-done.3.second_ref = bf16[16,512]{1,0:T(8,128)(2,1)S(1)} collective-permute-done((bf16[16,512]{1,0:T(8,128)(2,1)S(1)}, bf16[16,512]{1,0:T(8,128)(2,1)S(1)}, u32[]{:S(2)}, u32[]{:S(2)}) %collective-permute-start.3) | collective-permute-done | bytes 16416 | tf_op jit(solution)/shard_map/ppermute | solution.py:551
  26.2 0.0 collective-permute-done.1.far_ref
  26.3 1.3 %collective-permute-done.4.cross_ref = bf16[128,512]{1,0:T(8,128)(2,1)S(1)} collective-permute-done((bf16[128,512]{1,0:T(8,128)(2,1)S(1)}, bf16[128,512]{1,0:T(8,128)(2,1)S(1)}, u32[]{:S(2)}, u32[]{:S(2)}) %collective-permute-start.4) | collective-permute-done | bytes 131104 | tf_op jit(solution)/shard_map/ppermute | solution.py:545
  27.6 11.3 %block.1 = (bf16[128,512]{1,0:T(8,128)(2,1)}, bf16[768,512]{1,0:T(8,128)(2,1)}, bf16[768,512]{1,0:T(8,128)(2,1)}, bf16[256,512]{1,0:T(8,128)(2,1)}, f32[128,512]...) custom-call(s32[4]{0:T(128)S(1)} %pad_add_fusion.where_ref, ...), custom_call_target="tpu_custom_call" | custom-call | tf_op jit(solution)/shard_map/block/pallas_call | solution.py:97
  38.9 0.2 collective-permute-start.6
  39.1 0.4 collective-permute-start.5
  39.5 0.0 collective-permute-start.7
  39.5 1.8 %collective-permute-start.8 = (bf16[16,512]{1,0:T(8,128)(2,1)S(1)}, bf16[16,512]{1,0:T(8,128)(2,1)S(1)}, u32[]{:S(2)}, u32[]{:S(2)}) collective-permute-start(bf16[16,512]{1,0:T(8,128)(2,1)S(1)} %get-tuple-element.77), channel_id=1, source_target_pairs={{0,28},{4,8},{8,4},{12,16},{16,12},{20,24},{24,20},{28,0},{1,29},{... | collective-permute-start | bytes 49160 | tf_op jit(solution)/shard_map/ppermute | solution.py:551
  41.3 0.7 collective-permute-done.6
  42.0 1.5 %add_convert_fusion.1 = (bf16[1792,128]{1,0:T(8,128)(2,1)S(1)}, bf16[1792,128]{1,0:T(8,128)(2,1)S(1)}) fusion(bf16[4608,128]{1,0:T(8,128)(2,1)S(1)} %collective-permute-done.6, bf16[3584,128]{1,0:T(8,128)(2,1)} %get-tuple-element.74), kind=kLoop, calls=%fused_computation.1 | loop fusion | flops 1835008 | bytes 2752512 | tf_op jit(solution)/shard_map/convert_element_type | solution.py:589
  43.5 0.1 collective-permute-start.10
  43.6 0.0 collective-permute-done.7.first_ref
  43.6 2.3 %collective-permute-done.8.second_ref = bf16[16,512]{1,0:T(8,128)(2,1)S(1)} collective-permute-done((bf16[16,512]{1,0:T(8,128)(2,1)S(1)}, bf16[16,512]{1,0:T(8,128)(2,1)S(1)}, u32[]{:S(2)}, u32[]{:S(2)}) %collective-permute-start.8) | collective-permute-done | bytes 16416 | tf_op jit(solution)/shard_map/ppermute | solution.py:551
  45.9 0.0 collective-permute-done.5
  45.9 0.2 add_convert_fusion
  46.2 0.1 collective-permute-start.11
  46.3 0.6 collective-permute-start.9
  46.9 4.4 %collective-permute-done.9 = bf16[512,128]{1,0:T(8,128)(2,1)S(1)} collective-permute-done((bf16[512,128]{1,0:T(8,128)(2,1)S(1)}, bf16[512,128]{1,0:T(8,128)(2,1)S(1)}, u32[]{:S(2)}, u32[]{:S(2)}) %collective-permute-start.9) | collective-permute-done | bytes 131104 | tf_op jit(solution)/shard_map/ppermute | solution.py:545
  51.4 1.9 %node.1 = (bf16[128,512]{1,0:T(8,128)(2,1)S(1)}, bf16[128,512]{1,0:T(8,128)(2,1)}) custom-call(s32[4]{0:T(128)S(1)} %pad_add_fusion.where_ref, s32[1,128]{1,0:T(1,128)S(1)} %get-tuple-element.53.from_ref, s32[1,32]{1,0:T(1,128)S(1)} %get-tuple-element.54.cut_ref, bf16[512,512]{1,0:T(8,128)(2,1)S(1)} %get-tuple-element.64.w_send.w_send_ref, ...), custom_call_target="tpu_custom_call" | custom-call | tf_op jit(solution)/shard_map/node/pallas_call | solution.py:97
  53.3 3.6 %all-to-all-start.1 = ((bf16[8,16,512]{2,1,0:T(8,128)(2,1)}), bf16[8,16,512]{2,1,0:T(8,128)(2,1)S(1)}, u32[]{:S(2)}, u32[]{:S(2)}) async-start(bf16[8,16,512]{2,1,0:T(8,128)(2,1)} %bitcast.7), calls=%async_computation.1 | async-start | bytes 262144 | tf_op jit(solution)/shard_map/all_to_all | solution.py:651
  56.9 0.8 %collective-permute-done.11 = bf16[1792,128]{1,0:T(8,128)(2,1)S(1)} collective-permute-done((bf16[1792,128]{1,0:T(8,128)(2,1)S(1)}, bf16[1792,128]{1,0:T(8,128)(2,1)S(1)}, u32[]{:S(2)}, u32[]{:S(2)}) %collective-permute-start.11) | collective-permute-done | bytes 458784 | tf_op jit(solution)/shard_map/ppermute | solution.py:545
  57.7 0.2 add_convert_fusion.4
  58.0 1.3 %collective-permute-start.13 = (bf16[896,128]{1,0:T(8,128)(2,1)S(1)}, bf16[896,128]{1,0:T(8,128)(2,1)S(1)}, u32[]{:S(2)}, u32[]{:S(2)}) collective-permute-start(bf16[896,128]{1,0:T(8,128)(2,1)S(1)} %get-tuple-element.106), channel_id=1, source_target_pairs={{0,4},{4,0},{8,12},{12,8},{16,20},{20,16},{24,28},{28,24},{1,5},{5... | collective-permute-start | bytes 688136 | tf_op jit(solution)/shard_map/ppermute | solution.py:545
  59.3 0.5 collective-permute-start.12
  59.8 4.6 %all-to-all-done.1 = bf16[8,16,512]{2,1,0:T(8,128)(2,1)S(1)} async-done(((bf16[8,16,512]{2,1,0:T(8,128)(2,1)}), bf16[8,16,512]{2,1,0:T(8,128)(2,1)S(1)}, u32[]{:S(2)}, u32[]{:S(2)}) %all-to-all-start.1) | async-done | bytes 131104 | tf_op jit(solution)/shard_map/all_to_all | solution.py:651
  64.4 0.8 %back.1 = bf16[128,512]{1,0:T(8,128)(2,1)} custom-call(s32[1,128]{1,0:T(1,128)S(1)} %get-tuple-element.68.pick_ref, bf16[128,512]{1,0:T(8,128)(2,1)S(1)} %get-tuple-element.83.stay_ref, bf16[128,512]{1,0:T(8,128)(2,1)S(1)} %bitcast.10), custom_call_target="tpu_custom_call" | custom-call | tf_op jit(solution)/shard_map/back/pallas_call | solution.py:97
  65.2 0.1 add_convert_fusion.9
  65.3 0.6 collective-permute-start.15
  65.9 0.1 add_convert_fusion.10
  66.0 2.1 %collective-permute-start.14 = (bf16[448,128]{1,0:T(8,128)(2,1)S(1)}, bf16[448,128]{1,0:T(8,128)(2,1)S(1)}, u32[]{:S(2)}, u32[]{:S(2)}) collective-permute-start(bf16[448,128]{1,0:T(8,128)(2,1)S(1)} %get-tuple-element.112), channel_id=1, source_target_pairs={{0,8},{4,12},{8,0},{12,4},{16,24},{20,28},{24,16},{28,20},{1,9},{5... | collective-permute-start | bytes 344072 | tf_op jit(solution)/shard_map/ppermute | solution.py:545
  68.1 3.2 %edge_grad.1 = bf16[768,512]{1,0:T(8,128)(2,1)} custom-call(s32[768]{0:T(1024)} %receiver_hbm.5, bf16[768,512]{1,0:T(8,128)(2,1)} %get-tuple-element.95.pre_grad_hbm, bf16[768,512]{1,0:T(8,128)(2,1)} %edge_cot_hbm.3, bf16[1536,512]{1,0:T(8,128)(2,1)} %w_hbm.1, bf16[256,512]{1,0:T(8,128)(2,1)} %get-tuple-element.96.agg_parts_hbm), custom_call_target="tpu_custom_call" | custom-call | tf_op jit(solution)/shard_map/edge_grad/pallas_call | solution.py:97
  71.4 0.7 collective-permute-done.14
  72.0 0.1 select_convert_fusion
  72.1 2.1 %collective-permute-start.16 = (bf16[448,128]{1,0:T(8,128)(2,1)S(1)}, bf16[448,128]{1,0:T(8,128)(2,1)S(1)}, u32[]{:S(2)}, u32[]{:S(2)}) collective-permute-start(bf16[448,128]{1,0:T(8,128)(2,1)S(1)} %select_convert_fusion), channel_id=1, source_target_pairs={{0,16},{4,20},{8,24},{12,28},{16,0},{20,4},{24,8},{28,12},{1,17},{... | collective-permute-start | bytes 344072 | tf_op jit(solution)/shard_map/ppermute | solution.py:545
  74.2 3.6 %collective-permute-done.16 = bf16[448,128]{1,0:T(8,128)(2,1)S(1)} collective-permute-done((bf16[448,128]{1,0:T(8,128)(2,1)S(1)}, bf16[448,128]{1,0:T(8,128)(2,1)S(1)}, u32[]{:S(2)}, u32[]{:S(2)}) %collective-permute-start.16) | collective-permute-done | bytes 114720 | tf_op jit(solution)/shard_map/ppermute | solution.py:545
  77.8 0.8 convert_add_fusion.1
  (10 shorter events, 0.1 us)
Async XLA Ops:
  2.5 14.6 %all-to-all-start = ((bf16[8,16,512]{2,1,0:T(8,128)(2,1)}), bf16[8,16,512]{2,1,0:T(8,128)(2,1)S(1)}, u32[]{:S(2)}, u32[]{:S(2)}) async-start(bf16[8,16,512]{2,1,0:T(8,128)(2,1)} %bitcast.4), calls=%async_computation | async-start | bytes 262144 | tf_op jit(solution)/shard_map/all_to_all | solution.py:651
  18.0 8.2 %collective-permute-start.1 = (bf16[128,512]{1,0:T(8,128)(2,1)S(1)}, bf16[128,512]{1,0:T(8,128)(2,1)S(1)}, u32[]{:S(2)}, u32[]{:S(2)}) collective-permute-start(bf16[128,512]{1,0:T(8,128)(2,1)S(1)} %get-tuple-element.59.latent_ref), channel_id=1, source_target_pairs={{0,2},{1,3},{2,0},{3,1},{4,6},{5,7},{6,4},{7,5},{8,10},{9,11},{10,... | collective-permute-start | bytes 393224 | tf_op jit(solution)/shard_map/ppermute | solution.py:545
  19.6 4.8 %collective-permute-start.2 = (bf16[16,512]{1,0:T(8,128)(2,1)S(1)}, bf16[16,512]{1,0:T(8,128)(2,1)S(1)}, u32[]{:S(2)}, u32[]{:S(2)}) collective-permute-start(bf16[16,512]{1,0:T(8,128)(2,1)S(1)} %get-tuple-element.60), channel_id=1, source_target_pairs={{0,4},{4,0},{8,12},{12,8},{16,20},{20,16},{24,28},{28,24},{1,5},{5... | collective-permute-start | bytes 49160 | tf_op jit(solution)/shard_map/ppermute | solution.py:551
  19.8 6.4 %collective-permute-start.3 = (bf16[16,512]{1,0:T(8,128)(2,1)S(1)}, bf16[16,512]{1,0:T(8,128)(2,1)S(1)}, u32[]{:S(2)}, u32[]{:S(2)}) collective-permute-start(bf16[16,512]{1,0:T(8,128)(2,1)S(1)} %get-tuple-element.61), channel_id=1, source_target_pairs={{0,28},{4,8},{8,4},{12,16},{16,12},{20,24},{24,20},{28,0},{1,29},{... | collective-permute-start | bytes 49160 | tf_op jit(solution)/shard_map/ppermute | solution.py:551
  21.6 4.6 %collective-permute-start = (bf16[128,512]{1,0:T(8,128)(2,1)S(1)}, bf16[128,512]{1,0:T(8,128)(2,1)S(1)}, u32[]{:S(2)}, u32[]{:S(2)}) collective-permute-start(bf16[128,512]{1,0:T(8,128)(2,1)S(1)} %get-tuple-element.59.latent_ref), channel_id=1, source_target_pairs={{0,1},{1,0},{2,3},{3,2},{4,5},{5,4},{6,7},{7,6},{8,9},{9,8},{10,11... | collective-permute-start | bytes 393224 | tf_op jit(solution)/shard_map/ppermute | solution.py:545
  26.3 1.3 %collective-permute-start.4 = (bf16[128,512]{1,0:T(8,128)(2,1)S(1)}, bf16[128,512]{1,0:T(8,128)(2,1)S(1)}, u32[]{:S(2)}, u32[]{:S(2)}) collective-permute-start(bf16[128,512]{1,0:T(8,128)(2,1)S(1)} %collective-permute-done.1.far_ref), channel_id=1, source_target_pairs={{0,1},{1,0},{2,3},{3,2},{4,5},{5,4},{6,7},{7,6},{8,9},{9,8},{10,11... | collective-permute-start | bytes 393224 | tf_op jit(solution)/shard_map/ppermute | solution.py:545
  38.9 3.1 %collective-permute-start.6 = (bf16[4608,128]{1,0:T(8,128)(2,1)}, bf16[4608,128]{1,0:T(8,128)(2,1)S(1)}, u32[]{:S(2)}, u32[]{:S(2)}) collective-permute-start(bf16[4608,128]{1,0:T(8,128)(2,1)} %get-tuple-element.73), channel_id=1, source_target_pairs={{0,1},{1,0},{2,3},{3,2},{4,5},{5,4},{6,7},{7,6},{8,9},{9,8},{10,11... | collective-permute-start | bytes 3538952 | tf_op jit(solution)/shard_map/ppermute | solution.py:545
  39.1 6.8 %collective-permute-start.5 = (bf16[3584,128]{1,0:T(8,128)(2,1)}, bf16[3584,128]{1,0:T(8,128)(2,1)S(1)}, u32[]{:S(2)}, u32[]{:S(2)}) collective-permute-start(bf16[3584,128]{1,0:T(8,128)(2,1)} %get-tuple-element.71), channel_id=1, source_target_pairs={{0,1},{1,0},{2,3},{3,2},{4,5},{5,4},{6,7},{7,6},{8,9},{9,8},{10,11... | collective-permute-start | bytes 2752520 | tf_op jit(solution)/shard_map/ppermute | solution.py:545
  39.5 4.1 %collective-permute-start.7 = (bf16[16,512]{1,0:T(8,128)(2,1)S(1)}, bf16[16,512]{1,0:T(8,128)(2,1)S(1)}, u32[]{:S(2)}, u32[]{:S(2)}) collective-permute-start(bf16[16,512]{1,0:T(8,128)(2,1)S(1)} %get-tuple-element.76), channel_id=1, source_target_pairs={{0,4},{4,0},{8,12},{12,8},{16,20},{20,16},{24,28},{28,24},{1,5},{5... | collective-permute-start | bytes 49160 | tf_op jit(solution)/shard_map/ppermute | solution.py:551
  39.5 6.4 %collective-permute-start.8 = (bf16[16,512]{1,0:T(8,128)(2,1)S(1)}, bf16[16,512]{1,0:T(8,128)(2,1)S(1)}, u32[]{:S(2)}, u32[]{:S(2)}) collective-permute-start(bf16[16,512]{1,0:T(8,128)(2,1)S(1)} %get-tuple-element.77), channel_id=1, source_target_pairs={{0,28},{4,8},{8,4},{12,16},{16,12},{20,24},{24,20},{28,0},{1,29},{... | collective-permute-start | bytes 49160 | tf_op jit(solution)/shard_map/ppermute | solution.py:551
  42.0 3.9 %copy-start = (bf16[3584,128]{1,0:T(8,128)(2,1)S(1)}, bf16[3584,128]{1,0:T(8,128)(2,1)}, u32[]{:S(2)}) copy-start(bf16[3584,128]{1,0:T(8,128)(2,1)} %get-tuple-element.78) | copy-start | bytes 2752516
  43.5 14.2 %collective-permute-start.10 = (bf16[1792,128]{1,0:T(8,128)(2,1)S(1)}, bf16[1792,128]{1,0:T(8,128)(2,1)S(1)}, u32[]{:S(2)}, u32[]{:S(2)}) collective-permute-start(bf16[1792,128]{1,0:T(8,128)(2,1)S(1)} %get-tuple-element.102), channel_id=1, source_target_pairs={{0,4},{4,0},{8,12},{12,8},{16,20},{20,16},{24,28},{28,24},{1,5},{5... | collective-permute-start | bytes 1376264 | tf_op jit(solution)/shard_map/ppermute | solution.py:545
  46.2 11.5 %collective-permute-start.11 = (bf16[1792,128]{1,0:T(8,128)(2,1)S(1)}, bf16[1792,128]{1,0:T(8,128)(2,1)S(1)}, u32[]{:S(2)}, u32[]{:S(2)}) collective-permute-start(bf16[1792,128]{1,0:T(8,128)(2,1)S(1)} %get-tuple-element.104), channel_id=1, source_target_pairs={{0,8},{4,12},{8,0},{12,4},{16,24},{20,28},{24,16},{28,20},{1,9},{5... | collective-permute-start | bytes 1376264 | tf_op jit(solution)/shard_map/ppermute | solution.py:545
  46.3 5.0 %collective-permute-start.9 = (bf16[512,128]{1,0:T(8,128)(2,1)S(1)}, bf16[512,128]{1,0:T(8,128)(2,1)S(1)}, u32[]{:S(2)}, u32[]{:S(2)}) collective-permute-start(bf16[512,128]{1,0:T(8,128)(2,1)S(1)} %add_convert_fusion.8), channel_id=1, source_target_pairs={{0,2},{1,3},{2,0},{3,1},{4,6},{5,7},{6,4},{7,5},{8,10},{9,11},{10,... | collective-permute-start | bytes 393224 | tf_op jit(solution)/shard_map/ppermute | solution.py:545
  53.3 11.1 %all-to-all-start.1 = ((bf16[8,16,512]{2,1,0:T(8,128)(2,1)}), bf16[8,16,512]{2,1,0:T(8,128)(2,1)S(1)}, u32[]{:S(2)}, u32[]{:S(2)}) async-start(bf16[8,16,512]{2,1,0:T(8,128)(2,1)} %bitcast.7), calls=%async_computation.1 | async-start | bytes 262144 | tf_op jit(solution)/shard_map/all_to_all | solution.py:651
  58.0 7.3 %collective-permute-start.13 = (bf16[896,128]{1,0:T(8,128)(2,1)S(1)}, bf16[896,128]{1,0:T(8,128)(2,1)S(1)}, u32[]{:S(2)}, u32[]{:S(2)}) collective-permute-start(bf16[896,128]{1,0:T(8,128)(2,1)S(1)} %get-tuple-element.106), channel_id=1, source_target_pairs={{0,4},{4,0},{8,12},{12,8},{16,20},{20,16},{24,28},{28,24},{1,5},{5... | collective-permute-start | bytes 688136 | tf_op jit(solution)/shard_map/ppermute | solution.py:545
  59.3 6.6 %collective-permute-start.12 = (bf16[896,128]{1,0:T(8,128)(2,1)S(1)}, bf16[896,128]{1,0:T(8,128)(2,1)S(1)}, u32[]{:S(2)}, u32[]{:S(2)}) collective-permute-start(bf16[896,128]{1,0:T(8,128)(2,1)S(1)} %get-tuple-element.113), channel_id=1, source_target_pairs={{0,2},{1,3},{2,0},{3,1},{4,6},{5,7},{6,4},{7,5},{8,10},{9,11},{10,... | collective-permute-start | bytes 688136 | tf_op jit(solution)/shard_map/ppermute | solution.py:545
  65.3 6.1 %collective-permute-start.15 = (bf16[448,128]{1,0:T(8,128)(2,1)S(1)}, bf16[448,128]{1,0:T(8,128)(2,1)S(1)}, u32[]{:S(2)}, u32[]{:S(2)}) collective-permute-start(bf16[448,128]{1,0:T(8,128)(2,1)S(1)} %get-tuple-element.110), channel_id=1, source_target_pairs={{0,2},{1,3},{2,0},{3,1},{4,6},{5,7},{6,4},{7,5},{8,10},{9,11},{10,... | collective-permute-start | bytes 344072 | tf_op jit(solution)/shard_map/ppermute | solution.py:545
  66.0 6.1 %collective-permute-start.14 = (bf16[448,128]{1,0:T(8,128)(2,1)S(1)}, bf16[448,128]{1,0:T(8,128)(2,1)S(1)}, u32[]{:S(2)}, u32[]{:S(2)}) collective-permute-start(bf16[448,128]{1,0:T(8,128)(2,1)S(1)} %get-tuple-element.112), channel_id=1, source_target_pairs={{0,8},{4,12},{8,0},{12,4},{16,24},{20,28},{24,16},{28,20},{1,9},{5... | collective-permute-start | bytes 344072 | tf_op jit(solution)/shard_map/ppermute | solution.py:545
  72.1 5.8 %collective-permute-start.16 = (bf16[448,128]{1,0:T(8,128)(2,1)S(1)}, bf16[448,128]{1,0:T(8,128)(2,1)S(1)}, u32[]{:S(2)}, u32[]{:S(2)}) collective-permute-start(bf16[448,128]{1,0:T(8,128)(2,1)S(1)} %select_convert_fusion), channel_id=1, source_target_pairs={{0,16},{4,20},{8,24},{12,28},{16,0},{20,4},{24,8},{28,12},{1,17},{... | collective-permute-start | bytes 344072 | tf_op jit(solution)/shard_map/ppermute | solution.py:545
